TPU v7x, 32 devices: a whole 2x2x4 slice. The times are simulated.
32 devices in a mesh: groups: 2 (over y), row: 4 (over z), col: 4 (over x, core).
Axes of the slice: x: 2, y: 2, z: 4, core: 2. Of those that a mesh axis runs over, the one named last changes fastest.
Arguments:
- green_starting_blocks: float32 [4, 128, 2048], P('groups', None, ('row', 'col')), parts along dimension 0, may hold values from -3 to 3
- fit_vectors: bfloat16 [256, 4096], P('groups'), parts along dimension 0, may hold values from -0.75 to 0.75
- history: bfloat16 [4, 2048, 2048], P('groups', 'row', 'col'), parts along dimension 0, may hold values from -0.125 to 0.125
Outputs:
- green_final: float32 [4, 128, 2048], P('groups', None, ('row', 'col')), parts along dimension 0
There are 2 independent parts, one for each index of `groups`. A program takes and returns all parts, laid end to end along the dimension named above; each array names one. Nothing has to cross between parts.
All inputs are finite; a program needn't handle non-finite values.
Results may differ from a plain program's by a relative error of at most 0.03.
Values may be sent and summed in bfloat16 or wider, within the bound.
No kernel may reach another device: no remote copies, remote signals or barrier semaphores. Data moves between devices by JAX's collectives and lax.ppermute only.
A program may use at most 128 MiB of HBM per device.

v0:
```python
import jax
import jax.numpy as jnp
from jax import lax
from jax.sharding import PartitionSpec as P

NO = 64
NEW = 2
ITERS = 2


def pair_self_energy(pair_blocks, fit_vectors):
    pair_count = pair_blocks.shape[1]
    orbitals = pair_blocks.shape[2]
    aux_count = fit_vectors.shape[0]
    lowered = pair_blocks.astype(jnp.bfloat16)
    fit_basis = fit_vectors.reshape(aux_count * orbitals, orbitals)
    inner_side = jnp.transpose(lowered, (2, 0, 1, 3)).reshape(orbitals, 2 * pair_count * orbitals)
    left_prod = jnp.dot(fit_basis, inner_side, preferred_element_type=jnp.float32).astype(
        jnp.bfloat16
    )
    left_prod = left_prod.reshape(aux_count, orbitals, 2, pair_count, orbitals)
    fit_turned = jnp.transpose(
        fit_vectors.reshape(aux_count, orbitals, orbitals), (1, 0, 2)
    ).reshape(orbitals, aux_count * orbitals)
    right_prod = jnp.dot(
        lowered.reshape(2 * pair_count * orbitals, orbitals),
        fit_turned,
        preferred_element_type=jnp.float32,
    ).astype(jnp.bfloat16)
    right_prod = right_prod.reshape(2, pair_count, orbitals, aux_count, orbitals)
    bubble = (
        jnp.einsum("picnk,cniqk->npq", left_prod, right_prod, preferred_element_type=jnp.float32)
        / orbitals
    )
    bubble = bubble.astype(jnp.bfloat16)
    screened = jnp.einsum(
        "npq,qm->npm", bubble, fit_vectors, preferred_element_type=jnp.float32
    ).astype(jnp.bfloat16)
    screened = screened.reshape(pair_count, aux_count, orbitals, orbitals)
    scale_factor = (aux_count * orbitals) ** (-0.5)
    energy = (
        jnp.einsum("picnl,nplj->cnij", left_prod, screened, preferred_element_type=jnp.float32)
        * scale_factor
    )
    return energy.astype(jnp.bfloat16)


def local(green_starting_blocks, fit_vectors, history):
    row_count = green_starting_blocks.shape[1]
    span_cols = green_starting_blocks.shape[2]
    local_times = span_cols // NO
    row_devices = lax.axis_size("row")
    col_devices = lax.axis_size("col")
    row_ratio = row_devices // col_devices
    green_current = green_starting_blocks
    for iteration in range(ITERS):
        pair_blocks = green_current.reshape(2, NEW, NO, local_times, NO).transpose(0, 1, 3, 2, 4)
        pair_blocks = pair_blocks.reshape(2, NEW * local_times, NO, NO)
        energies = pair_self_energy(pair_blocks, fit_vectors)
        self_energy = energies.reshape(2, NEW, local_times, NO, NO).transpose(0, 1, 3, 2, 4)
        self_energy = self_energy.reshape(2, row_count, span_cols)
        segment = lax.all_gather(self_energy, "col", axis=2, tiled=True)
        seg_width = segment.shape[2]
        stacked = segment.reshape(2 * row_count, seg_width)
        real_rows = history[0]
        imag_rows = history[1]
        real_half = jnp.dot(stacked, real_rows, preferred_element_type=jnp.float32)
        imaginary_half = jnp.dot(stacked, imag_rows, preferred_element_type=jnp.float32)
        totals = (
            real_half[:row_count] - imaginary_half[row_count:],
            imaginary_half[:row_count] + real_half[row_count:],
        )
        partial_value = jnp.stack(totals)
        shaped = partial_value.reshape(2, row_count, 1, row_ratio, col_devices, span_cols)
        shuffled = lax.all_to_all(
            shaped.astype(jnp.bfloat16), "col", split_axis=4, concat_axis=2, tiled=True
        ).astype(shaped.dtype)
        shuffled = shuffled.reshape(2, row_count, row_devices, span_cols)
        summed = lax.psum_scatter(
            shuffled.astype(jnp.bfloat16), "row", scatter_dimension=2, tiled=True
        ).astype(jnp.float32)
        collision = summed.reshape(2, row_count, span_cols)
        green_current = green_starting_blocks + collision
    return green_current


def solution(mesh):
    in_specs = (P("groups", None, ("row", "col")), P("groups", None), P("groups", "row", "col"))
    out_specs = P("groups", None, ("row", "col"))
    return jax.shard_map(local, mesh=mesh, in_specs=in_specs, out_specs=out_specs, check_vma=False)
```

profile of v0, /device:TPU:0, one launch (start us, length us, event | category | flops | bytes accessed | tf_op | source)
XLA Modules:
  0.0 334.6 jit_solution(7470112163291721763)
XLA Ops:
  6.5 0.0 reduce-scatter.3.cloned.1.call-start
  6.5 0.9 convert_element_type.105
  7.5 0.1 convert_element_type.106
  7.6 0.1 copy.55
  7.7 1.6 copy.56
  9.3 3.3 reshape.178
  12.6 0.1 convert_element_type.110
  12.8 0.1 copy.53
  12.9 0.1 reshape.179
  13.0 1.8 copy.57
  14.8 3.3 reshape.182
  18.2 0.0 copy-start.1
  18.2 5.6 %convolution_convert_fusion.3 = bf16[8192,512]{1,0:T(8,128)(2,1)} fusion(bf16[8192,64]{1,0:T(8,128)(2,1)S(1)} %reshape.178, bf16[64,512]{1,0:T(8,128)(2,1)S(1)} %reshape.179), kind=kOutput, calls=%fused_computation.7 | convolution fusion | flops 541065216 | bytes 9502720 | tf_op jit(solution)/shard_map/dot_general | solution.py:18
  23.7 11.4 %copy.54 = bf16[8192,512]{0,1:T(8,128)(2,1)} copy(bf16[8192,512]{1,0:T(8,128)(2,1)} %convolution_convert_fusion.3) | data formatting | bytes 16777216 | tf_op jit(solution)/shard_map/convert_element_type | solution.py:18
  35.1 23.6 %reshape.180 = bf16[128,64,2,4,64]{1,0,4,3,2:T(8,128)(2,1)} reshape(bf16[8192,512]{0,1:T(8,128)(2,1)} %copy.54) | data formatting | bytes 16777216 | tf_op jit(solution)/shard_map/reshape | solution.py:21
  58.7 0.0 copy-done.1
  58.7 5.6 %convolution_convert_fusion.2 = bf16[512,8192]{1,0:T(8,128)(2,1)} fusion(bf16[512,64]{0,1:T(8,128)(2,1)S(1)} %convert_element_type.110, bf16[64,8192]{1,0:T(8,128)(2,1)S(1)} %reshape.182), kind=kOutput, calls=%fused_computation.6 | convolution fusion | flops 541065216 | bytes 9502720 | tf_op jit(solution)/shard_map/dot_general | solution.py:25
  64.3 23.6 %reshape.183 = bf16[2,4,64,128,64]{4,3,2,1,0:T(8,128)(2,1)} reshape(bf16[512,8192]{1,0:T(8,128)(2,1)} %convolution_convert_fusion.2) | data formatting | bytes 16777216 | tf_op jit(solution)/shard_map/reshape | solution.py:30
  87.9 18.9 %copy.59 = bf16[2,4,64,128,64]{3,2,4,1,0:T(8,128)(2,1)} copy(bf16[2,4,64,128,64]{4,3,2,1,0:T(8,128)(2,1)} %reshape.183) | data formatting | bytes 16777216 | tf_op jit(solution)/shard_map/reshape | solution.py:30
  106.8 0.0 copy-done
  106.8 14.8 %convolution_convert_fusion.5 = bf16[4,128,4096]{2,1,0:T(8,128)(2,1)} fusion(bf16[128,64,2,4,64]{1,0,4,3,2:T(8,128)(2,1)} %reshape.180, bf16[2,4,64,128,64]{3,2,4,1,0:T(8,128)(2,1)} %copy.59, bf16[128,4096]{1,0:T(8,128)(2,1)S(1)} %copy-done), kind=kOutput, calls=%fused_computation.10 | convolution fusion | flops 1612840960 | bytes 22020096 | tf_op jit(solution)/shard_map/npq,qm->npm/dot_general | solution.py:36
  121.6 6.3 %copy.60 = bf16[4,128,4096]{1,2,0:T(8,128)(2,1)} copy(bf16[4,128,4096]{2,1,0:T(8,128)(2,1)} %convolution_convert_fusion.5) | data formatting | bytes 8388608 | tf_op jit(solution)/shard_map/convert_element_type | solution.py:38
  128.0 10.1 %fusion.21 = bf16[4,64,64,2]{2,1,3,0:T(8,128)(2,1)S(1)} fusion(bf16[4,128,64,64,1]{1,3,2,4,0:T(8,128)(2,1)} %bitcast.117, bf16[128,64,2,4,64]{1,0,4,3,2:T(8,128)(2,1)} %reshape.180), kind=kOutput, calls=%fused_computation.21 | convolution fusion | flops 536936448 | bytes 12648448 | tf_op jit(solution)/shard_map/picnl,nplj->cnij/dot_general | solution.py:42
  138.0 0.1 copy.62
  138.2 0.1 reshape.186
  138.3 7.2 %all_gather.6 = bf16[2,128,512]{2,1,0:T(8,128)(2,1)S(1)} all-gather(bf16[2,128,128]{2,1,0:T(8,128)(2,1)S(1)} %reshape.186), channel_id=1, replica_groups=mesh['groups'=2,'row'=4,'col'=4] {'col'}, dimensions={2}, use_global_device_ids=true | all-gather | bytes 327680 | tf_op jit(solution)/shard_map/all_gather | solution.py:62
  145.5 1.3 fusion.31
  146.8 1.3 fusion.35
  148.2 0.1 fusion.44
  148.3 0.7 stack.18
  149.0 1.6 copy.63
  150.6 0.9 pad_maximum_fusion
  151.6 9.1 %all_to_all.24 = bf16[2,128,1,1,4,128]{5,1,0,3,2,4:T(8,128)(2,1)} all-to-all(bf16[2,128,1,1,4,128]{5,1,0,3,2,4:T(8,128)(2,1)S(1)} %pad_maximum_fusion), channel_id=1, replica_groups=mesh['groups'=2,'row'=4,'col'=4] {'col'}, dimensions={4} | all-to-all | bytes 524288 | tf_op jit(solution)/shard_map/all_to_all | solution.py:75
  160.7 0.0 reduce-scatter.3.cloned.1.call-update
  160.7 0.0 reduce-scatter.5.cloned.1.call-start
  160.7 20.1 %reduce-scatter.3.cloned.1.call-done = bf16[2,128,1,128]{3,1,0,2:T(8,128)(2,1)} async-done(((bf16[2,128,4,128]{3,1,0,2:T(8,128)(2,1)}), bf16[2,128,1,128]{3,1,0,2:T(8,128)(2,1)}) %reduce-scatter.3.cloned.1.call-update) | async-done | bytes 65552 | tf_op jit(solution)/shard_map/reduce_scatter | solution.py:79
  180.9 0.0 copy-done.4
  180.9 0.9 fusion.45
  181.7 0.1 convert_element_type.117
  181.8 0.8 copy.67
  182.6 1.7 convert_element_type.122
  184.3 0.1 copy.66
  184.4 0.0 copy-start.5
  184.4 0.1 reshape.190
  184.6 0.0 copy-start.2
  184.6 5.6 %fusion.4 = bf16[8192,512]{0,1:T(8,128)(2,1)} fusion(bf16[64,512]{1,0:T(8,128)(2,1)S(1)} %reshape.190, bf16[8192,64]{1,0:T(8,128)(2,1)S(1)} %reshape.178), kind=kOutput, calls=%fused_computation.8 | convolution fusion | flops 541065216 | bytes 9502720 | tf_op jit(solution)/shard_map/dot_general | solution.py:18
  190.2 0.0 copy-done.5
  190.2 5.6 %convolution_convert_fusion = bf16[512,8192]{1,0:T(8,128)(2,1)} fusion(bf16[512,64]{0,1:T(8,128)(2,1)S(1)} %copy-done.5, bf16[64,8192]{1,0:T(8,128)(2,1)S(1)} %copy-done.2), kind=kOutput, calls=%fused_computation.4 | convolution fusion | flops 541065216 | bytes 9502720 | tf_op jit(solution)/shard_map/dot_general | solution.py:25
  195.8 23.6 %reshape.191 = bf16[128,64,2,4,64]{1,0,4,3,2:T(8,128)(2,1)} reshape(bf16[8192,512]{0,1:T(8,128)(2,1)} %fusion.4) | data formatting | bytes 16777216 | tf_op jit(solution)/shard_map/reshape | solution.py:21
  219.4 23.6 %reshape.192 = bf16[2,4,64,128,64]{4,3,2,1,0:T(8,128)(2,1)} reshape(bf16[512,8192]{1,0:T(8,128)(2,1)} %convolution_convert_fusion) | data formatting | bytes 16777216 | tf_op jit(solution)/shard_map/reshape | solution.py:30
  243.0 18.8 %copy.69 = bf16[2,4,64,128,64]{3,2,4,1,0:T(8,128)(2,1)} copy(bf16[2,4,64,128,64]{4,3,2,1,0:T(8,128)(2,1)} %reshape.192) | data formatting | bytes 16777216 | tf_op jit(solution)/shard_map/reshape | solution.py:30
  261.7 14.8 %convolution_convert_fusion.4 = bf16[4,128,4096]{2,1,0:T(8,128)(2,1)} fusion(bf16[128,64,2,4,64]{1,0,4,3,2:T(8,128)(2,1)} %reshape.191, bf16[2,4,64,128,64]{3,2,4,1,0:T(8,128)(2,1)} %copy.69, bf16[128,4096]{1,0:T(8,128)(2,1)S(1)} %copy-done), kind=kOutput, calls=%fused_computation.9 | convolution fusion | flops 1612840960 | bytes 22020096 | tf_op jit(solution)/shard_map/npq,qm->npm/dot_general | solution.py:36
  276.6 6.3 %copy.70 = bf16[4,128,4096]{1,2,0:T(8,128)(2,1)} copy(bf16[4,128,4096]{2,1,0:T(8,128)(2,1)} %convolution_convert_fusion.4) | data formatting | bytes 8388608 | tf_op jit(solution)/shard_map/convert_element_type | solution.py:38
  282.9 10.1 %fusion.24 = bf16[4,64,64,2]{2,1,3,0:T(8,128)(2,1)S(1)} fusion(bf16[4,128,64,64,1]{1,3,2,4,0:T(8,128)(2,1)} %bitcast.118, bf16[128,64,2,4,64]{1,0,4,3,2:T(8,128)(2,1)} %reshape.191), kind=kOutput, calls=%fused_computation.22 | convolution fusion | flops 536936448 | bytes 12648448 | tf_op jit(solution)/shard_map/picnl,nplj->cnij/dot_general | solution.py:42
  293.1 0.1 copy.72
  293.2 0.1 reshape.195
  293.3 5.8 %all_gather.7 = bf16[2,128,512]{2,1,0:T(8,128)(2,1)S(1)} all-gather(bf16[2,128,128]{2,1,0:T(8,128)(2,1)S(1)} %reshape.195), channel_id=1, replica_groups=mesh['groups'=2,'row'=4,'col'=4] {'col'}, dimensions={2}, use_global_device_ids=true | all-gather | bytes 327680 | tf_op jit(solution)/shard_map/all_gather | solution.py:62
  299.1 0.3 fusion.29
  299.4 0.3 fusion.33
  299.7 0.1 fusion.42
  300.0 9.1 %all_to_all.25 = bf16[2,128,1,1,4,128]{5,1,0,3,2,4:T(8,128)(2,1)} all-to-all(bf16[2,128,1,1,4,128]{5,1,0,3,2,4:T(8,128)(2,1)S(1)} %pad_maximum_fusion.1), channel_id=1, replica_groups=mesh['groups'=2,'row'=4,'col'=4] {'col'}, dimensions={4} | all-to-all | bytes 524288 | tf_op jit(solution)/shard_map/all_to_all | solution.py:75
  309.1 0.0 reduce-scatter.5.cloned.1.call-update
  309.2 17.2 %reduce-scatter.5.cloned.1.call-done = bf16[2,128,1,128]{3,1,0,2:T(8,128)(2,1)} async-done(((bf16[2,128,4,128]{3,1,0,2:T(8,128)(2,1)}), bf16[2,128,1,128]{3,1,0,2:T(8,128)(2,1)}) %reduce-scatter.5.cloned.1.call-update) | async-done | bytes 65552 | tf_op jit(solution)/shard_map/reduce_scatter | solution.py:79
  326.3 1.5 convert_add_fusion
  (14 shorter events, 0.2 us)
Async XLA Ops:
  6.5 174.3 %reduce-scatter.3.cloned.1.call-start = ((), (), s32[]{:S(2)}) async-start(), calls=%async_computation.4 | async-start | bytes 327680 | tf_op jit(solution)/shard_map/reduce_scatter | solution.py:79
  18.2 40.6 %copy-start.1 = (bf16[64,8192]{1,0:T(8,128)(2,1)}, bf16[64,8192]{1,0:T(8,128)(2,1)S(1)}, u32[]{:S(2)}) copy-start(bf16[64,8192]{1,0:T(8,128)(2,1)S(1)} %reshape.182) | copy-start | bytes 3145732
  87.9 18.9 %copy-start = (bf16[128,4096]{1,0:T(8,128)(2,1)S(1)}, bf16[128,4096]{1,0:T(8,128)(2,1)}, u32[]{:S(2)}) copy-start(bf16[128,4096]{1,0:T(8,128)(2,1)} %param.4) | copy-start | bytes 3145732
  128.0 52.9 %copy-start.4 = (f32[2,128,128]{2,1,0:T(8,128)S(1)}, f32[2,128,128]{2,1,0:T(8,128)}, u32[]{:S(2)}) copy-start(f32[2,128,128]{2,1,0:T(8,128)} %param.3) | copy-start | bytes 393220
  160.7 165.6 %reduce-scatter.5.cloned.1.call-start = ((), (), s32[]{:S(2)}) async-start(), calls=%async_computation.5 | async-start | bytes 327680 | tf_op jit(solution)/shard_map/reduce_scatter | solution.py:79
  184.4 5.8 %copy-start.5 = (bf16[512,64]{0,1:T(8,128)(2,1)S(1)}, bf16[512,64]{0,1:T(8,128)(2,1)}, u32[]{:S(2)}) copy-start(bf16[512,64]{0,1:T(8,128)(2,1)} %convert_element_type.122) | copy-start | bytes 196612
  184.6 5.6 %copy-start.2 = (bf16[64,8192]{1,0:T(8,128)(2,1)S(1)}, bf16[64,8192]{1,0:T(8,128)(2,1)}, u32[]{:S(2)}) copy-start(bf16[64,8192]{1,0:T(8,128)(2,1)} %copy-done.1) | copy-start | bytes 3145732
  282.9 16.2 %copy-start.3 = (bf16[2,512,512]{2,1,0:T(8,128)(2,1)S(1)}, bf16[2,512,512]{2,1,0:T(8,128)(2,1)}, u32[]{:S(2)}) copy-start(bf16[2,512,512]{2,1,0:T(8,128)(2,1)} %param.5) | copy-start | bytes 3145732
Sparse Core Ops, SparseCore 0:
  160.8 19.9 reduce-scatter.2
  309.3 16.9 reduce-scatter.4
where the time goes:
time: 339 us; the launch traced here: 335 us
  local copies, waits for them, and re-layouts  173 us (51%)
  matrix products  75.5 us (22%)
  waiting for transfers between devices  37.3 us (11%)
  blocking collectives  31.2 us (9%)
  between operations  13.6 us (4%)
  other arithmetic  4.46 us (1%)
    reshape x4, local copies, waits for them, and re-layouts, pair_self_energy(): right_prod.reshape(2, pair_count, orbitals, aux_count, orbitals)  84.8 us
    reshape x2, local copies, waits for them, and re-layouts, pair_self_energy(): left_prod = left_prod.reshape(aux_count, orbitals, 2, pair_count, orbitals)  47.1 us
    reduce_scatter x2, waiting for transfers between devices, local(): lax.psum_scatter(shuffled.astype(jnp.bfloat16), 'row', scatter_dimension=...  37.3 us
    dot_general x2, matrix products, pair_self_energy(): jnp.einsum('npq,qm->npm', bubble, fit_vectors, preferred_element_type=jnp...  29.7 us
    dot_general x2, matrix products, pair_self_energy(): jnp.einsum('picnl,nplj->cnij', left_prod, screened, preferred_element_typ...  20.2 us
    all_to_all x2, blocking collectives, local(): lax.all_to_all(shaped.astype(jnp.bfloat16), 'col', split_axis=4, concat_a...  18.2 us
    all_gather x2, blocking collectives, local(): segment = lax.all_gather(self_energy, 'col', axis=2, tiled=True)  13 us
    convert_element_type x2, local copies, waits for them, and re-layouts, pair_self_energy(): screened = jnp.einsum('npq,qm->npm', bubble, fit_vectors, preferred_eleme...  12.7 us
  transfers between devices with their start and end apart: 2, of which 2 were waited for; matrix products, arithmetic and copies ran while one was open for 0% of the time, Pallas kernels for 0%

commit v1 on v0

v1 whole, which is shorter than its diff:
```python
import functools
import math

import jax
import jax.numpy as jnp
from jax import lax
from jax.experimental import pallas as pl
from jax.experimental.pallas import tpu as pltpu
from jax.sharding import PartitionSpec as P

ITERS = 2
BF16 = jnp.bfloat16
F32 = jnp.float32
LANES = 128
MIB = 2**20


def dot(a, b):
    return jnp.dot(a, b, preferred_element_type=F32)


def dot_nt(a, b):
    return lax.dot_general(a, b, (((1,), (1,)), ((), ())), preferred_element_type=F32)


def turn_kernel(orbitals, fit_ref, turned_ref, wide):
    flat = fit_ref.shape[1]
    per = LANES // orbitals
    for t in range(flat // LANES):
        wide[t * LANES : (t + 1) * LANES, :] = fit_ref[:, t * LANES : (t + 1) * LANES].astype(F32).T
    for t in range(flat // LANES):
        rows = [wide[pl.ds(t * per + h, orbitals, stride=orbitals), :] for h in range(per)]
        turned_ref[:, t * LANES : (t + 1) * LANES] = jnp.concatenate(rows, axis=0).T.astype(BF16)


def turn(fit, orbitals):
    aux, flat = fit.shape
    return pl.pallas_call(
        functools.partial(turn_kernel, orbitals),
        out_shape=jax.ShapeDtypeStruct((aux, flat), BF16),
        scratch_shapes=[pltpu.VMEM((flat, aux), F32)],
        compiler_params=pltpu.CompilerParams(vmem_limit_bytes=16 * MIB),
        name="turn_fit",
    )(fit)


def energy_kernel(orbitals, green_ref, fit_ref, turned_ref, out_ref, spread, left, under, screened):
    aux = fit_ref.shape[0]
    times = green_ref.shape[2] // orbitals
    new = green_ref.shape[1] // orbitals
    pairs = new * times
    pitch = 2 * orbitals + 1
    per = LANES // orbitals
    flipped = [
        [green_ref[c, a * orbitals : (a + 1) * orbitals, :].T.astype(BF16) for c in range(2)]
        for a in range(new)
    ]
    lhs = jnp.concatenate([flipped[a][c] for a in range(new) for c in range(2)], axis=0)
    zero = jnp.zeros_like(lhs)
    both = [
        jnp.concatenate([lhs if q == h else zero for q in range(per)], axis=1) for h in range(per)
    ]
    for i in range(0, orbitals, 2 * per):
        w = jnp.concatenate(
            [fit_ref[:, (i + per * g) * orbitals : (i + per * (g + 1)) * orbitals] for g in range(2)],
            axis=0,
        )
        for h in range(per):
            res = dot_nt(both[h], w)
            for g in range(2):
                for a in range(new):
                    for c in range(2):
                        for k in range(times):
                            r = ((a * 2 + c) * times + k) * orbitals
                            spread[
                                a * times + k,
                                pl.ds(c * orbitals + i + per * g + h, orbitals, stride=pitch),
                                :,
                            ] = res[r : r + orbitals, g * aux : (g + 1) * aux]
    around = [jnp.concatenate(flipped[a], axis=1) for a in range(new)]
    rows = 2 * orbitals
    for m in range(0, orbitals, 2):
        for n in range(pairs):
            a, k = divmod(n, times)
            x = [spread[n, pl.ds((m + h) * pitch, rows), :].astype(BF16) for h in range(2)]
            for h in range(2):
                left[n, (m + h) * rows : (m + h + 1) * rows, :] = x[h]
            r = dot(around[a][k * orbitals : (k + 1) * orbitals], jnp.concatenate(x, axis=1))
            for h in range(2):
                under[(m + h) * orbitals : (m + h + 1) * orbitals, n * aux : (n + 1) * aux] = r[
                    :, h * aux : (h + 1) * aux
                ].astype(BF16)
    pi = dot(turned_ref[...], under[...]) * (1.0 / orbitals)
    bubble = jnp.concatenate([pi[:, n * aux : (n + 1) * aux].T for n in range(pairs)], axis=0)
    screened[...] = dot(bubble.astype(BF16), fit_ref[...]).astype(BF16)
    scale = (aux * orbitals) ** -0.5
    accs = [jnp.zeros((rows, orbitals), F32) for _ in range(pairs)]
    for m in range(0, orbitals, 2):
        for n in range(pairs):
            a = jnp.concatenate(
                [left[n, (m + h) * rows : (m + h + 1) * rows, :] for h in range(2)], axis=1
            )
            w = screened[n * aux : (n + 1) * aux, m * orbitals : (m + 2) * orbitals]
            b = jnp.concatenate([w[:, :orbitals], w[:, orbitals:]], axis=0)
            accs[n] = accs[n] + dot(a, b)
    for n in range(pairs):
        a, k = divmod(n, times)
        block = (accs[n] * scale).astype(BF16)
        for c in range(2):
            out_ref[
                c, a * orbitals : (a + 1) * orbitals, k * orbitals : (k + 1) * orbitals
            ] = block[c * orbitals : (c + 1) * orbitals]


def energy(green, fit, turned, orbitals):
    aux, flat = fit.shape
    _, rows, span = green.shape
    pairs = rows // orbitals * (span // orbitals)
    return pl.pallas_call(
        functools.partial(energy_kernel, orbitals),
        out_shape=jax.ShapeDtypeStruct((2, rows, span), BF16),
        scratch_shapes=[
            pltpu.VMEM((pairs, orbitals * (2 * orbitals + 1), aux), F32),
            pltpu.VMEM((pairs, 2 * flat, aux), BF16),
            pltpu.VMEM((flat, pairs * aux), BF16),
            pltpu.VMEM((pairs * aux, flat), BF16),
        ],
        compiler_params=pltpu.CompilerParams(vmem_limit_bytes=42 * MIB),
        name="self_energy",
    )(green, fit, turned)


def collide_kernel(offsets, row_devices, place_ref, near_ref, far_ref, *refs):
    pieces, (keep_ref, send_ref, sums) = refs[:-3], refs[-3:]
    row, col = place_ref[0], place_ref[1]
    _, _, rows, span = near_ref.shape
    half = near_ref.shape[0]
    ratio = row_devices // len(pieces)
    blocks = []
    for b in range(2 * half):
        ref, at = (near_ref, b) if b < half else (far_ref, b - half)
        blocks.append(jnp.concatenate([ref[at, c] for c in range(2)], axis=0))
    for s, piece in enumerate(pieces):
        acc = None
        for b, offset in enumerate(offsets):
            at = pl.ds(pl.multiple_of((col ^ offset) * span, span), span)
            h = jnp.concatenate([piece[c, at, :] for c in range(2)], axis=1)
            r = dot(blocks[b], h)
            acc = r if acc is None else acc + r
        width = ratio * span
        real = acc[:rows, :width] - acc[rows:, width:]
        imag = acc[:rows, width:] + acc[rows:, :width]
        for rho in range(ratio):
            t = ((col ^ s) * ratio + rho) ^ row
            sums[t, 0] = real[:, rho * span : (rho + 1) * span]
            sums[t, 1] = imag[:, rho * span : (rho + 1) * span]
    for t in range(row_devices):
        if t & 1:
            send_ref[t // 2] = sums[t].astype(BF16)
        else:
            keep_ref[t // 2] = sums[t]


def collide(place, near, far, pieces, offsets, row_devices):
    _, _, rows, span = near.shape
    shape = (row_devices // 2, 2, rows, span)
    return pl.pallas_call(
        functools.partial(collide_kernel, offsets, row_devices),
        out_shape=(jax.ShapeDtypeStruct(shape, F32), jax.ShapeDtypeStruct(shape, BF16)),
        in_specs=[pl.BlockSpec(memory_space=pltpu.SMEM)]
        + [pl.BlockSpec(memory_space=pltpu.VMEM)] * (2 + len(pieces)),
        scratch_shapes=[pltpu.VMEM((row_devices, 2, rows, span), F32)],
        compiler_params=pltpu.CompilerParams(vmem_limit_bytes=32 * MIB),
        name="collide",
    )(place, near, far, *pieces)


def swap(x, axis, step):
    size = lax.axis_size(axis)
    return lax.ppermute(x, axis, [(d, d ^ step) for d in range(size)])


def bits(size):
    return [1 << b for b in range(size.bit_length() - 1)]


def local(green_start, fit, history):
    orbitals = math.isqrt(fit.shape[1])
    _, rows, span = green_start.shape
    row_devices = lax.axis_size("row")
    col_devices = lax.axis_size("col")
    ratio = row_devices // col_devices
    row, col = lax.axis_index("row"), lax.axis_index("col")
    place = jnp.stack([row, col]).astype(jnp.int32)

    depth = history.shape[1]
    split = history.reshape(2, depth, ratio, col_devices, span)
    pieces = []
    for s in range(col_devices):
        piece = lax.dynamic_index_in_dim(split, col ^ s, axis=3, keepdims=False)
        piece = piece.reshape(2, depth, ratio * span)
        pieces.append(swap(piece, "col", s) if s else piece)

    turned = turn(fit, orbitals)
    green = green_start
    for _ in range(ITERS):
        sigma = energy(green, fit, turned, orbitals)
        near, offsets = sigma[None], [0]
        far = None
        for step in reversed(bits(col_devices)):
            if far is not None:
                near = jnp.concatenate([near, far], axis=0)
            far = swap(near, "col", step)
            offsets = offsets + [o ^ step for o in offsets]
        keep, send = collide(place, near, far, pieces, offsets, row_devices)
        for step in bits(row_devices):
            if step > 1:
                send = keep[1::2].astype(BF16)
                keep = keep[0::2]
            keep = keep + swap(send, "row", step).astype(F32)
        green = green_start + keep[0]
    return green


def solution(mesh):
    in_specs = (P("groups", None, ("row", "col")), P("groups", None), P("groups", "row", "col"))
    out_specs = P("groups", None, ("row", "col"))
    return jax.shard_map(local, mesh=mesh, in_specs=in_specs, out_specs=out_specs, check_vma=False)
```

time: 339 us -> 74.9 us (0.22); the launches traced: 335 us -> 74.7 us
  local copies, waits for them, and re-layouts: 173 us -> 7.18 us
  matrix products: 75.5 us -> 0 us
  blocking collectives: 31.2 us -> 0 us
  Pallas kernels: 0 us -> 22.2 us
  starting transfers between devices: 0.04 us -> 14.6 us
  between operations: 13.6 us -> 0.13 us
  waiting for transfers between devices: 37.3 us -> 29.8 us
  other arithmetic: 4.46 us -> 0.86 us
    reshape x14 -> x1, local copies, waits for them, and re-layouts: 139 us -> 1.52 us  [local(): split = history.reshape(2, depth, ratio, col_devices, span)]
    dot_general x12 -> x0, matrix products: 75.5 us -> none  [the longest x2 29.7 us: pair_self_energy(): jnp.einsum('npq,qm->npm', bubble, fit_vectors, preferred_element_type=jnp...]
    reduce_scatter x2 -> x0, waiting for transfers between devices: 37.3 us -> none  [local(): lax.psum_scatter(shuffled.astype(jnp.bfloat16), 'row', scatter_dimension=...]
    ppermute x0 -> x11, waiting for transfers between devices: none -> 29.8 us  [swap(): return lax.ppermute(x, axis, [(d, d ^ step) for d in range(size)])]
    convert_element_type x11 -> x0, local copies, waits for them, and re-layouts: 27.1 us -> none  [the longest x2 12.7 us: pair_self_energy(): screened = jnp.einsum('npq,qm->npm', bubble, fit_vectors, preferred_eleme...]
    pallas_call x0 -> x5, Pallas kernels: none -> 22.2 us  [the longest x2 18.1 us: energy(): pl.pallas_call(functools.partial(energy_kernel, orbitals), out_shape=jax....]
    all_to_all x2 -> x0, blocking collectives: 18.2 us -> none  [local(): lax.all_to_all(shaped.astype(jnp.bfloat16), 'col', split_axis=4, concat_a...]
    ppermute x0 -> x11, starting transfers between devices: none -> 14.6 us  [swap(): return lax.ppermute(x, axis, [(d, d ^ step) for d in range(size)])]
  transfers between devices with their start and end apart: 2 -> 11, of which waited for: 2 -> 9; matrix products, arithmetic and copies ran while one was open for 0% -> 8% of each run, Pallas kernels for 0% -> 0%
where the time goes in v1:
time: 74.9 us; the launch traced here: 74.7 us
  waiting for transfers between devices  29.8 us (40%)
  Pallas kernels  22.2 us (30%)
  starting transfers between devices  14.6 us (19%)
  local copies, waits for them, and re-layouts  7.18 us (10%)
  other arithmetic  0.86 us (1%)
    ppermute x11, waiting for transfers between devices, swap(): return lax.ppermute(x, axis, [(d, d ^ step) for d in range(size)])  29.8 us
    pallas_call x2, Pallas kernels, energy(): pl.pallas_call(functools.partial(energy_kernel, orbitals), out_shape=jax....  18.1 us
    ppermute x11, starting transfers between devices, swap(): return lax.ppermute(x, axis, [(d, d ^ step) for d in range(size)])  14.6 us
    unnamed x10, local copies, waits for them, and re-layouts  3.47 us
    pallas_call x2, Pallas kernels, collide(): pl.pallas_call(functools.partial(collide_kernel, offsets, row_devices), o...  2.54 us
    dynamic_slice x1, local copies, waits for them, and re-layouts, local(): piece = lax.dynamic_index_in_dim(split, col ^ s, axis=3, keepdims=False)  2.16 us
    reshape x1, local copies, waits for them, and re-layouts, local(): split = history.reshape(2, depth, ratio, col_devices, span)  1.52 us
  transfers between devices with their start and end apart: 11, of which 9 were waited for; matrix products, arithmetic and copies ran while one was open for 8% of the time, Pallas kernels for 0%

profile of v1, /device:TPU:0, one launch (start us, length us, event | category | flops | bytes accessed | tf_op | source)
XLA Modules:
  0.0 74.7 jit_solution(16208332109315394875)
XLA Ops:
  0.0 0.0 copy-start
  0.0 1.2 %copy-done = bf16[128,4096]{1,0:T(8,128)(2,1)S(1)} copy-done((bf16[128,4096]{1,0:T(8,128)(2,1)S(1)}, bf16[128,4096]{1,0:T(8,128)(2,1)}, u32[]{:S(2)}) %copy-start) | copy-done | bytes 1048600
  1.2 0.0 copy-start.1
  1.2 0.0 copy-start.2
  1.2 1.5 %turn_fit.1.turned_ref = bf16[128,4096]{1,0:T(8,128)(2,1)S(1)} custom-call(bf16[128,4096]{1,0:T(8,128)(2,1)S(1)} %copy-done), custom_call_target="tpu_custom_call" | custom-call | tf_op jit(solution)/shard_map/turn_fit/pallas_call | solution.py:38
  2.7 0.0 copy-done.1
  2.7 0.0 copy-done.2
  2.8 9.1 %self_energy.2 = bf16[2,128,128]{2,1,0:T(8,128)(2,1)S(1)} custom-call(f32[2,128,128]{2,1,0:T(8,128)S(1)} %copy-done.2, bf16[128,4096]{1,0:T(8,128)(2,1)S(1)} %copy-done.1, bf16[128,4096]{1,0:T(8,128)(2,1)S(1)} %turn_fit.1.turned_ref), custom_call_target="tpu_custom_call" | custom-call | tf_op jit(solution)/shard_map/self_energy/pallas_call | solution.py:119
  11.8 3.0 %collective-permute-start = (bf16[1,2,128,128]{3,2,1,0:T(8,128)(2,1)S(1)}, bf16[1,2,128,128]{3,2,1,0:T(8,128)(2,1)S(1)}, u32[]{:S(2)}, u32[]{:S(2)}) collective-permute-start(bf16[1,2,128,128]{3,2,1,0:T(8,128)(2,1)S(1)} %bitcast.26), channel_id=1, source_target_pairs={{0,2},{1,3},{2,0},{3,1},{4,6},{5,7},{6,4},{7,5},{8,10},{9,11},{10,... | collective-permute-start | bytes 196616 | tf_op jit(solution)/shard_map/ppermute | solution.py:180
  14.8 1.5 %reshape.19 = bf16[2,512,1,4,128]{4,3,1,0,2:T(4,128)(2,1)S(1)} reshape(bf16[2,512,512]{2,1,0:T(8,128)(2,1)} %param.5) | data formatting | bytes 2097152 | tf_op jit(solution)/shard_map/reshape | solution.py:197
  16.4 2.2 %constant_dynamic-slice_fusion = (bf16[2,512,1,1,128]{4,3,1,0,2:T(2,128)(2,1)S(1)}, bf16[2,512,1,1,128]{4,3,1,0,2:T(2,128)(2,1)S(1)}, bf16[2,512,1,1,128]{4,3,1,...) fusion(bf16[2,512,1,4,128]{4,3,1,0,2:T(4,128)(2,1)S(1)} %reshape.19, s32[]{:T(128)S(6)} %select_n.16, s32[]{:T(128)S(6)} %select_n.15, ...), kind=kLoop, calls=%fused_computation.16 | loop fusion | bytes 2097168 | tf_op jit(solution)/shard_map/jit(dynamic_index_in_dim)/dynamic_slice | solution.py:200
  18.5 0.7 copy.18
  19.3 0.0 collective-permute-start.2
  19.3 0.7 copy.17
  20.0 0.0 collective-permute-start.3
  20.0 0.7 copy.16
  20.8 1.8 %collective-permute-start.4 = (bf16[2,512,128]{2,1,0:T(8,128)(2,1)}, bf16[2,512,128]{2,1,0:T(8,128)(2,1)S(1)}, u32[]{:S(2)}, u32[]{:S(2)}) collective-permute-start(bf16[2,512,128]{2,1,0:T(8,128)(2,1)} %bitcast.20), channel_id=1, source_target_pairs={{0,3},{1,2},{2,1},{3,0},{4,7},{5,6},{6,5},{7,4},{8,11},{9,10},{10,... | collective-permute-start | bytes 786440 | tf_op jit(solution)/shard_map/ppermute | solution.py:180
  22.6 0.0 collective-permute-done
  22.6 0.3 collective-permute-start.1
  23.0 0.1 pad_add_fusion.place_ref
  23.1 0.9 %collective-permute-done.1.far_ref = bf16[2,2,128,128]{3,2,1,0:T(8,128)(2,1)S(1)} collective-permute-done((bf16[2,2,128,128]{3,2,1,0:T(8,128)(2,1)S(1)}, bf16[2,2,128,128]{3,2,1,0:T(8,128)(2,1)S(1)}, u32[]{:S(2)}, u32[]{:S(2)}) %collective-permute-start.1) | collective-permute-done | bytes 131104 | tf_op jit(solution)/shard_map/ppermute | solution.py:180
  24.0 0.0 collective-permute-done.2.refs_1_
  24.0 5.3 %collective-permute-done.3.refs_2_ = bf16[2,512,128]{2,1,0:T(8,128)(2,1)S(1)} collective-permute-done((bf16[2,512,128]{2,1,0:T(8,128)(2,1)}, bf16[2,512,128]{2,1,0:T(8,128)(2,1)S(1)}, u32[]{:S(2)}, u32[]{:S(2)}) %collective-permute-start.3) | collective-permute-done | bytes 262176 | tf_op jit(solution)/shard_map/ppermute | solution.py:180
  29.3 4.8 %collective-permute-done.4.refs_3_ = bf16[2,512,128]{2,1,0:T(8,128)(2,1)S(1)} collective-permute-done((bf16[2,512,128]{2,1,0:T(8,128)(2,1)}, bf16[2,512,128]{2,1,0:T(8,128)(2,1)S(1)}, u32[]{:S(2)}, u32[]{:S(2)}) %collective-permute-start.4) | collective-permute-done | bytes 262176 | tf_op jit(solution)/shard_map/ppermute | solution.py:180
  34.2 1.3 %collide.2 = (f32[2,2,128,128]{3,2,1,0:T(8,128)S(1)}, bf16[2,2,128,128]{3,2,1,0:T(8,128)(2,1)S(1)}) custom-call(s32[2]{0:T(128)S(1)} %pad_add_fusion.place_ref, bf16[2,2,128,128]{3,2,1,0:T(8,128)(2,1)S(1)} %pad_maximum_fusion.near_ref, bf16[2,2,128,128]{3,2,1,0:T(8,128)(2,1)S(1)} %collective-permute-done.1.far_ref, bf16[2,512,128]{2,1,0:T(8,128)(2,1)S(1)} %bitcast.24, ...), custom_call_target="tpu_custom_call" | custom-call | tf_op jit(solution)/shard_map/collide/pallas_call | solution.py:167
  35.4 1.6 %collective-permute-start.5 = (bf16[2,2,128,128]{3,2,1,0:T(8,128)(2,1)S(1)}, bf16[2,2,128,128]{3,2,1,0:T(8,128)(2,1)S(1)}, u32[]{:S(2)}, u32[]{:S(2)}) collective-permute-start(bf16[2,2,128,128]{3,2,1,0:T(8,128)(2,1)S(1)} %get-tuple-element.10), channel_id=1, source_target_pairs={{0,4},{4,0},{8,12},{12,8},{1,5},{5,1},{9,13},{13,9},{2,6},{6,2},{1... | collective-permute-start | bytes 393224 | tf_op jit(solution)/shard_map/ppermute | solution.py:180
  37.1 4.0 %collective-permute-done.5 = bf16[2,2,128,128]{3,2,1,0:T(8,128)(2,1)S(1)} collective-permute-done((bf16[2,2,128,128]{3,2,1,0:T(8,128)(2,1)S(1)}, bf16[2,2,128,128]{3,2,1,0:T(8,128)(2,1)S(1)}, u32[]{:S(2)}, u32[]{:S(2)}) %collective-permute-start.5) | collective-permute-done | bytes 131104 | tf_op jit(solution)/shard_map/ppermute | solution.py:180
  41.2 2.7 %collective-permute-start.6 = (bf16[1,2,128,128]{3,2,1,0:T(8,128)(2,1)S(1)}, bf16[1,2,128,128]{3,2,1,0:T(8,128)(2,1)S(1)}, u32[]{:S(2)}, u32[]{:S(2)}) collective-permute-start(bf16[1,2,128,128]{3,2,1,0:T(8,128)(2,1)S(1)} %slice.39), channel_id=1, source_target_pairs={{0,8},{4,12},{8,0},{12,4},{1,9},{5,13},{9,1},{13,5},{2,10},{6,14},... | collective-permute-start | bytes 196616 | tf_op jit(solution)/shard_map/ppermute | solution.py:180
  43.8 2.7 %collective-permute-done.6 = bf16[1,2,128,128]{3,2,1,0:T(8,128)(2,1)S(1)} collective-permute-done((bf16[1,2,128,128]{3,2,1,0:T(8,128)(2,1)S(1)}, bf16[1,2,128,128]{3,2,1,0:T(8,128)(2,1)S(1)}, u32[]{:S(2)}, u32[]{:S(2)}) %collective-permute-start.6) | collective-permute-done | bytes 65568 | tf_op jit(solution)/shard_map/ppermute | solution.py:180
  46.6 9.1 %self_energy.3 = bf16[2,128,128]{2,1,0:T(8,128)(2,1)S(1)} custom-call(f32[2,128,128]{2,1,0:T(8,128)S(1)} %fusion.3.green_ref, bf16[128,4096]{1,0:T(8,128)(2,1)S(1)} %copy-done.1, bf16[128,4096]{1,0:T(8,128)(2,1)S(1)} %turn_fit.1.turned_ref), custom_call_target="tpu_custom_call" | custom-call | tf_op jit(solution)/shard_map/self_energy/pallas_call | solution.py:119
  55.6 0.6 collective-permute-start.7
  56.2 3.8 %collective-permute-done.7 = bf16[1,2,128,128]{3,2,1,0:T(8,128)(2,1)S(1)} collective-permute-done((bf16[1,2,128,128]{3,2,1,0:T(8,128)(2,1)S(1)}, bf16[1,2,128,128]{3,2,1,0:T(8,128)(2,1)S(1)}, u32[]{:S(2)}, u32[]{:S(2)}) %collective-permute-start.7) | collective-permute-done | bytes 65568 | tf_op jit(solution)/shard_map/ppermute | solution.py:180
  60.0 0.1 collective-permute-start.8
  60.1 1.3 %collective-permute-done.8.far_ref = bf16[2,2,128,128]{3,2,1,0:T(8,128)(2,1)S(1)} collective-permute-done((bf16[2,2,128,128]{3,2,1,0:T(8,128)(2,1)S(1)}, bf16[2,2,128,128]{3,2,1,0:T(8,128)(2,1)S(1)}, u32[]{:S(2)}, u32[]{:S(2)}) %collective-permute-start.8) | collective-permute-done | bytes 131104 | tf_op jit(solution)/shard_map/ppermute | solution.py:180
  61.4 1.3 %collide.3 = (f32[2,2,128,128]{3,2,1,0:T(8,128)S(1)}, bf16[2,2,128,128]{3,2,1,0:T(8,128)(2,1)S(1)}) custom-call(s32[2]{0:T(128)S(1)} %pad_add_fusion.place_ref, bf16[2,2,128,128]{3,2,1,0:T(8,128)(2,1)S(1)} %pad_maximum_fusion.1.near_ref, bf16[2,2,128,128]{3,2,1,0:T(8,128)(2,1)S(1)} %collective-permute-done.8.far_ref, bf16[2,512,128]{2,1,0:T(8,128)(2,1)S(1)} %bitcast.25, ...), custom_call_target="tpu_custom_call" | custom-call | tf_op jit(solution)/shard_map/collide/pallas_call | solution.py:167
  62.7 1.5 %collective-permute-start.9 = (bf16[2,2,128,128]{3,2,1,0:T(8,128)(2,1)S(1)}, bf16[2,2,128,128]{3,2,1,0:T(8,128)(2,1)S(1)}, u32[]{:S(2)}, u32[]{:S(2)}) collective-permute-start(bf16[2,2,128,128]{3,2,1,0:T(8,128)(2,1)S(1)} %get-tuple-element.12), channel_id=1, source_target_pairs={{0,4},{4,0},{8,12},{12,8},{1,5},{5,1},{9,13},{13,9},{2,6},{6,2},{1... | collective-permute-start | bytes 393224 | tf_op jit(solution)/shard_map/ppermute | solution.py:180
  64.2 4.1 %collective-permute-done.9 = bf16[2,2,128,128]{3,2,1,0:T(8,128)(2,1)S(1)} collective-permute-done((bf16[2,2,128,128]{3,2,1,0:T(8,128)(2,1)S(1)}, bf16[2,2,128,128]{3,2,1,0:T(8,128)(2,1)S(1)}, u32[]{:S(2)}, u32[]{:S(2)}) %collective-permute-start.9) | collective-permute-done | bytes 131104 | tf_op jit(solution)/shard_map/ppermute | solution.py:180
  68.3 2.9 %collective-permute-start.10 = (bf16[1,2,128,128]{3,2,1,0:T(8,128)(2,1)S(1)}, bf16[1,2,128,128]{3,2,1,0:T(8,128)(2,1)S(1)}, u32[]{:S(2)}, u32[]{:S(2)}) collective-permute-start(bf16[1,2,128,128]{3,2,1,0:T(8,128)(2,1)S(1)} %slice.38), channel_id=1, source_target_pairs={{0,8},{4,12},{8,0},{12,4},{1,9},{5,13},{9,1},{13,5},{2,10},{6,14},... | collective-permute-start | bytes 196616 | tf_op jit(solution)/shard_map/ppermute | solution.py:180
  71.3 2.8 %collective-permute-done.10 = bf16[1,2,128,128]{3,2,1,0:T(8,128)(2,1)S(1)} collective-permute-done((bf16[1,2,128,128]{3,2,1,0:T(8,128)(2,1)S(1)}, bf16[1,2,128,128]{3,2,1,0:T(8,128)(2,1)S(1)}, u32[]{:S(2)}, u32[]{:S(2)}) %collective-permute-start.10) | collective-permute-done | bytes 65568 | tf_op jit(solution)/shard_map/ppermute | solution.py:180
  74.0 0.7 fusion.1
  (8 shorter events, 0.2 us)
Async XLA Ops:
  0.0 1.2 %copy-start = (bf16[128,4096]{1,0:T(8,128)(2,1)S(1)}, bf16[128,4096]{1,0:T(8,128)(2,1)}, u32[]{:S(2)}) copy-start(bf16[128,4096]{1,0:T(8,128)(2,1)} %fit_ref.5) | copy-start | bytes 3145732
  1.2 1.5 %copy-start.1 = (bf16[128,4096]{1,0:T(8,128)(2,1)S(1)}, bf16[128,4096]{1,0:T(8,128)(2,1)}, u32[]{:S(2)}) copy-start(bf16[128,4096]{1,0:T(8,128)(2,1)} %fit_ref.5) | copy-start | bytes 3145732
  1.2 1.5 %copy-start.2 = (f32[2,128,128]{2,1,0:T(8,128)S(1)}, f32[2,128,128]{2,1,0:T(8,128)}, u32[]{:S(2)}) copy-start(f32[2,128,128]{2,1,0:T(8,128)} %green_ref.1) | copy-start | bytes 393220
  11.8 10.8 %collective-permute-start = (bf16[1,2,128,128]{3,2,1,0:T(8,128)(2,1)S(1)}, bf16[1,2,128,128]{3,2,1,0:T(8,128)(2,1)S(1)}, u32[]{:S(2)}, u32[]{:S(2)}) collective-permute-start(bf16[1,2,128,128]{3,2,1,0:T(8,128)(2,1)S(1)} %bitcast.26), channel_id=1, source_target_pairs={{0,2},{1,3},{2,0},{3,1},{4,6},{5,7},{6,4},{7,5},{8,10},{9,11},{10,... | collective-permute-start | bytes 196616 | tf_op jit(solution)/shard_map/ppermute | solution.py:180
  19.3 4.8 %collective-permute-start.2 = (bf16[2,512,128]{2,1,0:T(8,128)(2,1)}, bf16[2,512,128]{2,1,0:T(8,128)(2,1)S(1)}, u32[]{:S(2)}, u32[]{:S(2)}) collective-permute-start(bf16[2,512,128]{2,1,0:T(8,128)(2,1)} %bitcast.22), channel_id=1, source_target_pairs={{0,1},{1,0},{2,3},{3,2},{4,5},{5,4},{6,7},{7,6},{8,9},{9,8},{10,11... | collective-permute-start | bytes 786440 | tf_op jit(solution)/shard_map/ppermute | solution.py:180
  20.0 9.3 %collective-permute-start.3 = (bf16[2,512,128]{2,1,0:T(8,128)(2,1)}, bf16[2,512,128]{2,1,0:T(8,128)(2,1)S(1)}, u32[]{:S(2)}, u32[]{:S(2)}) collective-permute-start(bf16[2,512,128]{2,1,0:T(8,128)(2,1)} %bitcast.21), channel_id=1, source_target_pairs={{0,2},{1,3},{2,0},{3,1},{4,6},{5,7},{6,4},{7,5},{8,10},{9,11},{10,... | collective-permute-start | bytes 786440 | tf_op jit(solution)/shard_map/ppermute | solution.py:180
  20.8 13.4 %collective-permute-start.4 = (bf16[2,512,128]{2,1,0:T(8,128)(2,1)}, bf16[2,512,128]{2,1,0:T(8,128)(2,1)S(1)}, u32[]{:S(2)}, u32[]{:S(2)}) collective-permute-start(bf16[2,512,128]{2,1,0:T(8,128)(2,1)} %bitcast.20), channel_id=1, source_target_pairs={{0,3},{1,2},{2,1},{3,0},{4,7},{5,6},{6,5},{7,4},{8,11},{9,10},{10,... | collective-permute-start | bytes 786440 | tf_op jit(solution)/shard_map/ppermute | solution.py:180
  22.6 1.4 %collective-permute-start.1 = (bf16[2,2,128,128]{3,2,1,0:T(8,128)(2,1)S(1)}, bf16[2,2,128,128]{3,2,1,0:T(8,128)(2,1)S(1)}, u32[]{:S(2)}, u32[]{:S(2)}) collective-permute-start(bf16[2,2,128,128]{3,2,1,0:T(8,128)(2,1)S(1)} %pad_maximum_fusion.near_ref), channel_id=1, source_target_pairs={{0,1},{1,0},{2,3},{3,2},{4,5},{5,4},{6,7},{7,6},{8,9},{9,8},{10,11... | collective-permute-start | bytes 393224 | tf_op jit(solution)/shard_map/ppermute | solution.py:180
  35.4 5.7 %collective-permute-start.5 = (bf16[2,2,128,128]{3,2,1,0:T(8,128)(2,1)S(1)}, bf16[2,2,128,128]{3,2,1,0:T(8,128)(2,1)S(1)}, u32[]{:S(2)}, u32[]{:S(2)}) collective-permute-start(bf16[2,2,128,128]{3,2,1,0:T(8,128)(2,1)S(1)} %get-tuple-element.10), channel_id=1, source_target_pairs={{0,4},{4,0},{8,12},{12,8},{1,5},{5,1},{9,13},{13,9},{2,6},{6,2},{1... | collective-permute-start | bytes 393224 | tf_op jit(solution)/shard_map/ppermute | solution.py:180
  41.2 5.4 %collective-permute-start.6 = (bf16[1,2,128,128]{3,2,1,0:T(8,128)(2,1)S(1)}, bf16[1,2,128,128]{3,2,1,0:T(8,128)(2,1)S(1)}, u32[]{:S(2)}, u32[]{:S(2)}) collective-permute-start(bf16[1,2,128,128]{3,2,1,0:T(8,128)(2,1)S(1)} %slice.39), channel_id=1, source_target_pairs={{0,8},{4,12},{8,0},{12,4},{1,9},{5,13},{9,1},{13,5},{2,10},{6,14},... | collective-permute-start | bytes 196616 | tf_op jit(solution)/shard_map/ppermute | solution.py:180
  55.6 4.3 %collective-permute-start.7 = (bf16[1,2,128,128]{3,2,1,0:T(8,128)(2,1)S(1)}, bf16[1,2,128,128]{3,2,1,0:T(8,128)(2,1)S(1)}, u32[]{:S(2)}, u32[]{:S(2)}) collective-permute-start(bf16[1,2,128,128]{3,2,1,0:T(8,128)(2,1)S(1)} %bitcast.28), channel_id=1, source_target_pairs={{0,2},{1,3},{2,0},{3,1},{4,6},{5,7},{6,4},{7,5},{8,10},{9,11},{10,... | collective-permute-start | bytes 196616 | tf_op jit(solution)/shard_map/ppermute | solution.py:180
  60.0 1.4 %collective-permute-start.8 = (bf16[2,2,128,128]{3,2,1,0:T(8,128)(2,1)S(1)}, bf16[2,2,128,128]{3,2,1,0:T(8,128)(2,1)S(1)}, u32[]{:S(2)}, u32[]{:S(2)}) collective-permute-start(bf16[2,2,128,128]{3,2,1,0:T(8,128)(2,1)S(1)} %pad_maximum_fusion.1.near_ref), channel_id=1, source_target_pairs={{0,1},{1,0},{2,3},{3,2},{4,5},{5,4},{6,7},{7,6},{8,9},{9,8},{10,11... | collective-permute-start | bytes 393224 | tf_op jit(solution)/shard_map/ppermute | solution.py:180
  62.7 5.6 %collective-permute-start.9 = (bf16[2,2,128,128]{3,2,1,0:T(8,128)(2,1)S(1)}, bf16[2,2,128,128]{3,2,1,0:T(8,128)(2,1)S(1)}, u32[]{:S(2)}, u32[]{:S(2)}) collective-permute-start(bf16[2,2,128,128]{3,2,1,0:T(8,128)(2,1)S(1)} %get-tuple-element.12), channel_id=1, source_target_pairs={{0,4},{4,0},{8,12},{12,8},{1,5},{5,1},{9,13},{13,9},{2,6},{6,2},{1... | collective-permute-start | bytes 393224 | tf_op jit(solution)/shard_map/ppermute | solution.py:180
  68.3 5.7 %collective-permute-start.10 = (bf16[1,2,128,128]{3,2,1,0:T(8,128)(2,1)S(1)}, bf16[1,2,128,128]{3,2,1,0:T(8,128)(2,1)S(1)}, u32[]{:S(2)}, u32[]{:S(2)}) collective-permute-start(bf16[1,2,128,128]{3,2,1,0:T(8,128)(2,1)S(1)} %slice.38), channel_id=1, source_target_pairs={{0,8},{4,12},{8,0},{12,4},{1,9},{5,13},{9,1},{13,5},{2,10},{6,14},... | collective-permute-start | bytes 196616 | tf_op jit(solution)/shard_map/ppermute | solution.py:180

commit v2 on v1

--- a/solution.py
+++ b/solution.py
@@ -23,29 +23,47 @@
     return lax.dot_general(a, b, (((1,), (1,)), ((), ())), preferred_element_type=F32)
 
 
-def turn_kernel(orbitals, fit_ref, turned_ref, wide):
-    flat = fit_ref.shape[1]
-    per = LANES // orbitals
-    for t in range(flat // LANES):
-        wide[t * LANES : (t + 1) * LANES, :] = fit_ref[:, t * LANES : (t + 1) * LANES].astype(F32).T
-    for t in range(flat // LANES):
-        rows = [wide[pl.ds(t * per + h, orbitals, stride=orbitals), :] for h in range(per)]
-        turned_ref[:, t * LANES : (t + 1) * LANES] = jnp.concatenate(rows, axis=0).T.astype(BF16)
-
-
-def turn(fit, orbitals):
-    aux, flat = fit.shape
+def split_kernel(span, place_ref, history_ref, *refs):
+    pieces, sems = refs[:-1], refs[-1]
+    ratio = pieces[0].shape[2] // span
+    copies = []
+    for s, piece in enumerate(pieces):
+        for rho in range(ratio):
+            at = pl.multiple_of((rho * len(pieces) + (place_ref[1] ^ s)) * span, span)
+            copies.append(
+                pltpu.make_async_copy(
+                    history_ref.at[:, :, pl.ds(at, span)],
+                    piece.at[:, :, pl.ds(rho * span, span)],
+                    sems.at[s, rho],
+                )
+            )
+    for copy in copies:
+        copy.start()
+    for copy in copies:
+        copy.wait()
+
+
+def split_history(place, history, span, col_devices):
+    _, depth, width = history.shape
+    ratio = width // span // col_devices
+    piece = jax.ShapeDtypeStruct((2, depth, ratio * span), BF16)
     return pl.pallas_call(
-        functools.partial(turn_kernel, orbitals),
-        out_shape=jax.ShapeDtypeStruct((aux, flat), BF16),
-        scratch_shapes=[pltpu.VMEM((flat, aux), F32)],
+        functools.partial(split_kernel, span),
+        out_shape=[piece] * col_devices,
+        in_specs=[pl.BlockSpec(memory_space=pltpu.SMEM), pl.BlockSpec(memory_space=pltpu.VMEM)],
+        out_specs=[pl.BlockSpec(memory_space=pl.ANY)] * col_devices,
+        scratch_shapes=[pltpu.SemaphoreType.DMA((col_devices, ratio))],
         compiler_params=pltpu.CompilerParams(vmem_limit_bytes=16 * MIB),
-        name="turn_fit",
-    )(fit)
-
-
-def energy_kernel(orbitals, green_ref, fit_ref, turned_ref, out_ref, spread, left, under, screened):
-    aux = fit_ref.shape[0]
+        name="split_history",
+    )(place, history)
+
+
+def energy_kernel(orbitals, turn, green_ref, fit_ref, *refs):
+    if turn:
+        out_ref, turned_ref, spread, left, under, screened, wide = refs
+    else:
+        turned_ref, out_ref, spread, left, under, screened = refs
+    aux, flat = fit_ref.shape
     times = green_ref.shape[2] // orbitals
     new = green_ref.shape[1] // orbitals
     pairs = new * times
@@ -61,6 +79,10 @@
         jnp.concatenate([lhs if q == h else zero for q in range(per)], axis=1) for h in range(per)
     ]
     for i in range(0, orbitals, 2 * per):
+        if turn:
+            for t in range(i // per, i // per + 2):
+                at = slice(t * LANES, (t + 1) * LANES)
+                wide[at, :] = fit_ref[:, at].astype(F32).T
         w = jnp.concatenate(
             [fit_ref[:, (i + per * g) * orbitals : (i + per * (g + 1)) * orbitals] for g in range(2)],
             axis=0,
@@ -80,6 +102,10 @@
     around = [jnp.concatenate(flipped[a], axis=1) for a in range(new)]
     rows = 2 * orbitals
     for m in range(0, orbitals, 2):
+        if turn and m % per == 0:
+            x = [wide[pl.ds(m + h, orbitals, stride=orbitals), :] for h in range(per)]
+            at = slice(m * orbitals, (m + per) * orbitals)
+            turned_ref[:, at] = jnp.concatenate(x, axis=0).T.astype(BF16)
         for n in range(pairs):
             a, k = divmod(n, times)
             x = [spread[n, pl.ds((m + h) * pitch, rows), :].astype(BF16) for h in range(2)]
@@ -116,22 +142,25 @@
     aux, flat = fit.shape
     _, rows, span = green.shape
     pairs = rows // orbitals * (span // orbitals)
+    turn = turned is None
+    out_shape = jax.ShapeDtypeStruct((2, rows, span), BF16)
+    scratch = [
+        pltpu.VMEM((pairs, orbitals * (2 * orbitals + 1), aux), F32),
+        pltpu.VMEM((pairs, 2 * flat, aux), BF16),
+        pltpu.VMEM((flat, pairs * aux), BF16),
+        pltpu.VMEM((pairs * aux, flat), BF16),
+    ]
     return pl.pallas_call(
-        functools.partial(energy_kernel, orbitals),
-        out_shape=jax.ShapeDtypeStruct((2, rows, span), BF16),
-        scratch_shapes=[
-            pltpu.VMEM((pairs, orbitals * (2 * orbitals + 1), aux), F32),
-            pltpu.VMEM((pairs, 2 * flat, aux), BF16),
-            pltpu.VMEM((flat, pairs * aux), BF16),
-            pltpu.VMEM((pairs * aux, flat), BF16),
-        ],
-        compiler_params=pltpu.CompilerParams(vmem_limit_bytes=42 * MIB),
+        functools.partial(energy_kernel, orbitals, turn),
+        out_shape=[out_shape, jax.ShapeDtypeStruct((aux, flat), BF16)] if turn else out_shape,
+        scratch_shapes=scratch + [pltpu.VMEM((flat, aux), F32)] * turn,
+        compiler_params=pltpu.CompilerParams(vmem_limit_bytes=44 * MIB),
         name="self_energy",
-    )(green, fit, turned)
+    )(*((green, fit) if turn else (green, fit, turned)))
 
 
 def collide_kernel(offsets, row_devices, place_ref, near_ref, far_ref, *refs):
-    pieces, (keep_ref, send_ref, sums) = refs[:-3], refs[-3:]
+    pieces, keep_ref, sends, sums = refs[: -row_devices - 1], refs[-row_devices - 1], refs[-row_devices:-1], refs[-1]
     row, col = place_ref[0], place_ref[1]
     _, _, rows, span = near_ref.shape
     half = near_ref.shape[0]
@@ -154,19 +183,18 @@
             t = ((col ^ s) * ratio + rho) ^ row
             sums[t, 0] = real[:, rho * span : (rho + 1) * span]
             sums[t, 1] = imag[:, rho * span : (rho + 1) * span]
-    for t in range(row_devices):
-        if t & 1:
-            send_ref[t // 2] = sums[t].astype(BF16)
-        else:
-            keep_ref[t // 2] = sums[t]
+    keep_ref[...] = sums[0]
+    for t in range(1, row_devices):
+        sends[t - 1][...] = sums[t].astype(BF16)
 
 
 def collide(place, near, far, pieces, offsets, row_devices):
     _, _, rows, span = near.shape
-    shape = (row_devices // 2, 2, rows, span)
+    shape = (2, rows, span)
     return pl.pallas_call(
         functools.partial(collide_kernel, offsets, row_devices),
-        out_shape=(jax.ShapeDtypeStruct(shape, F32), jax.ShapeDtypeStruct(shape, BF16)),
+        out_shape=[jax.ShapeDtypeStruct(shape, F32)]
+        + [jax.ShapeDtypeStruct(shape, BF16)] * (row_devices - 1),
         in_specs=[pl.BlockSpec(memory_space=pltpu.SMEM)]
         + [pl.BlockSpec(memory_space=pltpu.VMEM)] * (2 + len(pieces)),
         scratch_shapes=[pltpu.VMEM((row_devices, 2, rows, span), F32)],
@@ -189,22 +217,18 @@
     _, rows, span = green_start.shape
     row_devices = lax.axis_size("row")
     col_devices = lax.axis_size("col")
-    ratio = row_devices // col_devices
-    row, col = lax.axis_index("row"), lax.axis_index("col")
-    place = jnp.stack([row, col]).astype(jnp.int32)
-
-    depth = history.shape[1]
-    split = history.reshape(2, depth, ratio, col_devices, span)
-    pieces = []
-    for s in range(col_devices):
-        piece = lax.dynamic_index_in_dim(split, col ^ s, axis=3, keepdims=False)
-        piece = piece.reshape(2, depth, ratio * span)
-        pieces.append(swap(piece, "col", s) if s else piece)
-
-    turned = turn(fit, orbitals)
-    green = green_start
+    place = jnp.stack([lax.axis_index("row"), lax.axis_index("col")]).astype(jnp.int32)
+
+    pieces = split_history(place, history, span, col_devices)
+    pieces = [swap(piece, "col", s) if s else piece for s, piece in enumerate(pieces)]
+
+    green, turned = green_start, None
     for _ in range(ITERS):
-        sigma = energy(green, fit, turned, orbitals)
+        if turned is None:
+            sigma, turned = energy(green, fit, None, orbitals)
+            sigma, pieces = lax.optimization_barrier((sigma, pieces))
+        else:
+            sigma = energy(green, fit, turned, orbitals)
         near, offsets = sigma[None], [0]
         far = None
         for step in reversed(bits(col_devices)):
@@ -212,13 +236,10 @@
                 near = jnp.concatenate([near, far], axis=0)
             far = swap(near, "col", step)
             offsets = offsets + [o ^ step for o in offsets]
-        keep, send = collide(place, near, far, pieces, offsets, row_devices)
-        for step in bits(row_devices):
-            if step > 1:
-                send = keep[1::2].astype(BF16)
-                keep = keep[0::2]
-            keep = keep + swap(send, "row", step).astype(F32)
-        green = green_start + keep[0]
+        keep, *sends = collide(place, near, far, pieces, offsets, row_devices)
+        green = green_start + keep
+        for step in sorted(range(1, row_devices), key=lambda t: -(t ^ 1)):
+            green = green + swap(sends[step - 1], "row", step).astype(F32)
     return green
 
 

time: 74.9 us -> 60.4 us (0.81)
  waiting for transfers between devices: 29.8 us -> 20 us
  local copies, waits for them, and re-layouts: 7.18 us -> 2.21 us
    ppermute x11 -> x13, waiting for transfers between devices: 29.8 us -> 20 us  [swap(): return lax.ppermute(x, axis, [(d, d ^ step) for d in range(size)])]
    dynamic_slice x1 -> x0, local copies, waits for them, and re-layouts: 2.16 us -> none  [local(): piece = lax.dynamic_index_in_dim(split, col ^ s, axis=3, keepdims=False)]
    reshape x1 -> x0, local copies, waits for them, and re-layouts: 1.52 us -> none  [local(): split = history.reshape(2, depth, ratio, col_devices, span)]
    unnamed x10 -> x6, local copies, waits for them, and re-layouts: 3.47 us -> 2.21 us
    ppermute x11 -> x13, starting transfers between devices: 14.6 us -> 14.7 us  [swap(): return lax.ppermute(x, axis, [(d, d ^ step) for d in range(size)])]
  transfers between devices with their start and end apart: 11 -> 13, of which waited for: 9 -> 11; matrix products, arithmetic and copies ran while one was open for 8% -> 0% of each run, Pallas kernels for 0% -> 16%
where the time goes in v2:
time: 60.4 us; the launch traced here: 60.3 us
  Pallas kernels  22.4 us (37%)
  waiting for transfers between devices  20 us (33%)
  starting transfers between devices  14.7 us (24%)
  local copies, waits for them, and re-layouts  2.21 us (4%)
  other arithmetic  0.83 us (1%)
    ppermute x13, waiting for transfers between devices, swap(): return lax.ppermute(x, axis, [(d, d ^ step) for d in range(size)])  20 us
    pallas_call x2, Pallas kernels, energy(): pl.pallas_call(functools.partial(energy_kernel, orbitals, turn), out_shap...  19.1 us
    ppermute x13, starting transfers between devices, swap(): return lax.ppermute(x, axis, [(d, d ^ step) for d in range(size)])  14.7 us
    pallas_call x2, Pallas kernels, collide(): pl.pallas_call(functools.partial(collide_kernel, offsets, row_devices), o...  2.54 us
    unnamed x6, local copies, waits for them, and re-layouts  2.21 us
  transfers between devices with their start and end apart: 13, of which 11 were waited for; matrix products, arithmetic and copies ran while one was open for 0% of the time, Pallas kernels for 16%

profile of v2, /device:TPU:0, one launch (start us, length us, event | category | flops | bytes accessed | tf_op | source)
XLA Modules:
  0.0 60.3 jit_solution(4472783623591765795)
XLA Ops:
  0.0 0.0 copy-start
  0.0 0.1 pad_add_fusion.place_ref
  0.1 0.0 copy-start.2
  0.1 1.3 %copy-done.2 = bf16[2,512,512]{2,1,0:T(8,128)(2,1)S(1)} copy-done((bf16[2,512,512]{2,1,0:T(8,128)(2,1)S(1)}, bf16[2,512,512]{2,1,0:T(8,128)(2,1)}, u32[]{:S(2)}) %copy-start.2) | copy-done | bytes 1048600
  1.4 0.8 %split_history.1 = (bf16[2,512,128]{2,1,0:T(8,128)(2,1)S(1)}, bf16[2,512,128]{2,1,0:T(8,128)(2,1)S(1)}, bf16[2,512,128]{2,1,0:T(8,128)(2,1)S(1)}, bf16[2,512,128]{2,1,0:T(8,128)(2,1)S(1)}) custom-call(s32[2]{0:T(128)S(1)} %pad_add_fusion.place_ref, bf16[2,512,512]{2,1,0:T(8,128)(2,1)S(1)} %copy-done.2), custom_call_target="tpu_custom_call" | custom-call | tf_op jit(solution)/shard_map/split_history/pallas_call | solution.py:50
  2.2 0.5 collective-permute-start
  2.7 2.6 %collective-permute-start.1 = (bf16[2,512,128]{2,1,0:T(8,128)(2,1)S(1)}, bf16[2,512,128]{2,1,0:T(8,128)(2,1)S(1)}, u32[]{:S(2)}, u32[]{:S(2)}) collective-permute-start(bf16[2,512,128]{2,1,0:T(8,128)(2,1)S(1)} %get-tuple-element.27), channel_id=1, source_target_pairs={{0,2},{1,3},{2,0},{3,1},{4,6},{5,7},{6,4},{7,5},{8,10},{9,11},{10,... | collective-permute-start | bytes 786440 | tf_op jit(solution)/shard_map/ppermute | solution.py:208
  5.2 0.1 collective-permute-start.2
  5.3 0.0 copy-done
  5.3 0.0 copy-start.1
  5.3 0.9 %copy-done.1 = f32[2,128,128]{2,1,0:T(8,128)S(1)} copy-done((f32[2,128,128]{2,1,0:T(8,128)S(1)}, f32[2,128,128]{2,1,0:T(8,128)}, u32[]{:S(2)}) %copy-start.1) | copy-done | bytes 131096
  6.2 9.8 %self_energy.2 = (bf16[2,128,128]{2,1,0:T(8,128)(2,1)S(1)}, bf16[128,4096]{1,0:T(8,128)(2,1)S(1)}) custom-call(f32[2,128,128]{2,1,0:T(8,128)S(1)} %copy-done.1, bf16[128,4096]{1,0:T(8,128)(2,1)S(1)} %copy-done), custom_call_target="tpu_custom_call" | custom-call | tf_op jit(solution)/shard_map/self_energy/pallas_call | solution.py:153
  16.0 0.0 collective-permute-done.refs_1_
  16.1 0.0 collective-permute-done.1.refs_2_
  16.1 1.4 %collective-permute-done.2.refs_3_ = bf16[2,512,128]{2,1,0:T(8,128)(2,1)S(1)} collective-permute-done((bf16[2,512,128]{2,1,0:T(8,128)(2,1)S(1)}, bf16[2,512,128]{2,1,0:T(8,128)(2,1)S(1)}, u32[]{:S(2)}, u32[]{:S(2)}) %collective-permute-start.2) | collective-permute-done | bytes 262176 | tf_op jit(solution)/shard_map/ppermute | solution.py:208
  17.5 1.6 %collective-permute-start.3 = (bf16[1,2,128,128]{3,2,1,0:T(8,128)(2,1)S(1)}, bf16[1,2,128,128]{3,2,1,0:T(8,128)(2,1)S(1)}, u32[]{:S(2)}, u32[]{:S(2)}) collective-permute-start(bf16[1,2,128,128]{3,2,1,0:T(8,128)(2,1)S(1)} %bitcast.6), channel_id=1, source_target_pairs={{0,2},{1,3},{2,0},{3,1},{4,6},{5,7},{6,4},{7,5},{8,10},{9,11},{10,... | collective-permute-start | bytes 196616 | tf_op jit(solution)/shard_map/ppermute | solution.py:208
  19.1 2.7 %collective-permute-done.3 = bf16[1,2,128,128]{3,2,1,0:T(8,128)(2,1)S(1)} collective-permute-done((bf16[1,2,128,128]{3,2,1,0:T(8,128)(2,1)S(1)}, bf16[1,2,128,128]{3,2,1,0:T(8,128)(2,1)S(1)}, u32[]{:S(2)}, u32[]{:S(2)}) %collective-permute-start.3) | collective-permute-done | bytes 65568 | tf_op jit(solution)/shard_map/ppermute | solution.py:208
  21.8 0.1 collective-permute-start.4
  21.9 1.3 %collective-permute-done.4.far_ref = bf16[2,2,128,128]{3,2,1,0:T(8,128)(2,1)S(1)} collective-permute-done((bf16[2,2,128,128]{3,2,1,0:T(8,128)(2,1)S(1)}, bf16[2,2,128,128]{3,2,1,0:T(8,128)(2,1)S(1)}, u32[]{:S(2)}, u32[]{:S(2)}) %collective-permute-start.4) | collective-permute-done | bytes 131104 | tf_op jit(solution)/shard_map/ppermute | solution.py:208
  23.2 1.3 %collide.2 = (f32[2,128,128]{2,1,0:T(8,128)S(1)}, bf16[2,128,128]{2,1,0:T(8,128)(2,1)S(1)}, bf16[2,128,128]{2,1,0:T(8,128)(2,1)S(1)}, bf16[2,128,128]{2,1,0:T(8,128)(2,1)S(1)}) custom-call(s32[2]{0:T(128)S(1)} %pad_add_fusion.place_ref, bf16[2,2,128,128]{3,2,1,0:T(8,128)(2,1)S(1)} %pad_maximum_fusion.near_ref, ...), custom_call_target="tpu_custom_call" | custom-call | tf_op jit(solution)/shard_map/collide/pallas_call | solution.py:194
  24.5 2.7 %collective-permute-start.5 = (bf16[2,128,128]{2,1,0:T(8,128)(2,1)S(1)}, bf16[2,128,128]{2,1,0:T(8,128)(2,1)S(1)}, u32[]{:S(2)}, u32[]{:S(2)}) collective-permute-start(bf16[2,128,128]{2,1,0:T(8,128)(2,1)S(1)} %get-tuple-element.35), channel_id=1, source_target_pairs={{0,8},{4,12},{8,0},{12,4},{1,9},{5,13},{9,1},{13,5},{2,10},{6,14},... | collective-permute-start | bytes 196616 | tf_op jit(solution)/shard_map/ppermute | solution.py:208
  27.2 1.3 %collective-permute-start.6 = (bf16[2,128,128]{2,1,0:T(8,128)(2,1)S(1)}, bf16[2,128,128]{2,1,0:T(8,128)(2,1)S(1)}, u32[]{:S(2)}, u32[]{:S(2)}) collective-permute-start(bf16[2,128,128]{2,1,0:T(8,128)(2,1)S(1)} %get-tuple-element.36), channel_id=1, source_target_pairs={{0,12},{4,8},{8,4},{12,0},{1,13},{5,9},{9,5},{13,1},{2,14},{6,10},... | collective-permute-start | bytes 196616 | tf_op jit(solution)/shard_map/ppermute | solution.py:208
  28.6 0.2 collective-permute-start.7
  28.8 2.6 %collective-permute-done.5 = bf16[2,128,128]{2,1,0:T(8,128)(2,1)S(1)} collective-permute-done((bf16[2,128,128]{2,1,0:T(8,128)(2,1)S(1)}, bf16[2,128,128]{2,1,0:T(8,128)(2,1)S(1)}, u32[]{:S(2)}, u32[]{:S(2)}) %collective-permute-start.5) | collective-permute-done | bytes 65568 | tf_op jit(solution)/shard_map/ppermute | solution.py:208
  31.4 2.3 %collective-permute-done.6 = bf16[2,128,128]{2,1,0:T(8,128)(2,1)S(1)} collective-permute-done((bf16[2,128,128]{2,1,0:T(8,128)(2,1)S(1)}, bf16[2,128,128]{2,1,0:T(8,128)(2,1)S(1)}, u32[]{:S(2)}, u32[]{:S(2)}) %collective-permute-start.6) | collective-permute-done | bytes 65568 | tf_op jit(solution)/shard_map/ppermute | solution.py:208
  33.6 0.3 collective-permute-done.7
  33.9 9.2 %self_energy.3 = bf16[2,128,128]{2,1,0:T(8,128)(2,1)S(1)} custom-call(f32[2,128,128]{2,1,0:T(8,128)S(1)} %convert_add_fusion.1.green_ref, bf16[128,4096]{1,0:T(8,128)(2,1)S(1)} %copy-done, bf16[128,4096]{1,0:T(8,128)(2,1)S(1)} %get-tuple-element.38.refs_0_), custom_call_target="tpu_custom_call" | custom-call | tf_op jit(solution)/shard_map/self_energy/pallas_call | solution.py:153
  43.2 1.6 %collective-permute-start.8 = (bf16[1,2,128,128]{3,2,1,0:T(8,128)(2,1)S(1)}, bf16[1,2,128,128]{3,2,1,0:T(8,128)(2,1)S(1)}, u32[]{:S(2)}, u32[]{:S(2)}) collective-permute-start(bf16[1,2,128,128]{3,2,1,0:T(8,128)(2,1)S(1)} %bitcast.4), channel_id=1, source_target_pairs={{0,2},{1,3},{2,0},{3,1},{4,6},{5,7},{6,4},{7,5},{8,10},{9,11},{10,... | collective-permute-start | bytes 196616 | tf_op jit(solution)/shard_map/ppermute | solution.py:208
  44.8 2.7 %collective-permute-done.8 = bf16[1,2,128,128]{3,2,1,0:T(8,128)(2,1)S(1)} collective-permute-done((bf16[1,2,128,128]{3,2,1,0:T(8,128)(2,1)S(1)}, bf16[1,2,128,128]{3,2,1,0:T(8,128)(2,1)S(1)}, u32[]{:S(2)}, u32[]{:S(2)}) %collective-permute-start.8) | collective-permute-done | bytes 65568 | tf_op jit(solution)/shard_map/ppermute | solution.py:208
  47.5 0.1 collective-permute-start.9
  47.6 1.3 %collective-permute-done.9.far_ref = bf16[2,2,128,128]{3,2,1,0:T(8,128)(2,1)S(1)} collective-permute-done((bf16[2,2,128,128]{3,2,1,0:T(8,128)(2,1)S(1)}, bf16[2,2,128,128]{3,2,1,0:T(8,128)(2,1)S(1)}, u32[]{:S(2)}, u32[]{:S(2)}) %collective-permute-start.9) | collective-permute-done | bytes 131104 | tf_op jit(solution)/shard_map/ppermute | solution.py:208
  48.9 1.3 %collide.3 = (f32[2,128,128]{2,1,0:T(8,128)S(1)}, bf16[2,128,128]{2,1,0:T(8,128)(2,1)S(1)}, bf16[2,128,128]{2,1,0:T(8,128)(2,1)S(1)}, bf16[2,128,128]{2,1,0:T(8,128)(2,1)S(1)}) custom-call(s32[2]{0:T(128)S(1)} %pad_add_fusion.place_ref, bf16[2,2,128,128]{3,2,1,0:T(8,128)(2,1)S(1)} %pad_maximum_fusion.1.near_ref, ...), custom_call_target="tpu_custom_call" | custom-call | tf_op jit(solution)/shard_map/collide/pallas_call | solution.py:194
  50.2 2.7 %collective-permute-start.10 = (bf16[2,128,128]{2,1,0:T(8,128)(2,1)S(1)}, bf16[2,128,128]{2,1,0:T(8,128)(2,1)S(1)}, u32[]{:S(2)}, u32[]{:S(2)}) collective-permute-start(bf16[2,128,128]{2,1,0:T(8,128)(2,1)S(1)} %get-tuple-element.40), channel_id=1, source_target_pairs={{0,8},{4,12},{8,0},{12,4},{1,9},{5,13},{9,1},{13,5},{2,10},{6,14},... | collective-permute-start | bytes 196616 | tf_op jit(solution)/shard_map/ppermute | solution.py:208
  52.9 0.7 %collective-permute-start.11 = (bf16[2,128,128]{2,1,0:T(8,128)(2,1)S(1)}, bf16[2,128,128]{2,1,0:T(8,128)(2,1)S(1)}, u32[]{:S(2)}, u32[]{:S(2)}) collective-permute-start(bf16[2,128,128]{2,1,0:T(8,128)(2,1)S(1)} %get-tuple-element.41), channel_id=1, source_target_pairs={{0,12},{4,8},{8,4},{12,0},{1,13},{5,9},{9,5},{13,1},{2,14},{6,10},... | collective-permute-start | bytes 196616 | tf_op jit(solution)/shard_map/ppermute | solution.py:208
  53.6 0.5 collective-permute-start.12
  54.1 4.0 %collective-permute-done.10 = bf16[2,128,128]{2,1,0:T(8,128)(2,1)S(1)} collective-permute-done((bf16[2,128,128]{2,1,0:T(8,128)(2,1)S(1)}, bf16[2,128,128]{2,1,0:T(8,128)(2,1)S(1)}, u32[]{:S(2)}, u32[]{:S(2)}) %collective-permute-start.10) | collective-permute-done | bytes 65568 | tf_op jit(solution)/shard_map/ppermute | solution.py:208
  58.1 1.2 %collective-permute-done.11 = bf16[2,128,128]{2,1,0:T(8,128)(2,1)S(1)} collective-permute-done((bf16[2,128,128]{2,1,0:T(8,128)(2,1)S(1)}, bf16[2,128,128]{2,1,0:T(8,128)(2,1)S(1)}, u32[]{:S(2)}, u32[]{:S(2)}) %collective-permute-start.11) | collective-permute-done | bytes 65568 | tf_op jit(solution)/shard_map/ppermute | solution.py:208
  59.3 0.2 collective-permute-done.12
  59.6 0.7 %convert_add_fusion = f32[2,128,128]{2,1,0:T(8,128)} fusion(bf16[2,128,128]{2,1,0:T(8,128)(2,1)S(1)} %collective-permute-done.12, bf16[2,128,128]{2,1,0:T(8,128)(2,1)S(1)} %collective-permute-done.11, bf16[2,128,128]{2,1,0:T(8,128)(2,1)S(1)} %collective-permute-done.10, f32[2,128,128]{2,1,0:T(8,128)S(1)} %copy-done.1, f32[2,128,128]{2,1,0:T(8,128)S(1)} %get-tuple-element.39), kind=kLoop, calls=%fused_computation.2 | loop fusion | flops 229376 | bytes 589824 | tf_op jit(solution)/shard_map/add | solution.py:242
  (3 shorter events, 0.1 us)
Async XLA Ops:
  0.0 5.3 %copy-start = (bf16[128,4096]{1,0:T(8,128)(2,1)S(1)}, bf16[128,4096]{1,0:T(8,128)(2,1)}, u32[]{:S(2)}) copy-start(bf16[128,4096]{1,0:T(8,128)(2,1)} %fit_ref.3) | copy-start | bytes 3145732
  0.1 1.3 %copy-start.2 = (bf16[2,512,512]{2,1,0:T(8,128)(2,1)S(1)}, bf16[2,512,512]{2,1,0:T(8,128)(2,1)}, u32[]{:S(2)}) copy-start(bf16[2,512,512]{2,1,0:T(8,128)(2,1)} %history_ref.1) | copy-start | bytes 3145732
  2.2 13.9 %collective-permute-start = (bf16[2,512,128]{2,1,0:T(8,128)(2,1)S(1)}, bf16[2,512,128]{2,1,0:T(8,128)(2,1)S(1)}, u32[]{:S(2)}, u32[]{:S(2)}) collective-permute-start(bf16[2,512,128]{2,1,0:T(8,128)(2,1)S(1)} %get-tuple-element.26), channel_id=1, source_target_pairs={{0,1},{1,0},{2,3},{3,2},{4,5},{5,4},{6,7},{7,6},{8,9},{9,8},{10,11... | collective-permute-start | bytes 786440 | tf_op jit(solution)/shard_map/ppermute | solution.py:208
  2.7 13.4 %collective-permute-start.1 = (bf16[2,512,128]{2,1,0:T(8,128)(2,1)S(1)}, bf16[2,512,128]{2,1,0:T(8,128)(2,1)S(1)}, u32[]{:S(2)}, u32[]{:S(2)}) collective-permute-start(bf16[2,512,128]{2,1,0:T(8,128)(2,1)S(1)} %get-tuple-element.27), channel_id=1, source_target_pairs={{0,2},{1,3},{2,0},{3,1},{4,6},{5,7},{6,4},{7,5},{8,10},{9,11},{10,... | collective-permute-start | bytes 786440 | tf_op jit(solution)/shard_map/ppermute | solution.py:208
  5.2 12.3 %collective-permute-start.2 = (bf16[2,512,128]{2,1,0:T(8,128)(2,1)S(1)}, bf16[2,512,128]{2,1,0:T(8,128)(2,1)S(1)}, u32[]{:S(2)}, u32[]{:S(2)}) collective-permute-start(bf16[2,512,128]{2,1,0:T(8,128)(2,1)S(1)} %get-tuple-element.28), channel_id=1, source_target_pairs={{0,3},{1,2},{2,1},{3,0},{4,7},{5,6},{6,5},{7,4},{8,11},{9,10},{10,... | collective-permute-start | bytes 786440 | tf_op jit(solution)/shard_map/ppermute | solution.py:208
  5.3 0.9 %copy-start.1 = (f32[2,128,128]{2,1,0:T(8,128)S(1)}, f32[2,128,128]{2,1,0:T(8,128)}, u32[]{:S(2)}) copy-start(f32[2,128,128]{2,1,0:T(8,128)} %green_ref.1) | copy-start | bytes 393220
  17.5 4.3 %collective-permute-start.3 = (bf16[1,2,128,128]{3,2,1,0:T(8,128)(2,1)S(1)}, bf16[1,2,128,128]{3,2,1,0:T(8,128)(2,1)S(1)}, u32[]{:S(2)}, u32[]{:S(2)}) collective-permute-start(bf16[1,2,128,128]{3,2,1,0:T(8,128)(2,1)S(1)} %bitcast.6), channel_id=1, source_target_pairs={{0,2},{1,3},{2,0},{3,1},{4,6},{5,7},{6,4},{7,5},{8,10},{9,11},{10,... | collective-permute-start | bytes 196616 | tf_op jit(solution)/shard_map/ppermute | solution.py:208
  21.8 1.4 %collective-permute-start.4 = (bf16[2,2,128,128]{3,2,1,0:T(8,128)(2,1)S(1)}, bf16[2,2,128,128]{3,2,1,0:T(8,128)(2,1)S(1)}, u32[]{:S(2)}, u32[]{:S(2)}) collective-permute-start(bf16[2,2,128,128]{3,2,1,0:T(8,128)(2,1)S(1)} %pad_maximum_fusion.near_ref), channel_id=1, source_target_pairs={{0,1},{1,0},{2,3},{3,2},{4,5},{5,4},{6,7},{7,6},{8,9},{9,8},{10,11... | collective-permute-start | bytes 393224 | tf_op jit(solution)/shard_map/ppermute | solution.py:208
  24.5 6.9 %collective-permute-start.5 = (bf16[2,128,128]{2,1,0:T(8,128)(2,1)S(1)}, bf16[2,128,128]{2,1,0:T(8,128)(2,1)S(1)}, u32[]{:S(2)}, u32[]{:S(2)}) collective-permute-start(bf16[2,128,128]{2,1,0:T(8,128)(2,1)S(1)} %get-tuple-element.35), channel_id=1, source_target_pairs={{0,8},{4,12},{8,0},{12,4},{1,9},{5,13},{9,1},{13,5},{2,10},{6,14},... | collective-permute-start | bytes 196616 | tf_op jit(solution)/shard_map/ppermute | solution.py:208
  27.2 6.4 %collective-permute-start.6 = (bf16[2,128,128]{2,1,0:T(8,128)(2,1)S(1)}, bf16[2,128,128]{2,1,0:T(8,128)(2,1)S(1)}, u32[]{:S(2)}, u32[]{:S(2)}) collective-permute-start(bf16[2,128,128]{2,1,0:T(8,128)(2,1)S(1)} %get-tuple-element.36), channel_id=1, source_target_pairs={{0,12},{4,8},{8,4},{12,0},{1,13},{5,9},{9,5},{13,1},{2,14},{6,10},... | collective-permute-start | bytes 196616 | tf_op jit(solution)/shard_map/ppermute | solution.py:208
  28.6 5.3 %collective-permute-start.7 = (bf16[2,128,128]{2,1,0:T(8,128)(2,1)S(1)}, bf16[2,128,128]{2,1,0:T(8,128)(2,1)S(1)}, u32[]{:S(2)}, u32[]{:S(2)}) collective-permute-start(bf16[2,128,128]{2,1,0:T(8,128)(2,1)S(1)} %get-tuple-element.37), channel_id=1, source_target_pairs={{0,4},{4,0},{8,12},{12,8},{1,5},{5,1},{9,13},{13,9},{2,6},{6,2},{1... | collective-permute-start | bytes 196616 | tf_op jit(solution)/shard_map/ppermute | solution.py:208
  43.2 4.3 %collective-permute-start.8 = (bf16[1,2,128,128]{3,2,1,0:T(8,128)(2,1)S(1)}, bf16[1,2,128,128]{3,2,1,0:T(8,128)(2,1)S(1)}, u32[]{:S(2)}, u32[]{:S(2)}) collective-permute-start(bf16[1,2,128,128]{3,2,1,0:T(8,128)(2,1)S(1)} %bitcast.4), channel_id=1, source_target_pairs={{0,2},{1,3},{2,0},{3,1},{4,6},{5,7},{6,4},{7,5},{8,10},{9,11},{10,... | collective-permute-start | bytes 196616 | tf_op jit(solution)/shard_map/ppermute | solution.py:208
  47.5 1.4 %collective-permute-start.9 = (bf16[2,2,128,128]{3,2,1,0:T(8,128)(2,1)S(1)}, bf16[2,2,128,128]{3,2,1,0:T(8,128)(2,1)S(1)}, u32[]{:S(2)}, u32[]{:S(2)}) collective-permute-start(bf16[2,2,128,128]{3,2,1,0:T(8,128)(2,1)S(1)} %pad_maximum_fusion.1.near_ref), channel_id=1, source_target_pairs={{0,1},{1,0},{2,3},{3,2},{4,5},{5,4},{6,7},{7,6},{8,9},{9,8},{10,11... | collective-permute-start | bytes 393224 | tf_op jit(solution)/shard_map/ppermute | solution.py:208
  50.2 7.9 %collective-permute-start.10 = (bf16[2,128,128]{2,1,0:T(8,128)(2,1)S(1)}, bf16[2,128,128]{2,1,0:T(8,128)(2,1)S(1)}, u32[]{:S(2)}, u32[]{:S(2)}) collective-permute-start(bf16[2,128,128]{2,1,0:T(8,128)(2,1)S(1)} %get-tuple-element.40), channel_id=1, source_target_pairs={{0,8},{4,12},{8,0},{12,4},{1,9},{5,13},{9,1},{13,5},{2,10},{6,14},... | collective-permute-start | bytes 196616 | tf_op jit(solution)/shard_map/ppermute | solution.py:208
  52.9 6.4 %collective-permute-start.11 = (bf16[2,128,128]{2,1,0:T(8,128)(2,1)S(1)}, bf16[2,128,128]{2,1,0:T(8,128)(2,1)S(1)}, u32[]{:S(2)}, u32[]{:S(2)}) collective-permute-start(bf16[2,128,128]{2,1,0:T(8,128)(2,1)S(1)} %get-tuple-element.41), channel_id=1, source_target_pairs={{0,12},{4,8},{8,4},{12,0},{1,13},{5,9},{9,5},{13,1},{2,14},{6,10},... | collective-permute-start | bytes 196616 | tf_op jit(solution)/shard_map/ppermute | solution.py:208
  53.6 5.9 %collective-permute-start.12 = (bf16[2,128,128]{2,1,0:T(8,128)(2,1)S(1)}, bf16[2,128,128]{2,1,0:T(8,128)(2,1)S(1)}, u32[]{:S(2)}, u32[]{:S(2)}) collective-permute-start(bf16[2,128,128]{2,1,0:T(8,128)(2,1)S(1)} %get-tuple-element.42), channel_id=1, source_target_pairs={{0,4},{4,0},{8,12},{12,8},{1,5},{5,1},{9,13},{13,9},{2,6},{6,2},{1... | collective-permute-start | bytes 196616 | tf_op jit(solution)/shard_map/ppermute | solution.py:208

commit v3 on v2

--- a/solution.py
+++ b/solution.py
@@ -23,18 +23,21 @@
     return lax.dot_general(a, b, (((1,), (1,)), ((), ())), preferred_element_type=F32)
 
 
-def split_kernel(span, place_ref, history_ref, *refs):
-    pieces, sems = refs[:-1], refs[-1]
-    ratio = pieces[0].shape[2] // span
-    copies = []
-    for s, piece in enumerate(pieces):
+def split_kernel(place_ref, green_ref, history_ref, green_out_ref, *refs):
+    groups, sems = refs[:-1], refs[-1]
+    columns = 1 << (len(groups) - 1)
+    span = green_ref.shape[2]
+    ratio = groups[0].shape[3] // span
+    copies = [pltpu.make_async_copy(green_ref, green_out_ref, sems.at[columns, 0])]
+    for d in range(columns):
+        piece = groups[d.bit_length()].at[d - (1 << d.bit_length() >> 1)]
         for rho in range(ratio):
-            at = pl.multiple_of((rho * len(pieces) + (place_ref[1] ^ s)) * span, span)
+            at = pl.multiple_of((rho * columns + (place_ref[1] ^ d)) * span, span)
             copies.append(
                 pltpu.make_async_copy(
                     history_ref.at[:, :, pl.ds(at, span)],
                     piece.at[:, :, pl.ds(rho * span, span)],
-                    sems.at[s, rho],
+                    sems.at[d, rho],
                 )
             )
     for copy in copies:
@@ -43,26 +46,33 @@
         copy.wait()
 
 
-def split_history(place, history, span, col_devices):
+def split_history(place, green, history, col_devices):
     _, depth, width = history.shape
+    span = green.shape[2]
     ratio = width // span // col_devices
-    piece = jax.ShapeDtypeStruct((2, depth, ratio * span), BF16)
+    anywhere = pl.BlockSpec(memory_space=pl.ANY)
+    sizes = [1, *bits(col_devices)]
     return pl.pallas_call(
-        functools.partial(split_kernel, span),
-        out_shape=[piece] * col_devices,
-        in_specs=[pl.BlockSpec(memory_space=pltpu.SMEM), pl.BlockSpec(memory_space=pltpu.VMEM)],
-        out_specs=[pl.BlockSpec(memory_space=pl.ANY)] * col_devices,
-        scratch_shapes=[pltpu.SemaphoreType.DMA((col_devices, ratio))],
+        split_kernel,
+        out_shape=[jax.ShapeDtypeStruct(green.shape, F32)]
+        + [jax.ShapeDtypeStruct((n, 2, depth, ratio * span), BF16) for n in sizes],
+        in_specs=[pl.BlockSpec(memory_space=pltpu.SMEM), anywhere, anywhere],
+        out_specs=[anywhere] * (1 + len(sizes)),
+        scratch_shapes=[pltpu.SemaphoreType.DMA((col_devices + 1, ratio))],
         compiler_params=pltpu.CompilerParams(vmem_limit_bytes=16 * MIB),
         name="split_history",
-    )(place, history)
+    )(
+        place,
+        pltpu.with_memory_space_constraint(green, pltpu.HBM),
+        pltpu.with_memory_space_constraint(history, pltpu.HBM),
+    )
 
 
 def energy_kernel(orbitals, turn, green_ref, fit_ref, *refs):
     if turn:
-        out_ref, turned_ref, spread, left, under, screened, wide = refs
+        out_ref, turned_ref, tall_ref, spread, left, under, wide = refs
     else:
-        turned_ref, out_ref, spread, left, under, screened = refs
+        turned_ref, tall_ref, out_ref, spread, left, under = refs
     aux, flat = fit_ref.shape
     times = green_ref.shape[2] // orbitals
     new = green_ref.shape[1] // orbitals
@@ -83,6 +93,7 @@
             for t in range(i // per, i // per + 2):
                 at = slice(t * LANES, (t + 1) * LANES)
                 wide[at, :] = fit_ref[:, at].astype(F32).T
+                tall_ref[at, :] = wide[at, :].astype(BF16)
         w = jnp.concatenate(
             [fit_ref[:, (i + per * g) * orbitals : (i + per * (g + 1)) * orbitals] for g in range(2)],
             axis=0,
@@ -101,6 +112,7 @@
                             ] = res[r : r + orbitals, g * aux : (g + 1) * aux]
     around = [jnp.concatenate(flipped[a], axis=1) for a in range(new)]
     rows = 2 * orbitals
+    group = 2
     for m in range(0, orbitals, 2):
         if turn and m % per == 0:
             x = [wide[pl.ds(m + h, orbitals, stride=orbitals), :] for h in range(per)]
@@ -116,22 +128,21 @@
                 under[(m + h) * orbitals : (m + h + 1) * orbitals, n * aux : (n + 1) * aux] = r[
                     :, h * aux : (h + 1) * aux
                 ].astype(BF16)
-    pi = dot(turned_ref[...], under[...]) * (1.0 / orbitals)
-    bubble = jnp.concatenate([pi[:, n * aux : (n + 1) * aux].T for n in range(pairs)], axis=0)
-    screened[...] = dot(bubble.astype(BF16), fit_ref[...]).astype(BF16)
+    bubble = dot(turned_ref[...], under[...]) * (1.0 / orbitals)
+    screened = under
+    screened[...] = dot(tall_ref[...], bubble.astype(BF16)).astype(BF16)
     scale = (aux * orbitals) ** -0.5
-    accs = [jnp.zeros((rows, orbitals), F32) for _ in range(pairs)]
-    for m in range(0, orbitals, 2):
-        for n in range(pairs):
-            a = jnp.concatenate(
-                [left[n, (m + h) * rows : (m + h + 1) * rows, :] for h in range(2)], axis=1
-            )
-            w = screened[n * aux : (n + 1) * aux, m * orbitals : (m + 2) * orbitals]
-            b = jnp.concatenate([w[:, :orbitals], w[:, orbitals:]], axis=0)
-            accs[n] = accs[n] + dot(a, b)
     for n in range(pairs):
+        acc = jnp.zeros((orbitals, rows), F32)
+        for l in range(0, orbitals, group):
+            a = [
+                screened[(l + h) * orbitals : (l + h + 1) * orbitals, n * aux : (n + 1) * aux]
+                for h in range(group)
+            ]
+            b = [left[n, (l + h) * rows : (l + h + 1) * rows, :] for h in range(group)]
+            acc = acc + dot_nt(jnp.concatenate(a, axis=1), jnp.concatenate(b, axis=1))
+        block = (acc * scale).T.astype(BF16)
         a, k = divmod(n, times)
-        block = (accs[n] * scale).astype(BF16)
         for c in range(2):
             out_ref[
                 c, a * orbitals : (a + 1) * orbitals, k * orbitals : (k + 1) * orbitals
@@ -144,19 +155,19 @@
     pairs = rows // orbitals * (span // orbitals)
     turn = turned is None
     out_shape = jax.ShapeDtypeStruct((2, rows, span), BF16)
+    forms = [jax.ShapeDtypeStruct((aux, flat), BF16), jax.ShapeDtypeStruct((flat, aux), BF16)]
     scratch = [
         pltpu.VMEM((pairs, orbitals * (2 * orbitals + 1), aux), F32),
         pltpu.VMEM((pairs, 2 * flat, aux), BF16),
         pltpu.VMEM((flat, pairs * aux), BF16),
-        pltpu.VMEM((pairs * aux, flat), BF16),
     ]
     return pl.pallas_call(
         functools.partial(energy_kernel, orbitals, turn),
-        out_shape=[out_shape, jax.ShapeDtypeStruct((aux, flat), BF16)] if turn else out_shape,
+        out_shape=[out_shape, *forms] if turn else out_shape,
         scratch_shapes=scratch + [pltpu.VMEM((flat, aux), F32)] * turn,
-        compiler_params=pltpu.CompilerParams(vmem_limit_bytes=44 * MIB),
+        compiler_params=pltpu.CompilerParams(vmem_limit_bytes=36 * MIB),
         name="self_energy",
-    )(*((green, fit) if turn else (green, fit, turned)))
+    )(green, fit, *(() if turn else turned))
 
 
 def collide_kernel(offsets, row_devices, place_ref, near_ref, far_ref, *refs):
@@ -169,13 +180,13 @@
     for b in range(2 * half):
         ref, at = (near_ref, b) if b < half else (far_ref, b - half)
         blocks.append(jnp.concatenate([ref[at, c] for c in range(2)], axis=0))
+    stacked = jnp.concatenate(blocks, axis=1)
     for s, piece in enumerate(pieces):
-        acc = None
-        for b, offset in enumerate(offsets):
+        depth = []
+        for offset in offsets:
             at = pl.ds(pl.multiple_of((col ^ offset) * span, span), span)
-            h = jnp.concatenate([piece[c, at, :] for c in range(2)], axis=1)
-            r = dot(blocks[b], h)
-            acc = r if acc is None else acc + r
+            depth.append(jnp.concatenate([piece[0, c, at, :] for c in range(2)], axis=1))
+        acc = dot(stacked, jnp.concatenate(depth, axis=0))
         width = ratio * span
         real = acc[:rows, :width] - acc[rows:, width:]
         imag = acc[:rows, width:] + acc[rows:, :width]
@@ -193,10 +204,12 @@
     shape = (2, rows, span)
     return pl.pallas_call(
         functools.partial(collide_kernel, offsets, row_devices),
+        grid=(1,),
         out_shape=[jax.ShapeDtypeStruct(shape, F32)]
         + [jax.ShapeDtypeStruct(shape, BF16)] * (row_devices - 1),
         in_specs=[pl.BlockSpec(memory_space=pltpu.SMEM)]
-        + [pl.BlockSpec(memory_space=pltpu.VMEM)] * (2 + len(pieces)),
+        + [pl.BlockSpec(memory_space=pltpu.VMEM)] * 2
+        + [pl.BlockSpec((1, *piece.shape[1:]), lambda _: (0, 0, 0, 0)) for piece in pieces],
         scratch_shapes=[pltpu.VMEM((row_devices, 2, rows, span), F32)],
         compiler_params=pltpu.CompilerParams(vmem_limit_bytes=32 * MIB),
         name="collide",
@@ -214,24 +227,34 @@
 
 def local(green_start, fit, history):
     orbitals = math.isqrt(fit.shape[1])
-    _, rows, span = green_start.shape
     row_devices = lax.axis_size("row")
     col_devices = lax.axis_size("col")
     place = jnp.stack([lax.axis_index("row"), lax.axis_index("col")]).astype(jnp.int32)
 
-    pieces = split_history(place, history, span, col_devices)
-    pieces = [swap(piece, "col", s) if s else piece for s, piece in enumerate(pieces)]
-
+    green_start, kept, *groups = split_history(place, green_start, history, col_devices)
+    held = {0: kept}
+
+    def pass_on(step):
+        for offset, array in list(held.items()):
+            if array.shape[0] > step:
+                held[offset ^ step] = swap(array[step : 2 * step], "col", step)
+        held[step] = swap(groups.pop(), "col", step)
+
+    steps = bits(col_devices)[::-1]
+    pass_on(steps[0])
     green, turned = green_start, None
     for _ in range(ITERS):
         if turned is None:
-            sigma, turned = energy(green, fit, None, orbitals)
-            sigma, pieces = lax.optimization_barrier((sigma, pieces))
+            sigma, *turned = energy(green, fit, None, orbitals)
+            sigma, held = lax.optimization_barrier((sigma, held))
+            for step in steps[1:]:
+                pass_on(step)
+            pieces = [held[offset] for offset in range(col_devices)]
         else:
             sigma = energy(green, fit, turned, orbitals)
         near, offsets = sigma[None], [0]
         far = None
-        for step in reversed(bits(col_devices)):
+        for step in steps:
             if far is not None:
                 near = jnp.concatenate([near, far], axis=0)
             far = swap(near, "col", step)

time: 60.4 us -> 59.3 us (0.982)
  local copies, waits for them, and re-layouts: 2.21 us -> 0.02 us
  starting transfers between devices: 14.7 us -> 15.6 us
    unnamed x6 -> x2, local copies, waits for them, and re-layouts: 2.21 us -> 0.01 us
    ppermute x13, starting transfers between devices: 14.7 us -> 15.6 us  [swap(): return lax.ppermute(x, axis, [(d, d ^ step) for d in range(size)])]
  transfers between devices with their start and end apart: 13 -> 13, of which waited for: 11 -> 11; matrix products, arithmetic and copies ran while one was open for 0% -> 0% of each run, Pallas kernels for 16% -> 17%
where the time goes in v3:
time: 59.3 us; the launch traced here: 59.1 us
  Pallas kernels  22.8 us (38%)
  waiting for transfers between devices  19.8 us (33%)
  starting transfers between devices  15.6 us (26%)
  other arithmetic  0.83 us (1%)
    ppermute x13, waiting for transfers between devices, swap(): return lax.ppermute(x, axis, [(d, d ^ step) for d in range(size)])  19.8 us
    pallas_call x2, Pallas kernels, energy(): pl.pallas_call(functools.partial(energy_kernel, orbitals, turn), out_shap...  18.9 us
    ppermute x13, starting transfers between devices, swap(): return lax.ppermute(x, axis, [(d, d ^ step) for d in range(size)])  15.6 us
    pallas_call x2, Pallas kernels, collide(): pl.pallas_call(functools.partial(collide_kernel, offsets, row_devices), g...  2.04 us
    pallas_call x1, Pallas kernels, split_history(): pl.pallas_call(split_kernel, out_shape=[jax.ShapeDtypeStruct(green.shape,...  1.86 us
  transfers between devices with their start and end apart: 13, of which 11 were waited for; matrix products, arithmetic and copies ran while one was open for 0% of the time, Pallas kernels for 17%

profile of v3, /device:TPU:0, one launch (start us, length us, event | category | flops | bytes accessed | tf_op | source)
XLA Modules:
  0.0 59.1 jit_solution(6399703281388226398)
XLA Ops:
  0.0 0.0 copy-start
  0.0 0.1 pad_add_fusion.place_ref
  0.1 1.9 %split_history.1 = (f32[2,128,128]{2,1,0:T(8,128)S(1)}, bf16[1,2,512,128]{3,2,1,0:T(8,128)(2,1)S(1)}, bf16[1,2,512,128]{3,2,1,0:T(8,128)(2,1)S(1)}, bf16[2,2,512,128]{3,2,1,0:T(8,128)(2,1)S(1)}) custom-call(s32[2]{0:T(128)S(1)} %pad_add_fusion.place_ref, f32[2,128,128]{2,1,0:T(8,128)} %green_ref.1, bf16[2,512,512]{2,1,0:T(8,128)(2,1)} %history_ref.1), custom_call_target="tpu_custom_call" | custom-call | tf_op jit(solution)/shard_map/split_history/pallas_call | solution.py:55
  1.9 3.0 %collective-permute-start = (bf16[2,2,512,128]{3,2,1,0:T(8,128)(2,1)S(1)}, bf16[2,2,512,128]{3,2,1,0:T(8,128)(2,1)S(1)}, u32[]{:S(2)}, u32[]{:S(2)}) collective-permute-start(bf16[2,2,512,128]{3,2,1,0:T(8,128)(2,1)S(1)} %get-tuple-element.26), channel_id=1, source_target_pairs={{0,2},{1,3},{2,0},{3,1},{4,6},{5,7},{6,4},{7,5},{8,10},{9,11},{10,... | collective-permute-start | bytes 1572872 | tf_op jit(solution)/shard_map/ppermute | solution.py:221
  5.0 0.0 copy-done
  5.0 9.8 %self_energy.2 = (bf16[2,128,128]{2,1,0:T(8,128)(2,1)S(1)}, bf16[128,4096]{1,0:T(8,128)(2,1)S(1)}, bf16[4096,128]{1,0:T(8,128)(2,1)S(1)}) custom-call(f32[2,128,128]{2,1,0:T(8,128)S(1)} %get-tuple-element.23.green_ref, bf16[128,4096]{1,0:T(8,128)(2,1)S(1)} %copy-done), custom_call_target="tpu_custom_call" | custom-call | tf_op jit(solution)/shard_map/self_energy/pallas_call | solution.py:164
  14.7 2.1 %collective-permute-done.refs_2_ = bf16[2,2,512,128]{3,2,1,0:T(8,128)(2,1)S(1)} collective-permute-done((bf16[2,2,512,128]{3,2,1,0:T(8,128)(2,1)S(1)}, bf16[2,2,512,128]{3,2,1,0:T(8,128)(2,1)S(1)}, u32[]{:S(2)}, u32[]{:S(2)}) %collective-permute-start) | collective-permute-done | bytes 524320 | tf_op jit(solution)/shard_map/ppermute | solution.py:221
  16.9 1.7 %collective-permute-start.1 = (bf16[1,2,128,128]{3,2,1,0:T(8,128)(2,1)S(1)}, bf16[1,2,128,128]{3,2,1,0:T(8,128)(2,1)S(1)}, u32[]{:S(2)}, u32[]{:S(2)}) collective-permute-start(bf16[1,2,128,128]{3,2,1,0:T(8,128)(2,1)S(1)} %bitcast.6), channel_id=1, source_target_pairs={{0,2},{1,3},{2,0},{3,1},{4,6},{5,7},{6,4},{7,5},{8,10},{9,11},{10,... | collective-permute-start | bytes 196616 | tf_op jit(solution)/shard_map/ppermute | solution.py:221
  18.6 0.0 collective-permute-start.3
  18.6 0.6 collective-permute-start.4
  19.2 1.9 %collective-permute-done.1 = bf16[1,2,128,128]{3,2,1,0:T(8,128)(2,1)S(1)} collective-permute-done((bf16[1,2,128,128]{3,2,1,0:T(8,128)(2,1)S(1)}, bf16[1,2,128,128]{3,2,1,0:T(8,128)(2,1)S(1)}, u32[]{:S(2)}, u32[]{:S(2)}) %collective-permute-start.1) | collective-permute-done | bytes 65568 | tf_op jit(solution)/shard_map/ppermute | solution.py:221
  21.2 0.1 collective-permute-start.2
  21.2 0.0 collective-permute-done.3.refs_1_
  21.3 1.3 %collective-permute-done.2.far_ref = bf16[2,2,128,128]{3,2,1,0:T(8,128)(2,1)S(1)} collective-permute-done((bf16[2,2,128,128]{3,2,1,0:T(8,128)(2,1)S(1)}, bf16[2,2,128,128]{3,2,1,0:T(8,128)(2,1)S(1)}, u32[]{:S(2)}, u32[]{:S(2)}) %collective-permute-start.2) | collective-permute-done | bytes 131104 | tf_op jit(solution)/shard_map/ppermute | solution.py:221
  22.6 0.0 collective-permute-done.4.refs_3_
  22.6 1.0 %collide.2 = (f32[2,128,128]{2,1,0:T(8,128)S(1)}, bf16[2,128,128]{2,1,0:T(8,128)(2,1)S(1)}, bf16[2,128,128]{2,1,0:T(8,128)(2,1)S(1)}, bf16[2,128,128]{2,1,0:T(8,128)(2,1)S(1)}) custom-call(s32[2]{0:T(128)S(1)} %pad_add_fusion.place_ref, bf16[2,2,128,128]{3,2,1,0:T(8,128)(2,1)S(1)} %pad_maximum_fusion.near_ref, ...), custom_call_target="tpu_custom_call" | custom-call | tf_op jit(solution)/shard_map/collide/pallas_call | solution.py:205
  23.6 2.9 %collective-permute-start.5 = (bf16[2,128,128]{2,1,0:T(8,128)(2,1)S(1)}, bf16[2,128,128]{2,1,0:T(8,128)(2,1)S(1)}, u32[]{:S(2)}, u32[]{:S(2)}) collective-permute-start(bf16[2,128,128]{2,1,0:T(8,128)(2,1)S(1)} %get-tuple-element.32), channel_id=1, source_target_pairs={{0,8},{4,12},{8,0},{12,4},{1,9},{5,13},{9,1},{13,5},{2,10},{6,14},... | collective-permute-start | bytes 196616 | tf_op jit(solution)/shard_map/ppermute | solution.py:221
  26.5 1.3 %collective-permute-start.6 = (bf16[2,128,128]{2,1,0:T(8,128)(2,1)S(1)}, bf16[2,128,128]{2,1,0:T(8,128)(2,1)S(1)}, u32[]{:S(2)}, u32[]{:S(2)}) collective-permute-start(bf16[2,128,128]{2,1,0:T(8,128)(2,1)S(1)} %get-tuple-element.33), channel_id=1, source_target_pairs={{0,12},{4,8},{8,4},{12,0},{1,13},{5,9},{9,5},{13,1},{2,14},{6,10},... | collective-permute-start | bytes 196616 | tf_op jit(solution)/shard_map/ppermute | solution.py:221
  27.9 0.2 collective-permute-start.7
  28.1 2.4 %collective-permute-done.5 = bf16[2,128,128]{2,1,0:T(8,128)(2,1)S(1)} collective-permute-done((bf16[2,128,128]{2,1,0:T(8,128)(2,1)S(1)}, bf16[2,128,128]{2,1,0:T(8,128)(2,1)S(1)}, u32[]{:S(2)}, u32[]{:S(2)}) %collective-permute-start.5) | collective-permute-done | bytes 65568 | tf_op jit(solution)/shard_map/ppermute | solution.py:221
  30.5 2.4 %collective-permute-done.6 = bf16[2,128,128]{2,1,0:T(8,128)(2,1)S(1)} collective-permute-done((bf16[2,128,128]{2,1,0:T(8,128)(2,1)S(1)}, bf16[2,128,128]{2,1,0:T(8,128)(2,1)S(1)}, u32[]{:S(2)}, u32[]{:S(2)}) %collective-permute-start.6) | collective-permute-done | bytes 65568 | tf_op jit(solution)/shard_map/ppermute | solution.py:221
  32.9 0.2 collective-permute-done.7
  33.1 9.1 %self_energy.3 = bf16[2,128,128]{2,1,0:T(8,128)(2,1)S(1)} custom-call(f32[2,128,128]{2,1,0:T(8,128)S(1)} %convert_add_fusion.1.green_ref, bf16[128,4096]{1,0:T(8,128)(2,1)S(1)} %copy-done, bf16[128,4096]{1,0:T(8,128)(2,1)S(1)} %get-tuple-element.35.refs_0_, bf16[4096,128]{1,0:T(8,128)(2,1)S(1)} %get-tuple-element.36.refs_1_), custom_call_target="tpu_custom_call" | custom-call | tf_op jit(solution)/shard_map/self_energy/pallas_call | solution.py:164
  42.2 1.7 %collective-permute-start.8 = (bf16[1,2,128,128]{3,2,1,0:T(8,128)(2,1)S(1)}, bf16[1,2,128,128]{3,2,1,0:T(8,128)(2,1)S(1)}, u32[]{:S(2)}, u32[]{:S(2)}) collective-permute-start(bf16[1,2,128,128]{3,2,1,0:T(8,128)(2,1)S(1)} %bitcast.4), channel_id=1, source_target_pairs={{0,2},{1,3},{2,0},{3,1},{4,6},{5,7},{6,4},{7,5},{8,10},{9,11},{10,... | collective-permute-start | bytes 196616 | tf_op jit(solution)/shard_map/ppermute | solution.py:221
  43.9 2.6 %collective-permute-done.8 = bf16[1,2,128,128]{3,2,1,0:T(8,128)(2,1)S(1)} collective-permute-done((bf16[1,2,128,128]{3,2,1,0:T(8,128)(2,1)S(1)}, bf16[1,2,128,128]{3,2,1,0:T(8,128)(2,1)S(1)}, u32[]{:S(2)}, u32[]{:S(2)}) %collective-permute-start.8) | collective-permute-done | bytes 65568 | tf_op jit(solution)/shard_map/ppermute | solution.py:221
  46.6 0.1 collective-permute-start.9
  46.6 1.3 %collective-permute-done.9.far_ref = bf16[2,2,128,128]{3,2,1,0:T(8,128)(2,1)S(1)} collective-permute-done((bf16[2,2,128,128]{3,2,1,0:T(8,128)(2,1)S(1)}, bf16[2,2,128,128]{3,2,1,0:T(8,128)(2,1)S(1)}, u32[]{:S(2)}, u32[]{:S(2)}) %collective-permute-start.9) | collective-permute-done | bytes 131104 | tf_op jit(solution)/shard_map/ppermute | solution.py:221
  48.0 1.0 %collide.3 = (f32[2,128,128]{2,1,0:T(8,128)S(1)}, bf16[2,128,128]{2,1,0:T(8,128)(2,1)S(1)}, bf16[2,128,128]{2,1,0:T(8,128)(2,1)S(1)}, bf16[2,128,128]{2,1,0:T(8,128)(2,1)S(1)}) custom-call(s32[2]{0:T(128)S(1)} %pad_add_fusion.place_ref, bf16[2,2,128,128]{3,2,1,0:T(8,128)(2,1)S(1)} %pad_maximum_fusion.1.near_ref, ...), custom_call_target="tpu_custom_call" | custom-call | tf_op jit(solution)/shard_map/collide/pallas_call | solution.py:205
  49.0 2.8 %collective-permute-start.10 = (bf16[2,128,128]{2,1,0:T(8,128)(2,1)S(1)}, bf16[2,128,128]{2,1,0:T(8,128)(2,1)S(1)}, u32[]{:S(2)}, u32[]{:S(2)}) collective-permute-start(bf16[2,128,128]{2,1,0:T(8,128)(2,1)S(1)} %get-tuple-element.38), channel_id=1, source_target_pairs={{0,8},{4,12},{8,0},{12,4},{1,9},{5,13},{9,1},{13,5},{2,10},{6,14},... | collective-permute-start | bytes 196616 | tf_op jit(solution)/shard_map/ppermute | solution.py:221
  51.8 0.7 %collective-permute-start.11 = (bf16[2,128,128]{2,1,0:T(8,128)(2,1)S(1)}, bf16[2,128,128]{2,1,0:T(8,128)(2,1)S(1)}, u32[]{:S(2)}, u32[]{:S(2)}) collective-permute-start(bf16[2,128,128]{2,1,0:T(8,128)(2,1)S(1)} %get-tuple-element.39), channel_id=1, source_target_pairs={{0,12},{4,8},{8,4},{12,0},{1,13},{5,9},{9,5},{13,1},{2,14},{6,10},... | collective-permute-start | bytes 196616 | tf_op jit(solution)/shard_map/ppermute | solution.py:221
  52.5 0.5 collective-permute-start.12
  53.0 4.0 %collective-permute-done.10 = bf16[2,128,128]{2,1,0:T(8,128)(2,1)S(1)} collective-permute-done((bf16[2,128,128]{2,1,0:T(8,128)(2,1)S(1)}, bf16[2,128,128]{2,1,0:T(8,128)(2,1)S(1)}, u32[]{:S(2)}, u32[]{:S(2)}) %collective-permute-start.10) | collective-permute-done | bytes 65568 | tf_op jit(solution)/shard_map/ppermute | solution.py:221
  57.0 1.2 %collective-permute-done.11 = bf16[2,128,128]{2,1,0:T(8,128)(2,1)S(1)} collective-permute-done((bf16[2,128,128]{2,1,0:T(8,128)(2,1)S(1)}, bf16[2,128,128]{2,1,0:T(8,128)(2,1)S(1)}, u32[]{:S(2)}, u32[]{:S(2)}) %collective-permute-start.11) | collective-permute-done | bytes 65568 | tf_op jit(solution)/shard_map/ppermute | solution.py:221
  58.2 0.2 collective-permute-done.12
  58.4 0.7 %convert_add_fusion = f32[2,128,128]{2,1,0:T(8,128)} fusion(bf16[2,128,128]{2,1,0:T(8,128)(2,1)S(1)} %collective-permute-done.12, bf16[2,128,128]{2,1,0:T(8,128)(2,1)S(1)} %collective-permute-done.11, bf16[2,128,128]{2,1,0:T(8,128)(2,1)S(1)} %collective-permute-done.10, f32[2,128,128]{2,1,0:T(8,128)S(1)} %get-tuple-element.23.green_ref, ...), kind=kLoop, calls=%fused_computation.2 | loop fusion | flops 229376 | bytes 589824 | tf_op jit(solution)/shard_map/add | solution.py:265
  (4 shorter events, 0.1 us)
Async XLA Ops:
  0.0 5.0 %copy-start = (bf16[128,4096]{1,0:T(8,128)(2,1)S(1)}, bf16[128,4096]{1,0:T(8,128)(2,1)}, u32[]{:S(2)}) copy-start(bf16[128,4096]{1,0:T(8,128)(2,1)} %fit_ref.3) | copy-start | bytes 3145732
  1.9 14.9 %collective-permute-start = (bf16[2,2,512,128]{3,2,1,0:T(8,128)(2,1)S(1)}, bf16[2,2,512,128]{3,2,1,0:T(8,128)(2,1)S(1)}, u32[]{:S(2)}, u32[]{:S(2)}) collective-permute-start(bf16[2,2,512,128]{3,2,1,0:T(8,128)(2,1)S(1)} %get-tuple-element.26), channel_id=1, source_target_pairs={{0,2},{1,3},{2,0},{3,1},{4,6},{5,7},{6,4},{7,5},{8,10},{9,11},{10,... | collective-permute-start | bytes 1572872 | tf_op jit(solution)/shard_map/ppermute | solution.py:221
  16.9 4.3 %collective-permute-start.1 = (bf16[1,2,128,128]{3,2,1,0:T(8,128)(2,1)S(1)}, bf16[1,2,128,128]{3,2,1,0:T(8,128)(2,1)S(1)}, u32[]{:S(2)}, u32[]{:S(2)}) collective-permute-start(bf16[1,2,128,128]{3,2,1,0:T(8,128)(2,1)S(1)} %bitcast.6), channel_id=1, source_target_pairs={{0,2},{1,3},{2,0},{3,1},{4,6},{5,7},{6,4},{7,5},{8,10},{9,11},{10,... | collective-permute-start | bytes 196616 | tf_op jit(solution)/shard_map/ppermute | solution.py:221
  18.6 2.6 %collective-permute-start.3 = (bf16[1,2,512,128]{3,2,1,0:T(8,128)(2,1)S(1)}, bf16[1,2,512,128]{3,2,1,0:T(8,128)(2,1)S(1)}, u32[]{:S(2)}, u32[]{:S(2)}) collective-permute-start(bf16[1,2,512,128]{3,2,1,0:T(8,128)(2,1)S(1)} %get-tuple-element.29), channel_id=1, source_target_pairs={{0,1},{1,0},{2,3},{3,2},{4,5},{5,4},{6,7},{7,6},{8,9},{9,8},{10,11... | collective-permute-start | bytes 786440 | tf_op jit(solution)/shard_map/ppermute | solution.py:221
  18.6 3.9 %collective-permute-start.4 = (bf16[1,2,512,128]{3,2,1,0:T(8,128)(2,1)S(1)}, bf16[1,2,512,128]{3,2,1,0:T(8,128)(2,1)S(1)}, u32[]{:S(2)}, u32[]{:S(2)}) collective-permute-start(bf16[1,2,512,128]{3,2,1,0:T(8,128)(2,1)S(1)} %slice.3), channel_id=1, source_target_pairs={{0,1},{1,0},{2,3},{3,2},{4,5},{5,4},{6,7},{7,6},{8,9},{9,8},{10,11... | collective-permute-start | bytes 786440 | tf_op jit(solution)/shard_map/ppermute | solution.py:221
  21.2 1.4 %collective-permute-start.2 = (bf16[2,2,128,128]{3,2,1,0:T(8,128)(2,1)S(1)}, bf16[2,2,128,128]{3,2,1,0:T(8,128)(2,1)S(1)}, u32[]{:S(2)}, u32[]{:S(2)}) collective-permute-start(bf16[2,2,128,128]{3,2,1,0:T(8,128)(2,1)S(1)} %pad_maximum_fusion.near_ref), channel_id=1, source_target_pairs={{0,1},{1,0},{2,3},{3,2},{4,5},{5,4},{6,7},{7,6},{8,9},{9,8},{10,11... | collective-permute-start | bytes 393224 | tf_op jit(solution)/shard_map/ppermute | solution.py:221
  23.6 6.9 %collective-permute-start.5 = (bf16[2,128,128]{2,1,0:T(8,128)(2,1)S(1)}, bf16[2,128,128]{2,1,0:T(8,128)(2,1)S(1)}, u32[]{:S(2)}, u32[]{:S(2)}) collective-permute-start(bf16[2,128,128]{2,1,0:T(8,128)(2,1)S(1)} %get-tuple-element.32), channel_id=1, source_target_pairs={{0,8},{4,12},{8,0},{12,4},{1,9},{5,13},{9,1},{13,5},{2,10},{6,14},... | collective-permute-start | bytes 196616 | tf_op jit(solution)/shard_map/ppermute | solution.py:221
  26.5 6.4 %collective-permute-start.6 = (bf16[2,128,128]{2,1,0:T(8,128)(2,1)S(1)}, bf16[2,128,128]{2,1,0:T(8,128)(2,1)S(1)}, u32[]{:S(2)}, u32[]{:S(2)}) collective-permute-start(bf16[2,128,128]{2,1,0:T(8,128)(2,1)S(1)} %get-tuple-element.33), channel_id=1, source_target_pairs={{0,12},{4,8},{8,4},{12,0},{1,13},{5,9},{9,5},{13,1},{2,14},{6,10},... | collective-permute-start | bytes 196616 | tf_op jit(solution)/shard_map/ppermute | solution.py:221
  27.9 5.2 %collective-permute-start.7 = (bf16[2,128,128]{2,1,0:T(8,128)(2,1)S(1)}, bf16[2,128,128]{2,1,0:T(8,128)(2,1)S(1)}, u32[]{:S(2)}, u32[]{:S(2)}) collective-permute-start(bf16[2,128,128]{2,1,0:T(8,128)(2,1)S(1)} %get-tuple-element.34), channel_id=1, source_target_pairs={{0,4},{4,0},{8,12},{12,8},{1,5},{5,1},{9,13},{13,9},{2,6},{6,2},{1... | collective-permute-start | bytes 196616 | tf_op jit(solution)/shard_map/ppermute | solution.py:221
  42.2 4.3 %collective-permute-start.8 = (bf16[1,2,128,128]{3,2,1,0:T(8,128)(2,1)S(1)}, bf16[1,2,128,128]{3,2,1,0:T(8,128)(2,1)S(1)}, u32[]{:S(2)}, u32[]{:S(2)}) collective-permute-start(bf16[1,2,128,128]{3,2,1,0:T(8,128)(2,1)S(1)} %bitcast.4), channel_id=1, source_target_pairs={{0,2},{1,3},{2,0},{3,1},{4,6},{5,7},{6,4},{7,5},{8,10},{9,11},{10,... | collective-permute-start | bytes 196616 | tf_op jit(solution)/shard_map/ppermute | solution.py:221
  46.6 1.4 %collective-permute-start.9 = (bf16[2,2,128,128]{3,2,1,0:T(8,128)(2,1)S(1)}, bf16[2,2,128,128]{3,2,1,0:T(8,128)(2,1)S(1)}, u32[]{:S(2)}, u32[]{:S(2)}) collective-permute-start(bf16[2,2,128,128]{3,2,1,0:T(8,128)(2,1)S(1)} %pad_maximum_fusion.1.near_ref), channel_id=1, source_target_pairs={{0,1},{1,0},{2,3},{3,2},{4,5},{5,4},{6,7},{7,6},{8,9},{9,8},{10,11... | collective-permute-start | bytes 393224 | tf_op jit(solution)/shard_map/ppermute | solution.py:221
  49.0 8.0 %collective-permute-start.10 = (bf16[2,128,128]{2,1,0:T(8,128)(2,1)S(1)}, bf16[2,128,128]{2,1,0:T(8,128)(2,1)S(1)}, u32[]{:S(2)}, u32[]{:S(2)}) collective-permute-start(bf16[2,128,128]{2,1,0:T(8,128)(2,1)S(1)} %get-tuple-element.38), channel_id=1, source_target_pairs={{0,8},{4,12},{8,0},{12,4},{1,9},{5,13},{9,1},{13,5},{2,10},{6,14},... | collective-permute-start | bytes 196616 | tf_op jit(solution)/shard_map/ppermute | solution.py:221
  51.8 6.4 %collective-permute-start.11 = (bf16[2,128,128]{2,1,0:T(8,128)(2,1)S(1)}, bf16[2,128,128]{2,1,0:T(8,128)(2,1)S(1)}, u32[]{:S(2)}, u32[]{:S(2)}) collective-permute-start(bf16[2,128,128]{2,1,0:T(8,128)(2,1)S(1)} %get-tuple-element.39), channel_id=1, source_target_pairs={{0,12},{4,8},{8,4},{12,0},{1,13},{5,9},{9,5},{13,1},{2,14},{6,10},... | collective-permute-start | bytes 196616 | tf_op jit(solution)/shard_map/ppermute | solution.py:221
  52.5 6.0 %collective-permute-start.12 = (bf16[2,128,128]{2,1,0:T(8,128)(2,1)S(1)}, bf16[2,128,128]{2,1,0:T(8,128)(2,1)S(1)}, u32[]{:S(2)}, u32[]{:S(2)}) collective-permute-start(bf16[2,128,128]{2,1,0:T(8,128)(2,1)S(1)} %get-tuple-element.40), channel_id=1, source_target_pairs={{0,4},{4,0},{8,12},{12,8},{1,5},{5,1},{9,13},{13,9},{2,6},{6,2},{1... | collective-permute-start | bytes 196616 | tf_op jit(solution)/shard_map/ppermute | solution.py:221

commit v4 on v3

--- a/solution.py
+++ b/solution.py
@@ -246,10 +246,6 @@
     for _ in range(ITERS):
         if turned is None:
             sigma, *turned = energy(green, fit, None, orbitals)
-            sigma, held = lax.optimization_barrier((sigma, held))
-            for step in steps[1:]:
-                pass_on(step)
-            pieces = [held[offset] for offset in range(col_devices)]
         else:
             sigma = energy(green, fit, turned, orbitals)
         near, offsets = sigma[None], [0]
@@ -258,6 +254,11 @@
             if far is not None:
                 near = jnp.concatenate([near, far], axis=0)
             far = swap(near, "col", step)
+            if held:
+                far, held = lax.optimization_barrier((far, held))
+                for later in steps[1:]:
+                    pass_on(later)
+                pieces, held = [held[offset] for offset in range(col_devices)], None
             offsets = offsets + [o ^ step for o in offsets]
         keep, *sends = collide(place, near, far, pieces, offsets, row_devices)
         green = green_start + keep

time: 59.3 us -> 57.4 us (0.968)
  starting transfers between devices: 15.6 us -> 13 us
  waiting for transfers between devices: 19.8 us -> 20.6 us
    ppermute x13, starting transfers between devices: 15.6 us -> 13 us  [swap(): return lax.ppermute(x, axis, [(d, d ^ step) for d in range(size)])]
    ppermute x13, waiting for transfers between devices: 19.8 us -> 20.6 us  [swap(): return lax.ppermute(x, axis, [(d, d ^ step) for d in range(size)])]
  transfers between devices with their start and end apart: 13 -> 13, of which waited for: 11 -> 10; matrix products, arithmetic and copies ran while one was open for 0% -> 0% of each run, Pallas kernels for 17% -> 17%
where the time goes in v4:
time: 57.4 us; the launch traced here: 57.3 us
  Pallas kernels  22.8 us (40%)
  waiting for transfers between devices  20.6 us (36%)
  starting transfers between devices  13 us (23%)
  other arithmetic  0.83 us (1%)
    ppermute x13, waiting for transfers between devices, swap(): return lax.ppermute(x, axis, [(d, d ^ step) for d in range(size)])  20.6 us
    pallas_call x2, Pallas kernels, energy(): pl.pallas_call(functools.partial(energy_kernel, orbitals, turn), out_shap...  18.9 us
    ppermute x13, starting transfers between devices, swap(): return lax.ppermute(x, axis, [(d, d ^ step) for d in range(size)])  13 us
    pallas_call x2, Pallas kernels, collide(): pl.pallas_call(functools.partial(collide_kernel, offsets, row_devices), g...  2.04 us
    pallas_call x1, Pallas kernels, split_history(): pl.pallas_call(split_kernel, out_shape=[jax.ShapeDtypeStruct(green.shape,...  1.86 us
  transfers between devices with their start and end apart: 13, of which 10 were waited for; matrix products, arithmetic and copies ran while one was open for 0% of the time, Pallas kernels for 17%

profile of v4, /device:TPU:0, one launch (start us, length us, event | category | flops | bytes accessed | tf_op | source)
XLA Modules:
  0.0 57.3 jit_solution(12990319510534469109)
XLA Ops:
  0.0 0.0 copy-start
  0.0 0.1 pad_add_fusion.place_ref
  0.1 1.9 %split_history.1 = (f32[2,128,128]{2,1,0:T(8,128)S(1)}, bf16[1,2,512,128]{3,2,1,0:T(8,128)(2,1)S(1)}, bf16[1,2,512,128]{3,2,1,0:T(8,128)(2,1)S(1)}, bf16[2,2,512,128]{3,2,1,0:T(8,128)(2,1)S(1)}) custom-call(s32[2]{0:T(128)S(1)} %pad_add_fusion.place_ref, f32[2,128,128]{2,1,0:T(8,128)} %green_ref.1, bf16[2,512,512]{2,1,0:T(8,128)(2,1)} %history_ref.1), custom_call_target="tpu_custom_call" | custom-call | tf_op jit(solution)/shard_map/split_history/pallas_call | solution.py:55
  1.9 3.0 %collective-permute-start.1 = (bf16[2,2,512,128]{3,2,1,0:T(8,128)(2,1)S(1)}, bf16[2,2,512,128]{3,2,1,0:T(8,128)(2,1)S(1)}, u32[]{:S(2)}, u32[]{:S(2)}) collective-permute-start(bf16[2,2,512,128]{3,2,1,0:T(8,128)(2,1)S(1)} %get-tuple-element.26), channel_id=1, source_target_pairs={{0,2},{1,3},{2,0},{3,1},{4,6},{5,7},{6,4},{7,5},{8,10},{9,11},{10,... | collective-permute-start | bytes 1572872 | tf_op jit(solution)/shard_map/ppermute | solution.py:221
  5.0 0.0 copy-done
  5.0 9.8 %self_energy.2 = (bf16[2,128,128]{2,1,0:T(8,128)(2,1)S(1)}, bf16[128,4096]{1,0:T(8,128)(2,1)S(1)}, bf16[4096,128]{1,0:T(8,128)(2,1)S(1)}) custom-call(f32[2,128,128]{2,1,0:T(8,128)S(1)} %get-tuple-element.23.green_ref, bf16[128,4096]{1,0:T(8,128)(2,1)S(1)} %copy-done), custom_call_target="tpu_custom_call" | custom-call | tf_op jit(solution)/shard_map/self_energy/pallas_call | solution.py:164
  14.7 0.1 collective-permute-start
  14.8 0.1 collective-permute-start.3
  14.9 4.2 %collective-permute-done = bf16[1,2,128,128]{3,2,1,0:T(8,128)(2,1)S(1)} collective-permute-done((bf16[1,2,128,128]{3,2,1,0:T(8,128)(2,1)S(1)}, bf16[1,2,128,128]{3,2,1,0:T(8,128)(2,1)S(1)}, u32[]{:S(2)}, u32[]{:S(2)}) %collective-permute-start) | collective-permute-done | bytes 65568 | tf_op jit(solution)/shard_map/ppermute | solution.py:221
  19.1 0.0 collective-permute-done.1.refs_2_
  19.1 0.1 collective-permute-start.4
  19.2 0.6 collective-permute-start.2
  19.8 0.0 collective-permute-done.3.refs_1_
  19.8 1.1 %collective-permute-done.2.far_ref = bf16[2,2,128,128]{3,2,1,0:T(8,128)(2,1)S(1)} collective-permute-done((bf16[2,2,128,128]{3,2,1,0:T(8,128)(2,1)S(1)}, bf16[2,2,128,128]{3,2,1,0:T(8,128)(2,1)S(1)}, u32[]{:S(2)}, u32[]{:S(2)}) %collective-permute-start.2) | collective-permute-done | bytes 131104 | tf_op jit(solution)/shard_map/ppermute | solution.py:221
  20.9 0.0 collective-permute-done.4.refs_3_
  20.9 1.0 %collide.2 = (f32[2,128,128]{2,1,0:T(8,128)S(1)}, bf16[2,128,128]{2,1,0:T(8,128)(2,1)S(1)}, bf16[2,128,128]{2,1,0:T(8,128)(2,1)S(1)}, bf16[2,128,128]{2,1,0:T(8,128)(2,1)S(1)}) custom-call(s32[2]{0:T(128)S(1)} %pad_add_fusion.place_ref, bf16[2,2,128,128]{3,2,1,0:T(8,128)(2,1)S(1)} %pad_maximum_fusion.near_ref, ...), custom_call_target="tpu_custom_call" | custom-call | tf_op jit(solution)/shard_map/collide/pallas_call | solution.py:205
  21.9 2.7 %collective-permute-start.5 = (bf16[2,128,128]{2,1,0:T(8,128)(2,1)S(1)}, bf16[2,128,128]{2,1,0:T(8,128)(2,1)S(1)}, u32[]{:S(2)}, u32[]{:S(2)}) collective-permute-start(bf16[2,128,128]{2,1,0:T(8,128)(2,1)S(1)} %get-tuple-element.32), channel_id=1, source_target_pairs={{0,8},{4,12},{8,0},{12,4},{1,9},{5,13},{9,1},{13,5},{2,10},{6,14},... | collective-permute-start | bytes 196616 | tf_op jit(solution)/shard_map/ppermute | solution.py:221
  24.6 1.3 %collective-permute-start.6 = (bf16[2,128,128]{2,1,0:T(8,128)(2,1)S(1)}, bf16[2,128,128]{2,1,0:T(8,128)(2,1)S(1)}, u32[]{:S(2)}, u32[]{:S(2)}) collective-permute-start(bf16[2,128,128]{2,1,0:T(8,128)(2,1)S(1)} %get-tuple-element.33), channel_id=1, source_target_pairs={{0,12},{4,8},{8,4},{12,0},{1,13},{5,9},{9,5},{13,1},{2,14},{6,10},... | collective-permute-start | bytes 196616 | tf_op jit(solution)/shard_map/ppermute | solution.py:221
  25.9 0.2 collective-permute-start.7
  26.2 2.7 %collective-permute-done.5 = bf16[2,128,128]{2,1,0:T(8,128)(2,1)S(1)} collective-permute-done((bf16[2,128,128]{2,1,0:T(8,128)(2,1)S(1)}, bf16[2,128,128]{2,1,0:T(8,128)(2,1)S(1)}, u32[]{:S(2)}, u32[]{:S(2)}) %collective-permute-start.5) | collective-permute-done | bytes 65568 | tf_op jit(solution)/shard_map/ppermute | solution.py:221
  28.8 2.2 %collective-permute-done.6 = bf16[2,128,128]{2,1,0:T(8,128)(2,1)S(1)} collective-permute-done((bf16[2,128,128]{2,1,0:T(8,128)(2,1)S(1)}, bf16[2,128,128]{2,1,0:T(8,128)(2,1)S(1)}, u32[]{:S(2)}, u32[]{:S(2)}) %collective-permute-start.6) | collective-permute-done | bytes 65568 | tf_op jit(solution)/shard_map/ppermute | solution.py:221
  31.1 0.3 collective-permute-done.7
  31.4 9.1 %self_energy.3 = bf16[2,128,128]{2,1,0:T(8,128)(2,1)S(1)} custom-call(f32[2,128,128]{2,1,0:T(8,128)S(1)} %convert_add_fusion.1.green_ref, bf16[128,4096]{1,0:T(8,128)(2,1)S(1)} %copy-done, bf16[128,4096]{1,0:T(8,128)(2,1)S(1)} %get-tuple-element.35.refs_0_, bf16[4096,128]{1,0:T(8,128)(2,1)S(1)} %get-tuple-element.36.refs_1_), custom_call_target="tpu_custom_call" | custom-call | tf_op jit(solution)/shard_map/self_energy/pallas_call | solution.py:164
  40.5 1.0 %collective-permute-start.8 = (bf16[1,2,128,128]{3,2,1,0:T(8,128)(2,1)S(1)}, bf16[1,2,128,128]{3,2,1,0:T(8,128)(2,1)S(1)}, u32[]{:S(2)}, u32[]{:S(2)}) collective-permute-start(bf16[1,2,128,128]{3,2,1,0:T(8,128)(2,1)S(1)} %bitcast.4), channel_id=1, source_target_pairs={{0,2},{1,3},{2,0},{3,1},{4,6},{5,7},{6,4},{7,5},{8,10},{9,11},{10,... | collective-permute-start | bytes 196616 | tf_op jit(solution)/shard_map/ppermute | solution.py:221
  41.5 3.3 %collective-permute-done.8 = bf16[1,2,128,128]{3,2,1,0:T(8,128)(2,1)S(1)} collective-permute-done((bf16[1,2,128,128]{3,2,1,0:T(8,128)(2,1)S(1)}, bf16[1,2,128,128]{3,2,1,0:T(8,128)(2,1)S(1)}, u32[]{:S(2)}, u32[]{:S(2)}) %collective-permute-start.8) | collective-permute-done | bytes 65568 | tf_op jit(solution)/shard_map/ppermute | solution.py:221
  44.8 0.1 collective-permute-start.9
  44.9 1.3 %collective-permute-done.9.far_ref = bf16[2,2,128,128]{3,2,1,0:T(8,128)(2,1)S(1)} collective-permute-done((bf16[2,2,128,128]{3,2,1,0:T(8,128)(2,1)S(1)}, bf16[2,2,128,128]{3,2,1,0:T(8,128)(2,1)S(1)}, u32[]{:S(2)}, u32[]{:S(2)}) %collective-permute-start.9) | collective-permute-done | bytes 131104 | tf_op jit(solution)/shard_map/ppermute | solution.py:221
  46.2 1.0 %collide.3 = (f32[2,128,128]{2,1,0:T(8,128)S(1)}, bf16[2,128,128]{2,1,0:T(8,128)(2,1)S(1)}, bf16[2,128,128]{2,1,0:T(8,128)(2,1)S(1)}, bf16[2,128,128]{2,1,0:T(8,128)(2,1)S(1)}) custom-call(s32[2]{0:T(128)S(1)} %pad_add_fusion.place_ref, bf16[2,2,128,128]{3,2,1,0:T(8,128)(2,1)S(1)} %pad_maximum_fusion.1.near_ref, ...), custom_call_target="tpu_custom_call" | custom-call | tf_op jit(solution)/shard_map/collide/pallas_call | solution.py:205
  47.3 2.7 %collective-permute-start.10 = (bf16[2,128,128]{2,1,0:T(8,128)(2,1)S(1)}, bf16[2,128,128]{2,1,0:T(8,128)(2,1)S(1)}, u32[]{:S(2)}, u32[]{:S(2)}) collective-permute-start(bf16[2,128,128]{2,1,0:T(8,128)(2,1)S(1)} %get-tuple-element.38), channel_id=1, source_target_pairs={{0,8},{4,12},{8,0},{12,4},{1,9},{5,13},{9,1},{13,5},{2,10},{6,14},... | collective-permute-start | bytes 196616 | tf_op jit(solution)/shard_map/ppermute | solution.py:221
  49.9 0.7 %collective-permute-start.11 = (bf16[2,128,128]{2,1,0:T(8,128)(2,1)S(1)}, bf16[2,128,128]{2,1,0:T(8,128)(2,1)S(1)}, u32[]{:S(2)}, u32[]{:S(2)}) collective-permute-start(bf16[2,128,128]{2,1,0:T(8,128)(2,1)S(1)} %get-tuple-element.39), channel_id=1, source_target_pairs={{0,12},{4,8},{8,4},{12,0},{1,13},{5,9},{9,5},{13,1},{2,14},{6,10},... | collective-permute-start | bytes 196616 | tf_op jit(solution)/shard_map/ppermute | solution.py:221
  50.7 0.5 collective-permute-start.12
  51.1 4.0 %collective-permute-done.10 = bf16[2,128,128]{2,1,0:T(8,128)(2,1)S(1)} collective-permute-done((bf16[2,128,128]{2,1,0:T(8,128)(2,1)S(1)}, bf16[2,128,128]{2,1,0:T(8,128)(2,1)S(1)}, u32[]{:S(2)}, u32[]{:S(2)}) %collective-permute-start.10) | collective-permute-done | bytes 65568 | tf_op jit(solution)/shard_map/ppermute | solution.py:221
  55.2 1.2 %collective-permute-done.11 = bf16[2,128,128]{2,1,0:T(8,128)(2,1)S(1)} collective-permute-done((bf16[2,128,128]{2,1,0:T(8,128)(2,1)S(1)}, bf16[2,128,128]{2,1,0:T(8,128)(2,1)S(1)}, u32[]{:S(2)}, u32[]{:S(2)}) %collective-permute-start.11) | collective-permute-done | bytes 65568 | tf_op jit(solution)/shard_map/ppermute | solution.py:221
  56.3 0.3 collective-permute-done.12
  56.6 0.7 %convert_add_fusion = f32[2,128,128]{2,1,0:T(8,128)} fusion(bf16[2,128,128]{2,1,0:T(8,128)(2,1)S(1)} %collective-permute-done.12, bf16[2,128,128]{2,1,0:T(8,128)(2,1)S(1)} %collective-permute-done.11, bf16[2,128,128]{2,1,0:T(8,128)(2,1)S(1)} %collective-permute-done.10, f32[2,128,128]{2,1,0:T(8,128)S(1)} %get-tuple-element.23.green_ref, ...), kind=kLoop, calls=%fused_computation.2 | loop fusion | flops 229376 | bytes 589824 | tf_op jit(solution)/shard_map/add | solution.py:266
  (4 shorter events, 0.1 us)
Async XLA Ops:
  0.0 5.0 %copy-start = (bf16[128,4096]{1,0:T(8,128)(2,1)S(1)}, bf16[128,4096]{1,0:T(8,128)(2,1)}, u32[]{:S(2)}) copy-start(bf16[128,4096]{1,0:T(8,128)(2,1)} %fit_ref.3) | copy-start | bytes 3145732
  1.9 17.1 %collective-permute-start.1 = (bf16[2,2,512,128]{3,2,1,0:T(8,128)(2,1)S(1)}, bf16[2,2,512,128]{3,2,1,0:T(8,128)(2,1)S(1)}, u32[]{:S(2)}, u32[]{:S(2)}) collective-permute-start(bf16[2,2,512,128]{3,2,1,0:T(8,128)(2,1)S(1)} %get-tuple-element.26), channel_id=1, source_target_pairs={{0,2},{1,3},{2,0},{3,1},{4,6},{5,7},{6,4},{7,5},{8,10},{9,11},{10,... | collective-permute-start | bytes 1572872 | tf_op jit(solution)/shard_map/ppermute | solution.py:221
  14.7 4.3 %collective-permute-start = (bf16[1,2,128,128]{3,2,1,0:T(8,128)(2,1)S(1)}, bf16[1,2,128,128]{3,2,1,0:T(8,128)(2,1)S(1)}, u32[]{:S(2)}, u32[]{:S(2)}) collective-permute-start(bf16[1,2,128,128]{3,2,1,0:T(8,128)(2,1)S(1)} %bitcast.6), channel_id=1, source_target_pairs={{0,2},{1,3},{2,0},{3,1},{4,6},{5,7},{6,4},{7,5},{8,10},{9,11},{10,... | collective-permute-start | bytes 196616 | tf_op jit(solution)/shard_map/ppermute | solution.py:221
  14.8 4.9 %collective-permute-start.3 = (bf16[1,2,512,128]{3,2,1,0:T(8,128)(2,1)S(1)}, bf16[1,2,512,128]{3,2,1,0:T(8,128)(2,1)S(1)}, u32[]{:S(2)}, u32[]{:S(2)}) collective-permute-start(bf16[1,2,512,128]{3,2,1,0:T(8,128)(2,1)S(1)} %get-tuple-element.29), channel_id=1, source_target_pairs={{0,1},{1,0},{2,3},{3,2},{4,5},{5,4},{6,7},{7,6},{8,9},{9,8},{10,11... | collective-permute-start | bytes 786440 | tf_op jit(solution)/shard_map/ppermute | solution.py:221
  19.1 1.8 %collective-permute-start.4 = (bf16[1,2,512,128]{3,2,1,0:T(8,128)(2,1)S(1)}, bf16[1,2,512,128]{3,2,1,0:T(8,128)(2,1)S(1)}, u32[]{:S(2)}, u32[]{:S(2)}) collective-permute-start(bf16[1,2,512,128]{3,2,1,0:T(8,128)(2,1)S(1)} %slice.3), channel_id=1, source_target_pairs={{0,1},{1,0},{2,3},{3,2},{4,5},{5,4},{6,7},{7,6},{8,9},{9,8},{10,11... | collective-permute-start | bytes 786440 | tf_op jit(solution)/shard_map/ppermute | solution.py:221
  19.2 1.7 %collective-permute-start.2 = (bf16[2,2,128,128]{3,2,1,0:T(8,128)(2,1)S(1)}, bf16[2,2,128,128]{3,2,1,0:T(8,128)(2,1)S(1)}, u32[]{:S(2)}, u32[]{:S(2)}) collective-permute-start(bf16[2,2,128,128]{3,2,1,0:T(8,128)(2,1)S(1)} %pad_maximum_fusion.near_ref), channel_id=1, source_target_pairs={{0,1},{1,0},{2,3},{3,2},{4,5},{5,4},{6,7},{7,6},{8,9},{9,8},{10,11... | collective-permute-start | bytes 393224 | tf_op jit(solution)/shard_map/ppermute | solution.py:221
  21.9 6.9 %collective-permute-start.5 = (bf16[2,128,128]{2,1,0:T(8,128)(2,1)S(1)}, bf16[2,128,128]{2,1,0:T(8,128)(2,1)S(1)}, u32[]{:S(2)}, u32[]{:S(2)}) collective-permute-start(bf16[2,128,128]{2,1,0:T(8,128)(2,1)S(1)} %get-tuple-element.32), channel_id=1, source_target_pairs={{0,8},{4,12},{8,0},{12,4},{1,9},{5,13},{9,1},{13,5},{2,10},{6,14},... | collective-permute-start | bytes 196616 | tf_op jit(solution)/shard_map/ppermute | solution.py:221
  24.6 6.5 %collective-permute-start.6 = (bf16[2,128,128]{2,1,0:T(8,128)(2,1)S(1)}, bf16[2,128,128]{2,1,0:T(8,128)(2,1)S(1)}, u32[]{:S(2)}, u32[]{:S(2)}) collective-permute-start(bf16[2,128,128]{2,1,0:T(8,128)(2,1)S(1)} %get-tuple-element.33), channel_id=1, source_target_pairs={{0,12},{4,8},{8,4},{12,0},{1,13},{5,9},{9,5},{13,1},{2,14},{6,10},... | collective-permute-start | bytes 196616 | tf_op jit(solution)/shard_map/ppermute | solution.py:221
  25.9 5.4 %collective-permute-start.7 = (bf16[2,128,128]{2,1,0:T(8,128)(2,1)S(1)}, bf16[2,128,128]{2,1,0:T(8,128)(2,1)S(1)}, u32[]{:S(2)}, u32[]{:S(2)}) collective-permute-start(bf16[2,128,128]{2,1,0:T(8,128)(2,1)S(1)} %get-tuple-element.34), channel_id=1, source_target_pairs={{0,4},{4,0},{8,12},{12,8},{1,5},{5,1},{9,13},{13,9},{2,6},{6,2},{1... | collective-permute-start | bytes 196616 | tf_op jit(solution)/shard_map/ppermute | solution.py:221
  40.5 4.3 %collective-permute-start.8 = (bf16[1,2,128,128]{3,2,1,0:T(8,128)(2,1)S(1)}, bf16[1,2,128,128]{3,2,1,0:T(8,128)(2,1)S(1)}, u32[]{:S(2)}, u32[]{:S(2)}) collective-permute-start(bf16[1,2,128,128]{3,2,1,0:T(8,128)(2,1)S(1)} %bitcast.4), channel_id=1, source_target_pairs={{0,2},{1,3},{2,0},{3,1},{4,6},{5,7},{6,4},{7,5},{8,10},{9,11},{10,... | collective-permute-start | bytes 196616 | tf_op jit(solution)/shard_map/ppermute | solution.py:221
  44.8 1.4 %collective-permute-start.9 = (bf16[2,2,128,128]{3,2,1,0:T(8,128)(2,1)S(1)}, bf16[2,2,128,128]{3,2,1,0:T(8,128)(2,1)S(1)}, u32[]{:S(2)}, u32[]{:S(2)}) collective-permute-start(bf16[2,2,128,128]{3,2,1,0:T(8,128)(2,1)S(1)} %pad_maximum_fusion.1.near_ref), channel_id=1, source_target_pairs={{0,1},{1,0},{2,3},{3,2},{4,5},{5,4},{6,7},{7,6},{8,9},{9,8},{10,11... | collective-permute-start | bytes 393224 | tf_op jit(solution)/shard_map/ppermute | solution.py:221
  47.3 7.9 %collective-permute-start.10 = (bf16[2,128,128]{2,1,0:T(8,128)(2,1)S(1)}, bf16[2,128,128]{2,1,0:T(8,128)(2,1)S(1)}, u32[]{:S(2)}, u32[]{:S(2)}) collective-permute-start(bf16[2,128,128]{2,1,0:T(8,128)(2,1)S(1)} %get-tuple-element.38), channel_id=1, source_target_pairs={{0,8},{4,12},{8,0},{12,4},{1,9},{5,13},{9,1},{13,5},{2,10},{6,14},... | collective-permute-start | bytes 196616 | tf_op jit(solution)/shard_map/ppermute | solution.py:221
  49.9 6.4 %collective-permute-start.11 = (bf16[2,128,128]{2,1,0:T(8,128)(2,1)S(1)}, bf16[2,128,128]{2,1,0:T(8,128)(2,1)S(1)}, u32[]{:S(2)}, u32[]{:S(2)}) collective-permute-start(bf16[2,128,128]{2,1,0:T(8,128)(2,1)S(1)} %get-tuple-element.39), channel_id=1, source_target_pairs={{0,12},{4,8},{8,4},{12,0},{1,13},{5,9},{9,5},{13,1},{2,14},{6,10},... | collective-permute-start | bytes 196616 | tf_op jit(solution)/shard_map/ppermute | solution.py:221
  50.7 5.9 %collective-permute-start.12 = (bf16[2,128,128]{2,1,0:T(8,128)(2,1)S(1)}, bf16[2,128,128]{2,1,0:T(8,128)(2,1)S(1)}, u32[]{:S(2)}, u32[]{:S(2)}) collective-permute-start(bf16[2,128,128]{2,1,0:T(8,128)(2,1)S(1)} %get-tuple-element.40), channel_id=1, source_target_pairs={{0,4},{4,0},{8,12},{12,8},{1,5},{5,1},{9,13},{13,9},{2,6},{6,2},{1... | collective-permute-start | bytes 196616 | tf_op jit(solution)/shard_map/ppermute | solution.py:221

commit v5 on v4

--- a/solution.py
+++ b/solution.py
@@ -70,9 +70,9 @@
 
 def energy_kernel(orbitals, turn, green_ref, fit_ref, *refs):
     if turn:
-        out_ref, turned_ref, tall_ref, spread, left, under, wide = refs
+        out_ref, turned_ref, tall_ref, spread, under, wide = refs
     else:
-        turned_ref, tall_ref, out_ref, spread, left, under = refs
+        turned_ref, tall_ref, out_ref, spread, under = refs
     aux, flat = fit_ref.shape
     times = green_ref.shape[2] // orbitals
     new = green_ref.shape[1] // orbitals
@@ -121,8 +121,6 @@
         for n in range(pairs):
             a, k = divmod(n, times)
             x = [spread[n, pl.ds((m + h) * pitch, rows), :].astype(BF16) for h in range(2)]
-            for h in range(2):
-                left[n, (m + h) * rows : (m + h + 1) * rows, :] = x[h]
             r = dot(around[a][k * orbitals : (k + 1) * orbitals], jnp.concatenate(x, axis=1))
             for h in range(2):
                 under[(m + h) * orbitals : (m + h + 1) * orbitals, n * aux : (n + 1) * aux] = r[
@@ -139,7 +137,7 @@
                 screened[(l + h) * orbitals : (l + h + 1) * orbitals, n * aux : (n + 1) * aux]
                 for h in range(group)
             ]
-            b = [left[n, (l + h) * rows : (l + h + 1) * rows, :] for h in range(group)]
+            b = [spread[n, pl.ds((l + h) * pitch, rows), :].astype(BF16) for h in range(group)]
             acc = acc + dot_nt(jnp.concatenate(a, axis=1), jnp.concatenate(b, axis=1))
         block = (acc * scale).T.astype(BF16)
         a, k = divmod(n, times)
@@ -158,14 +156,13 @@
     forms = [jax.ShapeDtypeStruct((aux, flat), BF16), jax.ShapeDtypeStruct((flat, aux), BF16)]
     scratch = [
         pltpu.VMEM((pairs, orbitals * (2 * orbitals + 1), aux), F32),
-        pltpu.VMEM((pairs, 2 * flat, aux), BF16),
         pltpu.VMEM((flat, pairs * aux), BF16),
     ]
     return pl.pallas_call(
         functools.partial(energy_kernel, orbitals, turn),
         out_shape=[out_shape, *forms] if turn else out_shape,
         scratch_shapes=scratch + [pltpu.VMEM((flat, aux), F32)] * turn,
-        compiler_params=pltpu.CompilerParams(vmem_limit_bytes=36 * MIB),
+        compiler_params=pltpu.CompilerParams(vmem_limit_bytes=28 * MIB),
         name="self_energy",
     )(green, fit, *(() if turn else turned))
 

time: 57.4 us -> 56.3 us (0.981)
  Pallas kernels: 22.8 us -> 21.6 us
    pallas_call x2, Pallas kernels: 18.9 us -> 17.7 us  [energy(): pl.pallas_call(functools.partial(energy_kernel, orbitals, turn), out_shap...]
where the time goes in v5:
time: 56.3 us; the launch traced here: 56.1 us
  Pallas kernels  21.6 us (38%)
  waiting for transfers between devices  20.4 us (36%)
  starting transfers between devices  13.2 us (23%)
  other arithmetic  0.84 us (1%)
    ppermute x13, waiting for transfers between devices, swap(): return lax.ppermute(x, axis, [(d, d ^ step) for d in range(size)])  20.4 us
    pallas_call x2, Pallas kernels, energy(): pl.pallas_call(functools.partial(energy_kernel, orbitals, turn), out_shap...  17.7 us
    ppermute x13, starting transfers between devices, swap(): return lax.ppermute(x, axis, [(d, d ^ step) for d in range(size)])  13.2 us
    pallas_call x2, Pallas kernels, collide(): pl.pallas_call(functools.partial(collide_kernel, offsets, row_devices), g...  2.04 us
    pallas_call x1, Pallas kernels, split_history(): pl.pallas_call(split_kernel, out_shape=[jax.ShapeDtypeStruct(green.shape,...  1.86 us
  transfers between devices with their start and end apart: 13, of which 10 were waited for; matrix products, arithmetic and copies ran while one was open for 0% of the time, Pallas kernels for 17%

profile of v5, /device:TPU:0, one launch (start us, length us, event | category | flops | bytes accessed | tf_op | source)
XLA Modules:
  0.0 56.1 jit_solution(12273759370696472800)
XLA Ops:
  0.0 0.0 copy-start
  0.0 0.1 pad_add_fusion.place_ref
  0.1 1.9 %split_history.1 = (f32[2,128,128]{2,1,0:T(8,128)S(1)}, bf16[1,2,512,128]{3,2,1,0:T(8,128)(2,1)S(1)}, bf16[1,2,512,128]{3,2,1,0:T(8,128)(2,1)S(1)}, bf16[2,2,512,128]{3,2,1,0:T(8,128)(2,1)S(1)}) custom-call(s32[2]{0:T(128)S(1)} %pad_add_fusion.place_ref, f32[2,128,128]{2,1,0:T(8,128)} %green_ref.1, bf16[2,512,512]{2,1,0:T(8,128)(2,1)} %history_ref.1), custom_call_target="tpu_custom_call" | custom-call | tf_op jit(solution)/shard_map/split_history/pallas_call | solution.py:55
  1.9 3.0 %collective-permute-start.1 = (bf16[2,2,512,128]{3,2,1,0:T(8,128)(2,1)S(1)}, bf16[2,2,512,128]{3,2,1,0:T(8,128)(2,1)S(1)}, u32[]{:S(2)}, u32[]{:S(2)}) collective-permute-start(bf16[2,2,512,128]{3,2,1,0:T(8,128)(2,1)S(1)} %get-tuple-element.26), channel_id=1, source_target_pairs={{0,2},{1,3},{2,0},{3,1},{4,6},{5,7},{6,4},{7,5},{8,10},{9,11},{10,... | collective-permute-start | bytes 1572872 | tf_op jit(solution)/shard_map/ppermute | solution.py:218
  5.0 0.0 copy-done
  5.0 9.6 %self_energy.2 = (bf16[2,128,128]{2,1,0:T(8,128)(2,1)S(1)}, bf16[128,4096]{1,0:T(8,128)(2,1)S(1)}, bf16[4096,128]{1,0:T(8,128)(2,1)S(1)}) custom-call(f32[2,128,128]{2,1,0:T(8,128)S(1)} %get-tuple-element.23.green_ref, bf16[128,4096]{1,0:T(8,128)(2,1)S(1)} %copy-done), custom_call_target="tpu_custom_call" | custom-call | tf_op jit(solution)/shard_map/self_energy/pallas_call | solution.py:161
  14.5 0.1 collective-permute-start
  14.6 0.1 collective-permute-start.3
  14.7 4.2 %collective-permute-done = bf16[1,2,128,128]{3,2,1,0:T(8,128)(2,1)S(1)} collective-permute-done((bf16[1,2,128,128]{3,2,1,0:T(8,128)(2,1)S(1)}, bf16[1,2,128,128]{3,2,1,0:T(8,128)(2,1)S(1)}, u32[]{:S(2)}, u32[]{:S(2)}) %collective-permute-start) | collective-permute-done | bytes 65568 | tf_op jit(solution)/shard_map/ppermute | solution.py:218
  18.9 0.0 collective-permute-done.1.refs_2_
  18.9 0.1 collective-permute-start.4
  19.0 0.6 collective-permute-start.2
  19.6 0.0 collective-permute-done.3.refs_1_
  19.6 1.1 %collective-permute-done.2.far_ref = bf16[2,2,128,128]{3,2,1,0:T(8,128)(2,1)S(1)} collective-permute-done((bf16[2,2,128,128]{3,2,1,0:T(8,128)(2,1)S(1)}, bf16[2,2,128,128]{3,2,1,0:T(8,128)(2,1)S(1)}, u32[]{:S(2)}, u32[]{:S(2)}) %collective-permute-start.2) | collective-permute-done | bytes 131104 | tf_op jit(solution)/shard_map/ppermute | solution.py:218
  20.7 0.0 collective-permute-done.4.refs_3_
  20.7 1.0 %collide.2 = (f32[2,128,128]{2,1,0:T(8,128)S(1)}, bf16[2,128,128]{2,1,0:T(8,128)(2,1)S(1)}, bf16[2,128,128]{2,1,0:T(8,128)(2,1)S(1)}, bf16[2,128,128]{2,1,0:T(8,128)(2,1)S(1)}) custom-call(s32[2]{0:T(128)S(1)} %pad_add_fusion.place_ref, bf16[2,2,128,128]{3,2,1,0:T(8,128)(2,1)S(1)} %pad_maximum_fusion.near_ref, ...), custom_call_target="tpu_custom_call" | custom-call | tf_op jit(solution)/shard_map/collide/pallas_call | solution.py:202
  21.7 2.6 %collective-permute-start.5 = (bf16[2,128,128]{2,1,0:T(8,128)(2,1)S(1)}, bf16[2,128,128]{2,1,0:T(8,128)(2,1)S(1)}, u32[]{:S(2)}, u32[]{:S(2)}) collective-permute-start(bf16[2,128,128]{2,1,0:T(8,128)(2,1)S(1)} %get-tuple-element.32), channel_id=1, source_target_pairs={{0,8},{4,12},{8,0},{12,4},{1,9},{5,13},{9,1},{13,5},{2,10},{6,14},... | collective-permute-start | bytes 196616 | tf_op jit(solution)/shard_map/ppermute | solution.py:218
  24.4 1.3 %collective-permute-start.6 = (bf16[2,128,128]{2,1,0:T(8,128)(2,1)S(1)}, bf16[2,128,128]{2,1,0:T(8,128)(2,1)S(1)}, u32[]{:S(2)}, u32[]{:S(2)}) collective-permute-start(bf16[2,128,128]{2,1,0:T(8,128)(2,1)S(1)} %get-tuple-element.33), channel_id=1, source_target_pairs={{0,12},{4,8},{8,4},{12,0},{1,13},{5,9},{9,5},{13,1},{2,14},{6,10},... | collective-permute-start | bytes 196616 | tf_op jit(solution)/shard_map/ppermute | solution.py:218
  25.7 0.2 collective-permute-start.7
  25.9 2.7 %collective-permute-done.5 = bf16[2,128,128]{2,1,0:T(8,128)(2,1)S(1)} collective-permute-done((bf16[2,128,128]{2,1,0:T(8,128)(2,1)S(1)}, bf16[2,128,128]{2,1,0:T(8,128)(2,1)S(1)}, u32[]{:S(2)}, u32[]{:S(2)}) %collective-permute-start.5) | collective-permute-done | bytes 65568 | tf_op jit(solution)/shard_map/ppermute | solution.py:218
  28.6 2.2 %collective-permute-done.6 = bf16[2,128,128]{2,1,0:T(8,128)(2,1)S(1)} collective-permute-done((bf16[2,128,128]{2,1,0:T(8,128)(2,1)S(1)}, bf16[2,128,128]{2,1,0:T(8,128)(2,1)S(1)}, u32[]{:S(2)}, u32[]{:S(2)}) %collective-permute-start.6) | collective-permute-done | bytes 65568 | tf_op jit(solution)/shard_map/ppermute | solution.py:218
  30.8 0.3 collective-permute-done.7
  31.2 8.1 %self_energy.3 = bf16[2,128,128]{2,1,0:T(8,128)(2,1)S(1)} custom-call(f32[2,128,128]{2,1,0:T(8,128)S(1)} %convert_add_fusion.1.green_ref, bf16[128,4096]{1,0:T(8,128)(2,1)S(1)} %copy-done, bf16[128,4096]{1,0:T(8,128)(2,1)S(1)} %get-tuple-element.35.refs_0_, bf16[4096,128]{1,0:T(8,128)(2,1)S(1)} %get-tuple-element.36.refs_1_), custom_call_target="tpu_custom_call" | custom-call | tf_op jit(solution)/shard_map/self_energy/pallas_call | solution.py:161
  39.3 1.2 %collective-permute-start.8 = (bf16[1,2,128,128]{3,2,1,0:T(8,128)(2,1)S(1)}, bf16[1,2,128,128]{3,2,1,0:T(8,128)(2,1)S(1)}, u32[]{:S(2)}, u32[]{:S(2)}) collective-permute-start(bf16[1,2,128,128]{3,2,1,0:T(8,128)(2,1)S(1)} %bitcast.4), channel_id=1, source_target_pairs={{0,2},{1,3},{2,0},{3,1},{4,6},{5,7},{6,4},{7,5},{8,10},{9,11},{10,... | collective-permute-start | bytes 196616 | tf_op jit(solution)/shard_map/ppermute | solution.py:218
  40.5 3.1 %collective-permute-done.8 = bf16[1,2,128,128]{3,2,1,0:T(8,128)(2,1)S(1)} collective-permute-done((bf16[1,2,128,128]{3,2,1,0:T(8,128)(2,1)S(1)}, bf16[1,2,128,128]{3,2,1,0:T(8,128)(2,1)S(1)}, u32[]{:S(2)}, u32[]{:S(2)}) %collective-permute-start.8) | collective-permute-done | bytes 65568 | tf_op jit(solution)/shard_map/ppermute | solution.py:218
  43.7 0.1 collective-permute-start.9
  43.7 1.3 %collective-permute-done.9.far_ref = bf16[2,2,128,128]{3,2,1,0:T(8,128)(2,1)S(1)} collective-permute-done((bf16[2,2,128,128]{3,2,1,0:T(8,128)(2,1)S(1)}, bf16[2,2,128,128]{3,2,1,0:T(8,128)(2,1)S(1)}, u32[]{:S(2)}, u32[]{:S(2)}) %collective-permute-start.9) | collective-permute-done | bytes 131104 | tf_op jit(solution)/shard_map/ppermute | solution.py:218
  45.1 1.0 %collide.3 = (f32[2,128,128]{2,1,0:T(8,128)S(1)}, bf16[2,128,128]{2,1,0:T(8,128)(2,1)S(1)}, bf16[2,128,128]{2,1,0:T(8,128)(2,1)S(1)}, bf16[2,128,128]{2,1,0:T(8,128)(2,1)S(1)}) custom-call(s32[2]{0:T(128)S(1)} %pad_add_fusion.place_ref, bf16[2,2,128,128]{3,2,1,0:T(8,128)(2,1)S(1)} %pad_maximum_fusion.1.near_ref, ...), custom_call_target="tpu_custom_call" | custom-call | tf_op jit(solution)/shard_map/collide/pallas_call | solution.py:202
  46.1 2.7 %collective-permute-start.10 = (bf16[2,128,128]{2,1,0:T(8,128)(2,1)S(1)}, bf16[2,128,128]{2,1,0:T(8,128)(2,1)S(1)}, u32[]{:S(2)}, u32[]{:S(2)}) collective-permute-start(bf16[2,128,128]{2,1,0:T(8,128)(2,1)S(1)} %get-tuple-element.38), channel_id=1, source_target_pairs={{0,8},{4,12},{8,0},{12,4},{1,9},{5,13},{9,1},{13,5},{2,10},{6,14},... | collective-permute-start | bytes 196616 | tf_op jit(solution)/shard_map/ppermute | solution.py:218
  48.8 0.7 %collective-permute-start.11 = (bf16[2,128,128]{2,1,0:T(8,128)(2,1)S(1)}, bf16[2,128,128]{2,1,0:T(8,128)(2,1)S(1)}, u32[]{:S(2)}, u32[]{:S(2)}) collective-permute-start(bf16[2,128,128]{2,1,0:T(8,128)(2,1)S(1)} %get-tuple-element.39), channel_id=1, source_target_pairs={{0,12},{4,8},{8,4},{12,0},{1,13},{5,9},{9,5},{13,1},{2,14},{6,10},... | collective-permute-start | bytes 196616 | tf_op jit(solution)/shard_map/ppermute | solution.py:218
  49.5 0.5 collective-permute-start.12
  50.0 4.0 %collective-permute-done.10 = bf16[2,128,128]{2,1,0:T(8,128)(2,1)S(1)} collective-permute-done((bf16[2,128,128]{2,1,0:T(8,128)(2,1)S(1)}, bf16[2,128,128]{2,1,0:T(8,128)(2,1)S(1)}, u32[]{:S(2)}, u32[]{:S(2)}) %collective-permute-start.10) | collective-permute-done | bytes 65568 | tf_op jit(solution)/shard_map/ppermute | solution.py:218
  54.0 1.2 %collective-permute-done.11 = bf16[2,128,128]{2,1,0:T(8,128)(2,1)S(1)} collective-permute-done((bf16[2,128,128]{2,1,0:T(8,128)(2,1)S(1)}, bf16[2,128,128]{2,1,0:T(8,128)(2,1)S(1)}, u32[]{:S(2)}, u32[]{:S(2)}) %collective-permute-start.11) | collective-permute-done | bytes 65568 | tf_op jit(solution)/shard_map/ppermute | solution.py:218
  55.2 0.3 collective-permute-done.12
  55.4 0.7 %convert_add_fusion = f32[2,128,128]{2,1,0:T(8,128)} fusion(bf16[2,128,128]{2,1,0:T(8,128)(2,1)S(1)} %collective-permute-done.12, bf16[2,128,128]{2,1,0:T(8,128)(2,1)S(1)} %collective-permute-done.11, bf16[2,128,128]{2,1,0:T(8,128)(2,1)S(1)} %collective-permute-done.10, f32[2,128,128]{2,1,0:T(8,128)S(1)} %get-tuple-element.23.green_ref, ...), kind=kLoop, calls=%fused_computation.2 | loop fusion | flops 229376 | bytes 589824 | tf_op jit(solution)/shard_map/add | solution.py:263
  (4 shorter events, 0.1 us)
Async XLA Ops:
  0.0 5.0 %copy-start = (bf16[128,4096]{1,0:T(8,128)(2,1)S(1)}, bf16[128,4096]{1,0:T(8,128)(2,1)}, u32[]{:S(2)}) copy-start(bf16[128,4096]{1,0:T(8,128)(2,1)} %fit_ref.3) | copy-start | bytes 3145732
  1.9 16.9 %collective-permute-start.1 = (bf16[2,2,512,128]{3,2,1,0:T(8,128)(2,1)S(1)}, bf16[2,2,512,128]{3,2,1,0:T(8,128)(2,1)S(1)}, u32[]{:S(2)}, u32[]{:S(2)}) collective-permute-start(bf16[2,2,512,128]{3,2,1,0:T(8,128)(2,1)S(1)} %get-tuple-element.26), channel_id=1, source_target_pairs={{0,2},{1,3},{2,0},{3,1},{4,6},{5,7},{6,4},{7,5},{8,10},{9,11},{10,... | collective-permute-start | bytes 1572872 | tf_op jit(solution)/shard_map/ppermute | solution.py:218
  14.5 4.3 %collective-permute-start = (bf16[1,2,128,128]{3,2,1,0:T(8,128)(2,1)S(1)}, bf16[1,2,128,128]{3,2,1,0:T(8,128)(2,1)S(1)}, u32[]{:S(2)}, u32[]{:S(2)}) collective-permute-start(bf16[1,2,128,128]{3,2,1,0:T(8,128)(2,1)S(1)} %bitcast.6), channel_id=1, source_target_pairs={{0,2},{1,3},{2,0},{3,1},{4,6},{5,7},{6,4},{7,5},{8,10},{9,11},{10,... | collective-permute-start | bytes 196616 | tf_op jit(solution)/shard_map/ppermute | solution.py:218
  14.6 4.9 %collective-permute-start.3 = (bf16[1,2,512,128]{3,2,1,0:T(8,128)(2,1)S(1)}, bf16[1,2,512,128]{3,2,1,0:T(8,128)(2,1)S(1)}, u32[]{:S(2)}, u32[]{:S(2)}) collective-permute-start(bf16[1,2,512,128]{3,2,1,0:T(8,128)(2,1)S(1)} %get-tuple-element.29), channel_id=1, source_target_pairs={{0,1},{1,0},{2,3},{3,2},{4,5},{5,4},{6,7},{7,6},{8,9},{9,8},{10,11... | collective-permute-start | bytes 786440 | tf_op jit(solution)/shard_map/ppermute | solution.py:218
  18.9 1.8 %collective-permute-start.4 = (bf16[1,2,512,128]{3,2,1,0:T(8,128)(2,1)S(1)}, bf16[1,2,512,128]{3,2,1,0:T(8,128)(2,1)S(1)}, u32[]{:S(2)}, u32[]{:S(2)}) collective-permute-start(bf16[1,2,512,128]{3,2,1,0:T(8,128)(2,1)S(1)} %slice.3), channel_id=1, source_target_pairs={{0,1},{1,0},{2,3},{3,2},{4,5},{5,4},{6,7},{7,6},{8,9},{9,8},{10,11... | collective-permute-start | bytes 786440 | tf_op jit(solution)/shard_map/ppermute | solution.py:218
  19.0 1.7 %collective-permute-start.2 = (bf16[2,2,128,128]{3,2,1,0:T(8,128)(2,1)S(1)}, bf16[2,2,128,128]{3,2,1,0:T(8,128)(2,1)S(1)}, u32[]{:S(2)}, u32[]{:S(2)}) collective-permute-start(bf16[2,2,128,128]{3,2,1,0:T(8,128)(2,1)S(1)} %pad_maximum_fusion.near_ref), channel_id=1, source_target_pairs={{0,1},{1,0},{2,3},{3,2},{4,5},{5,4},{6,7},{7,6},{8,9},{9,8},{10,11... | collective-permute-start | bytes 393224 | tf_op jit(solution)/shard_map/ppermute | solution.py:218
  21.7 6.9 %collective-permute-start.5 = (bf16[2,128,128]{2,1,0:T(8,128)(2,1)S(1)}, bf16[2,128,128]{2,1,0:T(8,128)(2,1)S(1)}, u32[]{:S(2)}, u32[]{:S(2)}) collective-permute-start(bf16[2,128,128]{2,1,0:T(8,128)(2,1)S(1)} %get-tuple-element.32), channel_id=1, source_target_pairs={{0,8},{4,12},{8,0},{12,4},{1,9},{5,13},{9,1},{13,5},{2,10},{6,14},... | collective-permute-start | bytes 196616 | tf_op jit(solution)/shard_map/ppermute | solution.py:218
  24.4 6.5 %collective-permute-start.6 = (bf16[2,128,128]{2,1,0:T(8,128)(2,1)S(1)}, bf16[2,128,128]{2,1,0:T(8,128)(2,1)S(1)}, u32[]{:S(2)}, u32[]{:S(2)}) collective-permute-start(bf16[2,128,128]{2,1,0:T(8,128)(2,1)S(1)} %get-tuple-element.33), channel_id=1, source_target_pairs={{0,12},{4,8},{8,4},{12,0},{1,13},{5,9},{9,5},{13,1},{2,14},{6,10},... | collective-permute-start | bytes 196616 | tf_op jit(solution)/shard_map/ppermute | solution.py:218
  25.7 5.4 %collective-permute-start.7 = (bf16[2,128,128]{2,1,0:T(8,128)(2,1)S(1)}, bf16[2,128,128]{2,1,0:T(8,128)(2,1)S(1)}, u32[]{:S(2)}, u32[]{:S(2)}) collective-permute-start(bf16[2,128,128]{2,1,0:T(8,128)(2,1)S(1)} %get-tuple-element.34), channel_id=1, source_target_pairs={{0,4},{4,0},{8,12},{12,8},{1,5},{5,1},{9,13},{13,9},{2,6},{6,2},{1... | collective-permute-start | bytes 196616 | tf_op jit(solution)/shard_map/ppermute | solution.py:218
  39.3 4.3 %collective-permute-start.8 = (bf16[1,2,128,128]{3,2,1,0:T(8,128)(2,1)S(1)}, bf16[1,2,128,128]{3,2,1,0:T(8,128)(2,1)S(1)}, u32[]{:S(2)}, u32[]{:S(2)}) collective-permute-start(bf16[1,2,128,128]{3,2,1,0:T(8,128)(2,1)S(1)} %bitcast.4), channel_id=1, source_target_pairs={{0,2},{1,3},{2,0},{3,1},{4,6},{5,7},{6,4},{7,5},{8,10},{9,11},{10,... | collective-permute-start | bytes 196616 | tf_op jit(solution)/shard_map/ppermute | solution.py:218
  43.7 1.4 %collective-permute-start.9 = (bf16[2,2,128,128]{3,2,1,0:T(8,128)(2,1)S(1)}, bf16[2,2,128,128]{3,2,1,0:T(8,128)(2,1)S(1)}, u32[]{:S(2)}, u32[]{:S(2)}) collective-permute-start(bf16[2,2,128,128]{3,2,1,0:T(8,128)(2,1)S(1)} %pad_maximum_fusion.1.near_ref), channel_id=1, source_target_pairs={{0,1},{1,0},{2,3},{3,2},{4,5},{5,4},{6,7},{7,6},{8,9},{9,8},{10,11... | collective-permute-start | bytes 393224 | tf_op jit(solution)/shard_map/ppermute | solution.py:218
  46.1 7.9 %collective-permute-start.10 = (bf16[2,128,128]{2,1,0:T(8,128)(2,1)S(1)}, bf16[2,128,128]{2,1,0:T(8,128)(2,1)S(1)}, u32[]{:S(2)}, u32[]{:S(2)}) collective-permute-start(bf16[2,128,128]{2,1,0:T(8,128)(2,1)S(1)} %get-tuple-element.38), channel_id=1, source_target_pairs={{0,8},{4,12},{8,0},{12,4},{1,9},{5,13},{9,1},{13,5},{2,10},{6,14},... | collective-permute-start | bytes 196616 | tf_op jit(solution)/shard_map/ppermute | solution.py:218
  48.8 6.4 %collective-permute-start.11 = (bf16[2,128,128]{2,1,0:T(8,128)(2,1)S(1)}, bf16[2,128,128]{2,1,0:T(8,128)(2,1)S(1)}, u32[]{:S(2)}, u32[]{:S(2)}) collective-permute-start(bf16[2,128,128]{2,1,0:T(8,128)(2,1)S(1)} %get-tuple-element.39), channel_id=1, source_target_pairs={{0,12},{4,8},{8,4},{12,0},{1,13},{5,9},{9,5},{13,1},{2,14},{6,10},... | collective-permute-start | bytes 196616 | tf_op jit(solution)/shard_map/ppermute | solution.py:218
  49.5 6.0 %collective-permute-start.12 = (bf16[2,128,128]{2,1,0:T(8,128)(2,1)S(1)}, bf16[2,128,128]{2,1,0:T(8,128)(2,1)S(1)}, u32[]{:S(2)}, u32[]{:S(2)}) collective-permute-start(bf16[2,128,128]{2,1,0:T(8,128)(2,1)S(1)} %get-tuple-element.40), channel_id=1, source_target_pairs={{0,4},{4,0},{8,12},{12,8},{1,5},{5,1},{9,13},{13,9},{2,6},{6,2},{1... | collective-permute-start | bytes 196616 | tf_op jit(solution)/shard_map/ppermute | solution.py:218

commit v6 on v5

--- a/solution.py
+++ b/solution.py
@@ -92,8 +92,11 @@
         if turn:
             for t in range(i // per, i // per + 2):
                 at = slice(t * LANES, (t + 1) * LANES)
-                wide[at, :] = fit_ref[:, at].astype(F32).T
-                tall_ref[at, :] = wide[at, :].astype(BF16)
+                y = fit_ref[:, at].astype(F32).T
+                tall_ref[at, :] = y.astype(BF16)
+                for h in range(per):
+                    r = (t * per + h) * (orbitals + 1)
+                    wide[r : r + orbitals, :] = y[h * orbitals : (h + 1) * orbitals]
         w = jnp.concatenate(
             [fit_ref[:, (i + per * g) * orbitals : (i + per * (g + 1)) * orbitals] for g in range(2)],
             axis=0,
@@ -115,7 +118,7 @@
     group = 2
     for m in range(0, orbitals, 2):
         if turn and m % per == 0:
-            x = [wide[pl.ds(m + h, orbitals, stride=orbitals), :] for h in range(per)]
+            x = [wide[pl.ds(m + h, orbitals, stride=orbitals + 1), :] for h in range(per)]
             at = slice(m * orbitals, (m + per) * orbitals)
             turned_ref[:, at] = jnp.concatenate(x, axis=0).T.astype(BF16)
         for n in range(pairs):
@@ -161,8 +164,8 @@
     return pl.pallas_call(
         functools.partial(energy_kernel, orbitals, turn),
         out_shape=[out_shape, *forms] if turn else out_shape,
-        scratch_shapes=scratch + [pltpu.VMEM((flat, aux), F32)] * turn,
-        compiler_params=pltpu.CompilerParams(vmem_limit_bytes=28 * MIB),
+        scratch_shapes=scratch + [pltpu.VMEM((orbitals * (orbitals + 1), aux), F32)] * turn,
+        compiler_params=pltpu.CompilerParams(vmem_limit_bytes=34 * MIB),
         name="self_energy",
     )(green, fit, *(() if turn else turned))
 

time: 56.3 us -> 55.9 us (level)
  Pallas kernels: 21.6 us -> 20.6 us
  starting transfers between devices: 13.2 us -> 14 us
    pallas_call x2, Pallas kernels: 17.7 us -> 16.7 us  [energy(): pl.pallas_call(functools.partial(energy_kernel, orbitals, turn), out_shap...]
    ppermute x13, starting transfers between devices: 13.2 us -> 14 us  [swap(): return lax.ppermute(x, axis, [(d, d ^ step) for d in range(size)])]
  transfers between devices with their start and end apart: 13 -> 13, of which waited for: 10 -> 10; matrix products, arithmetic and copies ran while one was open for 0% -> 0% of each run, Pallas kernels for 17% -> 15%
where the time goes in v6:
time: 55.9 us; the launch traced here: 55.7 us
  Pallas kernels  20.6 us (37%)
  waiting for transfers between devices  20.2 us (36%)
  starting transfers between devices  14 us (25%)
  other arithmetic  0.84 us (2%)
    ppermute x13, waiting for transfers between devices, swap(): return lax.ppermute(x, axis, [(d, d ^ step) for d in range(size)])  20.2 us
    pallas_call x2, Pallas kernels, energy(): pl.pallas_call(functools.partial(energy_kernel, orbitals, turn), out_shap...  16.7 us
    ppermute x13, starting transfers between devices, swap(): return lax.ppermute(x, axis, [(d, d ^ step) for d in range(size)])  14 us
    pallas_call x2, Pallas kernels, collide(): pl.pallas_call(functools.partial(collide_kernel, offsets, row_devices), g...  2.04 us
    pallas_call x1, Pallas kernels, split_history(): pl.pallas_call(split_kernel, out_shape=[jax.ShapeDtypeStruct(green.shape,...  1.86 us
  transfers between devices with their start and end apart: 13, of which 10 were waited for; matrix products, arithmetic and copies ran while one was open for 0% of the time, Pallas kernels for 15%

profile of v6, /device:TPU:0, one launch (start us, length us, event | category | flops | bytes accessed | tf_op | source)
XLA Modules:
  0.0 55.7 jit_solution(596251178261983347)
XLA Ops:
  0.0 0.0 copy-start
  0.0 0.1 pad_add_fusion.place_ref
  0.1 1.9 %split_history.1 = (f32[2,128,128]{2,1,0:T(8,128)S(1)}, bf16[1,2,512,128]{3,2,1,0:T(8,128)(2,1)S(1)}, bf16[1,2,512,128]{3,2,1,0:T(8,128)(2,1)S(1)}, bf16[2,2,512,128]{3,2,1,0:T(8,128)(2,1)S(1)}) custom-call(s32[2]{0:T(128)S(1)} %pad_add_fusion.place_ref, f32[2,128,128]{2,1,0:T(8,128)} %green_ref.1, bf16[2,512,512]{2,1,0:T(8,128)(2,1)} %history_ref.1), custom_call_target="tpu_custom_call" | custom-call | tf_op jit(solution)/shard_map/split_history/pallas_call | solution.py:55
  1.9 3.0 %collective-permute-start.1 = (bf16[2,2,512,128]{3,2,1,0:T(8,128)(2,1)S(1)}, bf16[2,2,512,128]{3,2,1,0:T(8,128)(2,1)S(1)}, u32[]{:S(2)}, u32[]{:S(2)}) collective-permute-start(bf16[2,2,512,128]{3,2,1,0:T(8,128)(2,1)S(1)} %get-tuple-element.26), channel_id=1, source_target_pairs={{0,2},{1,3},{2,0},{3,1},{4,6},{5,7},{6,4},{7,5},{8,10},{9,11},{10,... | collective-permute-start | bytes 1572872 | tf_op jit(solution)/shard_map/ppermute | solution.py:221
  5.0 0.0 copy-done
  5.0 8.6 %self_energy.2 = (bf16[2,128,128]{2,1,0:T(8,128)(2,1)S(1)}, bf16[128,4096]{1,0:T(8,128)(2,1)S(1)}, bf16[4096,128]{1,0:T(8,128)(2,1)S(1)}) custom-call(f32[2,128,128]{2,1,0:T(8,128)S(1)} %get-tuple-element.23.green_ref, bf16[128,4096]{1,0:T(8,128)(2,1)S(1)} %copy-done), custom_call_target="tpu_custom_call" | custom-call | tf_op jit(solution)/shard_map/self_energy/pallas_call | solution.py:164
  13.6 0.1 collective-permute-start
  13.7 0.1 collective-permute-start.3
  13.7 4.5 %collective-permute-done = bf16[1,2,128,128]{3,2,1,0:T(8,128)(2,1)S(1)} collective-permute-done((bf16[1,2,128,128]{3,2,1,0:T(8,128)(2,1)S(1)}, bf16[1,2,128,128]{3,2,1,0:T(8,128)(2,1)S(1)}, u32[]{:S(2)}, u32[]{:S(2)}) %collective-permute-start) | collective-permute-done | bytes 65568 | tf_op jit(solution)/shard_map/ppermute | solution.py:221
  18.3 0.0 collective-permute-done.1.refs_2_
  18.3 0.1 collective-permute-start.4
  18.4 0.6 collective-permute-start.2
  19.0 0.0 collective-permute-done.3.refs_1_
  19.0 1.1 %collective-permute-done.2.far_ref = bf16[2,2,128,128]{3,2,1,0:T(8,128)(2,1)S(1)} collective-permute-done((bf16[2,2,128,128]{3,2,1,0:T(8,128)(2,1)S(1)}, bf16[2,2,128,128]{3,2,1,0:T(8,128)(2,1)S(1)}, u32[]{:S(2)}, u32[]{:S(2)}) %collective-permute-start.2) | collective-permute-done | bytes 131104 | tf_op jit(solution)/shard_map/ppermute | solution.py:221
  20.1 0.0 collective-permute-done.4.refs_3_
  20.1 1.0 %collide.2 = (f32[2,128,128]{2,1,0:T(8,128)S(1)}, bf16[2,128,128]{2,1,0:T(8,128)(2,1)S(1)}, bf16[2,128,128]{2,1,0:T(8,128)(2,1)S(1)}, bf16[2,128,128]{2,1,0:T(8,128)(2,1)S(1)}) custom-call(s32[2]{0:T(128)S(1)} %pad_add_fusion.place_ref, bf16[2,2,128,128]{3,2,1,0:T(8,128)(2,1)S(1)} %pad_maximum_fusion.near_ref, ...), custom_call_target="tpu_custom_call" | custom-call | tf_op jit(solution)/shard_map/collide/pallas_call | solution.py:205
  21.1 2.9 %collective-permute-start.5 = (bf16[2,128,128]{2,1,0:T(8,128)(2,1)S(1)}, bf16[2,128,128]{2,1,0:T(8,128)(2,1)S(1)}, u32[]{:S(2)}, u32[]{:S(2)}) collective-permute-start(bf16[2,128,128]{2,1,0:T(8,128)(2,1)S(1)} %get-tuple-element.32), channel_id=1, source_target_pairs={{0,8},{4,12},{8,0},{12,4},{1,9},{5,13},{9,1},{13,5},{2,10},{6,14},... | collective-permute-start | bytes 196616 | tf_op jit(solution)/shard_map/ppermute | solution.py:221
  24.0 1.3 %collective-permute-start.6 = (bf16[2,128,128]{2,1,0:T(8,128)(2,1)S(1)}, bf16[2,128,128]{2,1,0:T(8,128)(2,1)S(1)}, u32[]{:S(2)}, u32[]{:S(2)}) collective-permute-start(bf16[2,128,128]{2,1,0:T(8,128)(2,1)S(1)} %get-tuple-element.33), channel_id=1, source_target_pairs={{0,12},{4,8},{8,4},{12,0},{1,13},{5,9},{9,5},{13,1},{2,14},{6,10},... | collective-permute-start | bytes 196616 | tf_op jit(solution)/shard_map/ppermute | solution.py:221
  25.4 0.2 collective-permute-start.7
  25.6 2.5 %collective-permute-done.5 = bf16[2,128,128]{2,1,0:T(8,128)(2,1)S(1)} collective-permute-done((bf16[2,128,128]{2,1,0:T(8,128)(2,1)S(1)}, bf16[2,128,128]{2,1,0:T(8,128)(2,1)S(1)}, u32[]{:S(2)}, u32[]{:S(2)}) %collective-permute-start.5) | collective-permute-done | bytes 65568 | tf_op jit(solution)/shard_map/ppermute | solution.py:221
  28.1 2.4 %collective-permute-done.6 = bf16[2,128,128]{2,1,0:T(8,128)(2,1)S(1)} collective-permute-done((bf16[2,128,128]{2,1,0:T(8,128)(2,1)S(1)}, bf16[2,128,128]{2,1,0:T(8,128)(2,1)S(1)}, u32[]{:S(2)}, u32[]{:S(2)}) %collective-permute-start.6) | collective-permute-done | bytes 65568 | tf_op jit(solution)/shard_map/ppermute | solution.py:221
  30.5 0.2 collective-permute-done.7
  30.8 8.1 %self_energy.3 = bf16[2,128,128]{2,1,0:T(8,128)(2,1)S(1)} custom-call(f32[2,128,128]{2,1,0:T(8,128)S(1)} %convert_add_fusion.1.green_ref, bf16[128,4096]{1,0:T(8,128)(2,1)S(1)} %copy-done, bf16[128,4096]{1,0:T(8,128)(2,1)S(1)} %get-tuple-element.35.refs_0_, bf16[4096,128]{1,0:T(8,128)(2,1)S(1)} %get-tuple-element.36.refs_1_), custom_call_target="tpu_custom_call" | custom-call | tf_op jit(solution)/shard_map/self_energy/pallas_call | solution.py:164
  38.8 1.7 %collective-permute-start.8 = (bf16[1,2,128,128]{3,2,1,0:T(8,128)(2,1)S(1)}, bf16[1,2,128,128]{3,2,1,0:T(8,128)(2,1)S(1)}, u32[]{:S(2)}, u32[]{:S(2)}) collective-permute-start(bf16[1,2,128,128]{3,2,1,0:T(8,128)(2,1)S(1)} %bitcast.4), channel_id=1, source_target_pairs={{0,2},{1,3},{2,0},{3,1},{4,6},{5,7},{6,4},{7,5},{8,10},{9,11},{10,... | collective-permute-start | bytes 196616 | tf_op jit(solution)/shard_map/ppermute | solution.py:221
  40.5 2.7 %collective-permute-done.8 = bf16[1,2,128,128]{3,2,1,0:T(8,128)(2,1)S(1)} collective-permute-done((bf16[1,2,128,128]{3,2,1,0:T(8,128)(2,1)S(1)}, bf16[1,2,128,128]{3,2,1,0:T(8,128)(2,1)S(1)}, u32[]{:S(2)}, u32[]{:S(2)}) %collective-permute-start.8) | collective-permute-done | bytes 65568 | tf_op jit(solution)/shard_map/ppermute | solution.py:221
  43.2 0.1 collective-permute-start.9
  43.2 1.3 %collective-permute-done.9.far_ref = bf16[2,2,128,128]{3,2,1,0:T(8,128)(2,1)S(1)} collective-permute-done((bf16[2,2,128,128]{3,2,1,0:T(8,128)(2,1)S(1)}, bf16[2,2,128,128]{3,2,1,0:T(8,128)(2,1)S(1)}, u32[]{:S(2)}, u32[]{:S(2)}) %collective-permute-start.9) | collective-permute-done | bytes 131104 | tf_op jit(solution)/shard_map/ppermute | solution.py:221
  44.6 1.0 %collide.3 = (f32[2,128,128]{2,1,0:T(8,128)S(1)}, bf16[2,128,128]{2,1,0:T(8,128)(2,1)S(1)}, bf16[2,128,128]{2,1,0:T(8,128)(2,1)S(1)}, bf16[2,128,128]{2,1,0:T(8,128)(2,1)S(1)}) custom-call(s32[2]{0:T(128)S(1)} %pad_add_fusion.place_ref, bf16[2,2,128,128]{3,2,1,0:T(8,128)(2,1)S(1)} %pad_maximum_fusion.1.near_ref, ...), custom_call_target="tpu_custom_call" | custom-call | tf_op jit(solution)/shard_map/collide/pallas_call | solution.py:205
  45.6 2.8 %collective-permute-start.10 = (bf16[2,128,128]{2,1,0:T(8,128)(2,1)S(1)}, bf16[2,128,128]{2,1,0:T(8,128)(2,1)S(1)}, u32[]{:S(2)}, u32[]{:S(2)}) collective-permute-start(bf16[2,128,128]{2,1,0:T(8,128)(2,1)S(1)} %get-tuple-element.38), channel_id=1, source_target_pairs={{0,8},{4,12},{8,0},{12,4},{1,9},{5,13},{9,1},{13,5},{2,10},{6,14},... | collective-permute-start | bytes 196616 | tf_op jit(solution)/shard_map/ppermute | solution.py:221
  48.4 0.7 %collective-permute-start.11 = (bf16[2,128,128]{2,1,0:T(8,128)(2,1)S(1)}, bf16[2,128,128]{2,1,0:T(8,128)(2,1)S(1)}, u32[]{:S(2)}, u32[]{:S(2)}) collective-permute-start(bf16[2,128,128]{2,1,0:T(8,128)(2,1)S(1)} %get-tuple-element.39), channel_id=1, source_target_pairs={{0,12},{4,8},{8,4},{12,0},{1,13},{5,9},{9,5},{13,1},{2,14},{6,10},... | collective-permute-start | bytes 196616 | tf_op jit(solution)/shard_map/ppermute | solution.py:221
  49.1 0.5 collective-permute-start.12
  49.6 4.0 %collective-permute-done.10 = bf16[2,128,128]{2,1,0:T(8,128)(2,1)S(1)} collective-permute-done((bf16[2,128,128]{2,1,0:T(8,128)(2,1)S(1)}, bf16[2,128,128]{2,1,0:T(8,128)(2,1)S(1)}, u32[]{:S(2)}, u32[]{:S(2)}) %collective-permute-start.10) | collective-permute-done | bytes 65568 | tf_op jit(solution)/shard_map/ppermute | solution.py:221
  53.6 1.2 %collective-permute-done.11 = bf16[2,128,128]{2,1,0:T(8,128)(2,1)S(1)} collective-permute-done((bf16[2,128,128]{2,1,0:T(8,128)(2,1)S(1)}, bf16[2,128,128]{2,1,0:T(8,128)(2,1)S(1)}, u32[]{:S(2)}, u32[]{:S(2)}) %collective-permute-start.11) | collective-permute-done | bytes 65568 | tf_op jit(solution)/shard_map/ppermute | solution.py:221
  54.8 0.2 collective-permute-done.12
  55.0 0.7 %convert_add_fusion = f32[2,128,128]{2,1,0:T(8,128)} fusion(bf16[2,128,128]{2,1,0:T(8,128)(2,1)S(1)} %collective-permute-done.12, bf16[2,128,128]{2,1,0:T(8,128)(2,1)S(1)} %collective-permute-done.11, bf16[2,128,128]{2,1,0:T(8,128)(2,1)S(1)} %collective-permute-done.10, f32[2,128,128]{2,1,0:T(8,128)S(1)} %get-tuple-element.23.green_ref, ...), kind=kLoop, calls=%fused_computation.2 | loop fusion | flops 229376 | bytes 589824 | tf_op jit(solution)/shard_map/add | solution.py:266
  (4 shorter events, 0.1 us)
Async XLA Ops:
  0.0 5.0 %copy-start = (bf16[128,4096]{1,0:T(8,128)(2,1)S(1)}, bf16[128,4096]{1,0:T(8,128)(2,1)}, u32[]{:S(2)}) copy-start(bf16[128,4096]{1,0:T(8,128)(2,1)} %fit_ref.3) | copy-start | bytes 3145732
  1.9 16.3 %collective-permute-start.1 = (bf16[2,2,512,128]{3,2,1,0:T(8,128)(2,1)S(1)}, bf16[2,2,512,128]{3,2,1,0:T(8,128)(2,1)S(1)}, u32[]{:S(2)}, u32[]{:S(2)}) collective-permute-start(bf16[2,2,512,128]{3,2,1,0:T(8,128)(2,1)S(1)} %get-tuple-element.26), channel_id=1, source_target_pairs={{0,2},{1,3},{2,0},{3,1},{4,6},{5,7},{6,4},{7,5},{8,10},{9,11},{10,... | collective-permute-start | bytes 1572872 | tf_op jit(solution)/shard_map/ppermute | solution.py:221
  13.6 4.7 %collective-permute-start = (bf16[1,2,128,128]{3,2,1,0:T(8,128)(2,1)S(1)}, bf16[1,2,128,128]{3,2,1,0:T(8,128)(2,1)S(1)}, u32[]{:S(2)}, u32[]{:S(2)}) collective-permute-start(bf16[1,2,128,128]{3,2,1,0:T(8,128)(2,1)S(1)} %bitcast.6), channel_id=1, source_target_pairs={{0,2},{1,3},{2,0},{3,1},{4,6},{5,7},{6,4},{7,5},{8,10},{9,11},{10,... | collective-permute-start | bytes 196616 | tf_op jit(solution)/shard_map/ppermute | solution.py:221
  13.7 5.3 %collective-permute-start.3 = (bf16[1,2,512,128]{3,2,1,0:T(8,128)(2,1)S(1)}, bf16[1,2,512,128]{3,2,1,0:T(8,128)(2,1)S(1)}, u32[]{:S(2)}, u32[]{:S(2)}) collective-permute-start(bf16[1,2,512,128]{3,2,1,0:T(8,128)(2,1)S(1)} %get-tuple-element.29), channel_id=1, source_target_pairs={{0,1},{1,0},{2,3},{3,2},{4,5},{5,4},{6,7},{7,6},{8,9},{9,8},{10,11... | collective-permute-start | bytes 786440 | tf_op jit(solution)/shard_map/ppermute | solution.py:221
  18.3 1.8 %collective-permute-start.4 = (bf16[1,2,512,128]{3,2,1,0:T(8,128)(2,1)S(1)}, bf16[1,2,512,128]{3,2,1,0:T(8,128)(2,1)S(1)}, u32[]{:S(2)}, u32[]{:S(2)}) collective-permute-start(bf16[1,2,512,128]{3,2,1,0:T(8,128)(2,1)S(1)} %slice.3), channel_id=1, source_target_pairs={{0,1},{1,0},{2,3},{3,2},{4,5},{5,4},{6,7},{7,6},{8,9},{9,8},{10,11... | collective-permute-start | bytes 786440 | tf_op jit(solution)/shard_map/ppermute | solution.py:221
  18.4 1.7 %collective-permute-start.2 = (bf16[2,2,128,128]{3,2,1,0:T(8,128)(2,1)S(1)}, bf16[2,2,128,128]{3,2,1,0:T(8,128)(2,1)S(1)}, u32[]{:S(2)}, u32[]{:S(2)}) collective-permute-start(bf16[2,2,128,128]{3,2,1,0:T(8,128)(2,1)S(1)} %pad_maximum_fusion.near_ref), channel_id=1, source_target_pairs={{0,1},{1,0},{2,3},{3,2},{4,5},{5,4},{6,7},{7,6},{8,9},{9,8},{10,11... | collective-permute-start | bytes 393224 | tf_op jit(solution)/shard_map/ppermute | solution.py:221
  21.1 7.0 %collective-permute-start.5 = (bf16[2,128,128]{2,1,0:T(8,128)(2,1)S(1)}, bf16[2,128,128]{2,1,0:T(8,128)(2,1)S(1)}, u32[]{:S(2)}, u32[]{:S(2)}) collective-permute-start(bf16[2,128,128]{2,1,0:T(8,128)(2,1)S(1)} %get-tuple-element.32), channel_id=1, source_target_pairs={{0,8},{4,12},{8,0},{12,4},{1,9},{5,13},{9,1},{13,5},{2,10},{6,14},... | collective-permute-start | bytes 196616 | tf_op jit(solution)/shard_map/ppermute | solution.py:221
  24.0 6.5 %collective-permute-start.6 = (bf16[2,128,128]{2,1,0:T(8,128)(2,1)S(1)}, bf16[2,128,128]{2,1,0:T(8,128)(2,1)S(1)}, u32[]{:S(2)}, u32[]{:S(2)}) collective-permute-start(bf16[2,128,128]{2,1,0:T(8,128)(2,1)S(1)} %get-tuple-element.33), channel_id=1, source_target_pairs={{0,12},{4,8},{8,4},{12,0},{1,13},{5,9},{9,5},{13,1},{2,14},{6,10},... | collective-permute-start | bytes 196616 | tf_op jit(solution)/shard_map/ppermute | solution.py:221
  25.4 5.3 %collective-permute-start.7 = (bf16[2,128,128]{2,1,0:T(8,128)(2,1)S(1)}, bf16[2,128,128]{2,1,0:T(8,128)(2,1)S(1)}, u32[]{:S(2)}, u32[]{:S(2)}) collective-permute-start(bf16[2,128,128]{2,1,0:T(8,128)(2,1)S(1)} %get-tuple-element.34), channel_id=1, source_target_pairs={{0,4},{4,0},{8,12},{12,8},{1,5},{5,1},{9,13},{13,9},{2,6},{6,2},{1... | collective-permute-start | bytes 196616 | tf_op jit(solution)/shard_map/ppermute | solution.py:221
  38.8 4.3 %collective-permute-start.8 = (bf16[1,2,128,128]{3,2,1,0:T(8,128)(2,1)S(1)}, bf16[1,2,128,128]{3,2,1,0:T(8,128)(2,1)S(1)}, u32[]{:S(2)}, u32[]{:S(2)}) collective-permute-start(bf16[1,2,128,128]{3,2,1,0:T(8,128)(2,1)S(1)} %bitcast.4), channel_id=1, source_target_pairs={{0,2},{1,3},{2,0},{3,1},{4,6},{5,7},{6,4},{7,5},{8,10},{9,11},{10,... | collective-permute-start | bytes 196616 | tf_op jit(solution)/shard_map/ppermute | solution.py:221
  43.2 1.4 %collective-permute-start.9 = (bf16[2,2,128,128]{3,2,1,0:T(8,128)(2,1)S(1)}, bf16[2,2,128,128]{3,2,1,0:T(8,128)(2,1)S(1)}, u32[]{:S(2)}, u32[]{:S(2)}) collective-permute-start(bf16[2,2,128,128]{3,2,1,0:T(8,128)(2,1)S(1)} %pad_maximum_fusion.1.near_ref), channel_id=1, source_target_pairs={{0,1},{1,0},{2,3},{3,2},{4,5},{5,4},{6,7},{7,6},{8,9},{9,8},{10,11... | collective-permute-start | bytes 393224 | tf_op jit(solution)/shard_map/ppermute | solution.py:221
  45.6 8.0 %collective-permute-start.10 = (bf16[2,128,128]{2,1,0:T(8,128)(2,1)S(1)}, bf16[2,128,128]{2,1,0:T(8,128)(2,1)S(1)}, u32[]{:S(2)}, u32[]{:S(2)}) collective-permute-start(bf16[2,128,128]{2,1,0:T(8,128)(2,1)S(1)} %get-tuple-element.38), channel_id=1, source_target_pairs={{0,8},{4,12},{8,0},{12,4},{1,9},{5,13},{9,1},{13,5},{2,10},{6,14},... | collective-permute-start | bytes 196616 | tf_op jit(solution)/shard_map/ppermute | solution.py:221
  48.4 6.4 %collective-permute-start.11 = (bf16[2,128,128]{2,1,0:T(8,128)(2,1)S(1)}, bf16[2,128,128]{2,1,0:T(8,128)(2,1)S(1)}, u32[]{:S(2)}, u32[]{:S(2)}) collective-permute-start(bf16[2,128,128]{2,1,0:T(8,128)(2,1)S(1)} %get-tuple-element.39), channel_id=1, source_target_pairs={{0,12},{4,8},{8,4},{12,0},{1,13},{5,9},{9,5},{13,1},{2,14},{6,10},... | collective-permute-start | bytes 196616 | tf_op jit(solution)/shard_map/ppermute | solution.py:221
  49.1 5.9 %collective-permute-start.12 = (bf16[2,128,128]{2,1,0:T(8,128)(2,1)S(1)}, bf16[2,128,128]{2,1,0:T(8,128)(2,1)S(1)}, u32[]{:S(2)}, u32[]{:S(2)}) collective-permute-start(bf16[2,128,128]{2,1,0:T(8,128)(2,1)S(1)} %get-tuple-element.40), channel_id=1, source_target_pairs={{0,4},{4,0},{8,12},{12,8},{1,5},{5,1},{9,13},{13,9},{2,6},{6,2},{1... | collective-permute-start | bytes 196616 | tf_op jit(solution)/shard_map/ppermute | solution.py:221

commit v7 on v6

--- a/solution.py
+++ b/solution.py
@@ -158,13 +158,13 @@
     out_shape = jax.ShapeDtypeStruct((2, rows, span), BF16)
     forms = [jax.ShapeDtypeStruct((aux, flat), BF16), jax.ShapeDtypeStruct((flat, aux), BF16)]
     scratch = [
-        pltpu.VMEM((pairs, orbitals * (2 * orbitals + 1), aux), F32),
+        pltpu.VMEM((pairs, (orbitals + 1) * (2 * orbitals + 1), aux), F32),
         pltpu.VMEM((flat, pairs * aux), BF16),
     ]
     return pl.pallas_call(
         functools.partial(energy_kernel, orbitals, turn),
         out_shape=[out_shape, *forms] if turn else out_shape,
-        scratch_shapes=scratch + [pltpu.VMEM((orbitals * (orbitals + 1), aux), F32)] * turn,
+        scratch_shapes=scratch + [pltpu.VMEM((orbitals * (orbitals + 2), aux), F32)] * turn,
         compiler_params=pltpu.CompilerParams(vmem_limit_bytes=34 * MIB),
         name="self_energy",
     )(green, fit, *(() if turn else turned))

time: 55.9 us -> 55.9 us (level)
  no operation moved by 1% of the time
where the time goes in v7:
time: 55.9 us; the launch traced here: 55.7 us
  Pallas kernels  20.6 us (37%)
  waiting for transfers between devices  20.2 us (36%)
  starting transfers between devices  14 us (25%)
  other arithmetic  0.84 us (2%)
    ppermute x13, waiting for transfers between devices, swap(): return lax.ppermute(x, axis, [(d, d ^ step) for d in range(size)])  20.2 us
    pallas_call x2, Pallas kernels, energy(): pl.pallas_call(functools.partial(energy_kernel, orbitals, turn), out_shap...  16.7 us
    ppermute x13, starting transfers between devices, swap(): return lax.ppermute(x, axis, [(d, d ^ step) for d in range(size)])  14 us
    pallas_call x2, Pallas kernels, collide(): pl.pallas_call(functools.partial(collide_kernel, offsets, row_devices), g...  2.04 us
    pallas_call x1, Pallas kernels, split_history(): pl.pallas_call(split_kernel, out_shape=[jax.ShapeDtypeStruct(green.shape,...  1.86 us
  transfers between devices with their start and end apart: 13, of which 10 were waited for; matrix products, arithmetic and copies ran while one was open for 0% of the time, Pallas kernels for 15%

profile of v7, /device:TPU:0, one launch (start us, length us, event | category | flops | bytes accessed | tf_op | source)
XLA Modules:
  0.0 55.7 jit_solution(8611352783435057769)
XLA Ops:
  0.0 0.0 copy-start
  0.0 0.1 pad_add_fusion.place_ref
  0.1 1.9 %split_history.1 = (f32[2,128,128]{2,1,0:T(8,128)S(1)}, bf16[1,2,512,128]{3,2,1,0:T(8,128)(2,1)S(1)}, bf16[1,2,512,128]{3,2,1,0:T(8,128)(2,1)S(1)}, bf16[2,2,512,128]{3,2,1,0:T(8,128)(2,1)S(1)}) custom-call(s32[2]{0:T(128)S(1)} %pad_add_fusion.place_ref, f32[2,128,128]{2,1,0:T(8,128)} %green_ref.1, bf16[2,512,512]{2,1,0:T(8,128)(2,1)} %history_ref.1), custom_call_target="tpu_custom_call" | custom-call | tf_op jit(solution)/shard_map/split_history/pallas_call | solution.py:55
  1.9 3.0 %collective-permute-start.1 = (bf16[2,2,512,128]{3,2,1,0:T(8,128)(2,1)S(1)}, bf16[2,2,512,128]{3,2,1,0:T(8,128)(2,1)S(1)}, u32[]{:S(2)}, u32[]{:S(2)}) collective-permute-start(bf16[2,2,512,128]{3,2,1,0:T(8,128)(2,1)S(1)} %get-tuple-element.26), channel_id=1, source_target_pairs={{0,2},{1,3},{2,0},{3,1},{4,6},{5,7},{6,4},{7,5},{8,10},{9,11},{10,... | collective-permute-start | bytes 1572872 | tf_op jit(solution)/shard_map/ppermute | solution.py:221
  5.0 0.0 copy-done
  5.0 8.6 %self_energy.2 = (bf16[2,128,128]{2,1,0:T(8,128)(2,1)S(1)}, bf16[128,4096]{1,0:T(8,128)(2,1)S(1)}, bf16[4096,128]{1,0:T(8,128)(2,1)S(1)}) custom-call(f32[2,128,128]{2,1,0:T(8,128)S(1)} %get-tuple-element.23.green_ref, bf16[128,4096]{1,0:T(8,128)(2,1)S(1)} %copy-done), custom_call_target="tpu_custom_call" | custom-call | tf_op jit(solution)/shard_map/self_energy/pallas_call | solution.py:164
  13.6 0.1 collective-permute-start
  13.7 0.1 collective-permute-start.3
  13.7 4.5 %collective-permute-done = bf16[1,2,128,128]{3,2,1,0:T(8,128)(2,1)S(1)} collective-permute-done((bf16[1,2,128,128]{3,2,1,0:T(8,128)(2,1)S(1)}, bf16[1,2,128,128]{3,2,1,0:T(8,128)(2,1)S(1)}, u32[]{:S(2)}, u32[]{:S(2)}) %collective-permute-start) | collective-permute-done | bytes 65568 | tf_op jit(solution)/shard_map/ppermute | solution.py:221
  18.3 0.0 collective-permute-done.1.refs_2_
  18.3 0.1 collective-permute-start.4
  18.4 0.6 collective-permute-start.2
  19.0 0.0 collective-permute-done.3.refs_1_
  19.0 1.1 %collective-permute-done.2.far_ref = bf16[2,2,128,128]{3,2,1,0:T(8,128)(2,1)S(1)} collective-permute-done((bf16[2,2,128,128]{3,2,1,0:T(8,128)(2,1)S(1)}, bf16[2,2,128,128]{3,2,1,0:T(8,128)(2,1)S(1)}, u32[]{:S(2)}, u32[]{:S(2)}) %collective-permute-start.2) | collective-permute-done | bytes 131104 | tf_op jit(solution)/shard_map/ppermute | solution.py:221
  20.1 0.0 collective-permute-done.4.refs_3_
  20.1 1.0 %collide.2 = (f32[2,128,128]{2,1,0:T(8,128)S(1)}, bf16[2,128,128]{2,1,0:T(8,128)(2,1)S(1)}, bf16[2,128,128]{2,1,0:T(8,128)(2,1)S(1)}, bf16[2,128,128]{2,1,0:T(8,128)(2,1)S(1)}) custom-call(s32[2]{0:T(128)S(1)} %pad_add_fusion.place_ref, bf16[2,2,128,128]{3,2,1,0:T(8,128)(2,1)S(1)} %pad_maximum_fusion.near_ref, ...), custom_call_target="tpu_custom_call" | custom-call | tf_op jit(solution)/shard_map/collide/pallas_call | solution.py:205
  21.1 2.9 %collective-permute-start.5 = (bf16[2,128,128]{2,1,0:T(8,128)(2,1)S(1)}, bf16[2,128,128]{2,1,0:T(8,128)(2,1)S(1)}, u32[]{:S(2)}, u32[]{:S(2)}) collective-permute-start(bf16[2,128,128]{2,1,0:T(8,128)(2,1)S(1)} %get-tuple-element.32), channel_id=1, source_target_pairs={{0,8},{4,12},{8,0},{12,4},{1,9},{5,13},{9,1},{13,5},{2,10},{6,14},... | collective-permute-start | bytes 196616 | tf_op jit(solution)/shard_map/ppermute | solution.py:221
  24.0 1.3 %collective-permute-start.6 = (bf16[2,128,128]{2,1,0:T(8,128)(2,1)S(1)}, bf16[2,128,128]{2,1,0:T(8,128)(2,1)S(1)}, u32[]{:S(2)}, u32[]{:S(2)}) collective-permute-start(bf16[2,128,128]{2,1,0:T(8,128)(2,1)S(1)} %get-tuple-element.33), channel_id=1, source_target_pairs={{0,12},{4,8},{8,4},{12,0},{1,13},{5,9},{9,5},{13,1},{2,14},{6,10},... | collective-permute-start | bytes 196616 | tf_op jit(solution)/shard_map/ppermute | solution.py:221
  25.4 0.2 collective-permute-start.7
  25.6 2.5 %collective-permute-done.5 = bf16[2,128,128]{2,1,0:T(8,128)(2,1)S(1)} collective-permute-done((bf16[2,128,128]{2,1,0:T(8,128)(2,1)S(1)}, bf16[2,128,128]{2,1,0:T(8,128)(2,1)S(1)}, u32[]{:S(2)}, u32[]{:S(2)}) %collective-permute-start.5) | collective-permute-done | bytes 65568 | tf_op jit(solution)/shard_map/ppermute | solution.py:221
  28.1 2.4 %collective-permute-done.6 = bf16[2,128,128]{2,1,0:T(8,128)(2,1)S(1)} collective-permute-done((bf16[2,128,128]{2,1,0:T(8,128)(2,1)S(1)}, bf16[2,128,128]{2,1,0:T(8,128)(2,1)S(1)}, u32[]{:S(2)}, u32[]{:S(2)}) %collective-permute-start.6) | collective-permute-done | bytes 65568 | tf_op jit(solution)/shard_map/ppermute | solution.py:221
  30.5 0.2 collective-permute-done.7
  30.8 8.1 %self_energy.3 = bf16[2,128,128]{2,1,0:T(8,128)(2,1)S(1)} custom-call(f32[2,128,128]{2,1,0:T(8,128)S(1)} %convert_add_fusion.1.green_ref, bf16[128,4096]{1,0:T(8,128)(2,1)S(1)} %copy-done, bf16[128,4096]{1,0:T(8,128)(2,1)S(1)} %get-tuple-element.35.refs_0_, bf16[4096,128]{1,0:T(8,128)(2,1)S(1)} %get-tuple-element.36.refs_1_), custom_call_target="tpu_custom_call" | custom-call | tf_op jit(solution)/shard_map/self_energy/pallas_call | solution.py:164
  38.8 1.7 %collective-permute-start.8 = (bf16[1,2,128,128]{3,2,1,0:T(8,128)(2,1)S(1)}, bf16[1,2,128,128]{3,2,1,0:T(8,128)(2,1)S(1)}, u32[]{:S(2)}, u32[]{:S(2)}) collective-permute-start(bf16[1,2,128,128]{3,2,1,0:T(8,128)(2,1)S(1)} %bitcast.4), channel_id=1, source_target_pairs={{0,2},{1,3},{2,0},{3,1},{4,6},{5,7},{6,4},{7,5},{8,10},{9,11},{10,... | collective-permute-start | bytes 196616 | tf_op jit(solution)/shard_map/ppermute | solution.py:221
  40.5 2.7 %collective-permute-done.8 = bf16[1,2,128,128]{3,2,1,0:T(8,128)(2,1)S(1)} collective-permute-done((bf16[1,2,128,128]{3,2,1,0:T(8,128)(2,1)S(1)}, bf16[1,2,128,128]{3,2,1,0:T(8,128)(2,1)S(1)}, u32[]{:S(2)}, u32[]{:S(2)}) %collective-permute-start.8) | collective-permute-done | bytes 65568 | tf_op jit(solution)/shard_map/ppermute | solution.py:221
  43.2 0.1 collective-permute-start.9
  43.2 1.3 %collective-permute-done.9.far_ref = bf16[2,2,128,128]{3,2,1,0:T(8,128)(2,1)S(1)} collective-permute-done((bf16[2,2,128,128]{3,2,1,0:T(8,128)(2,1)S(1)}, bf16[2,2,128,128]{3,2,1,0:T(8,128)(2,1)S(1)}, u32[]{:S(2)}, u32[]{:S(2)}) %collective-permute-start.9) | collective-permute-done | bytes 131104 | tf_op jit(solution)/shard_map/ppermute | solution.py:221
  44.6 1.0 %collide.3 = (f32[2,128,128]{2,1,0:T(8,128)S(1)}, bf16[2,128,128]{2,1,0:T(8,128)(2,1)S(1)}, bf16[2,128,128]{2,1,0:T(8,128)(2,1)S(1)}, bf16[2,128,128]{2,1,0:T(8,128)(2,1)S(1)}) custom-call(s32[2]{0:T(128)S(1)} %pad_add_fusion.place_ref, bf16[2,2,128,128]{3,2,1,0:T(8,128)(2,1)S(1)} %pad_maximum_fusion.1.near_ref, ...), custom_call_target="tpu_custom_call" | custom-call | tf_op jit(solution)/shard_map/collide/pallas_call | solution.py:205
  45.6 2.8 %collective-permute-start.10 = (bf16[2,128,128]{2,1,0:T(8,128)(2,1)S(1)}, bf16[2,128,128]{2,1,0:T(8,128)(2,1)S(1)}, u32[]{:S(2)}, u32[]{:S(2)}) collective-permute-start(bf16[2,128,128]{2,1,0:T(8,128)(2,1)S(1)} %get-tuple-element.38), channel_id=1, source_target_pairs={{0,8},{4,12},{8,0},{12,4},{1,9},{5,13},{9,1},{13,5},{2,10},{6,14},... | collective-permute-start | bytes 196616 | tf_op jit(solution)/shard_map/ppermute | solution.py:221
  48.4 0.7 %collective-permute-start.11 = (bf16[2,128,128]{2,1,0:T(8,128)(2,1)S(1)}, bf16[2,128,128]{2,1,0:T(8,128)(2,1)S(1)}, u32[]{:S(2)}, u32[]{:S(2)}) collective-permute-start(bf16[2,128,128]{2,1,0:T(8,128)(2,1)S(1)} %get-tuple-element.39), channel_id=1, source_target_pairs={{0,12},{4,8},{8,4},{12,0},{1,13},{5,9},{9,5},{13,1},{2,14},{6,10},... | collective-permute-start | bytes 196616 | tf_op jit(solution)/shard_map/ppermute | solution.py:221
  49.1 0.5 collective-permute-start.12
  49.6 4.0 %collective-permute-done.10 = bf16[2,128,128]{2,1,0:T(8,128)(2,1)S(1)} collective-permute-done((bf16[2,128,128]{2,1,0:T(8,128)(2,1)S(1)}, bf16[2,128,128]{2,1,0:T(8,128)(2,1)S(1)}, u32[]{:S(2)}, u32[]{:S(2)}) %collective-permute-start.10) | collective-permute-done | bytes 65568 | tf_op jit(solution)/shard_map/ppermute | solution.py:221
  53.6 1.2 %collective-permute-done.11 = bf16[2,128,128]{2,1,0:T(8,128)(2,1)S(1)} collective-permute-done((bf16[2,128,128]{2,1,0:T(8,128)(2,1)S(1)}, bf16[2,128,128]{2,1,0:T(8,128)(2,1)S(1)}, u32[]{:S(2)}, u32[]{:S(2)}) %collective-permute-start.11) | collective-permute-done | bytes 65568 | tf_op jit(solution)/shard_map/ppermute | solution.py:221
  54.8 0.2 collective-permute-done.12
  55.0 0.7 %convert_add_fusion = f32[2,128,128]{2,1,0:T(8,128)} fusion(bf16[2,128,128]{2,1,0:T(8,128)(2,1)S(1)} %collective-permute-done.12, bf16[2,128,128]{2,1,0:T(8,128)(2,1)S(1)} %collective-permute-done.11, bf16[2,128,128]{2,1,0:T(8,128)(2,1)S(1)} %collective-permute-done.10, f32[2,128,128]{2,1,0:T(8,128)S(1)} %get-tuple-element.23.green_ref, ...), kind=kLoop, calls=%fused_computation.2 | loop fusion | flops 229376 | bytes 589824 | tf_op jit(solution)/shard_map/add | solution.py:266
  (4 shorter events, 0.1 us)
Async XLA Ops:
  0.0 5.0 %copy-start = (bf16[128,4096]{1,0:T(8,128)(2,1)S(1)}, bf16[128,4096]{1,0:T(8,128)(2,1)}, u32[]{:S(2)}) copy-start(bf16[128,4096]{1,0:T(8,128)(2,1)} %fit_ref.3) | copy-start | bytes 3145732
  1.9 16.3 %collective-permute-start.1 = (bf16[2,2,512,128]{3,2,1,0:T(8,128)(2,1)S(1)}, bf16[2,2,512,128]{3,2,1,0:T(8,128)(2,1)S(1)}, u32[]{:S(2)}, u32[]{:S(2)}) collective-permute-start(bf16[2,2,512,128]{3,2,1,0:T(8,128)(2,1)S(1)} %get-tuple-element.26), channel_id=1, source_target_pairs={{0,2},{1,3},{2,0},{3,1},{4,6},{5,7},{6,4},{7,5},{8,10},{9,11},{10,... | collective-permute-start | bytes 1572872 | tf_op jit(solution)/shard_map/ppermute | solution.py:221
  13.6 4.7 %collective-permute-start = (bf16[1,2,128,128]{3,2,1,0:T(8,128)(2,1)S(1)}, bf16[1,2,128,128]{3,2,1,0:T(8,128)(2,1)S(1)}, u32[]{:S(2)}, u32[]{:S(2)}) collective-permute-start(bf16[1,2,128,128]{3,2,1,0:T(8,128)(2,1)S(1)} %bitcast.6), channel_id=1, source_target_pairs={{0,2},{1,3},{2,0},{3,1},{4,6},{5,7},{6,4},{7,5},{8,10},{9,11},{10,... | collective-permute-start | bytes 196616 | tf_op jit(solution)/shard_map/ppermute | solution.py:221
  13.7 5.3 %collective-permute-start.3 = (bf16[1,2,512,128]{3,2,1,0:T(8,128)(2,1)S(1)}, bf16[1,2,512,128]{3,2,1,0:T(8,128)(2,1)S(1)}, u32[]{:S(2)}, u32[]{:S(2)}) collective-permute-start(bf16[1,2,512,128]{3,2,1,0:T(8,128)(2,1)S(1)} %get-tuple-element.29), channel_id=1, source_target_pairs={{0,1},{1,0},{2,3},{3,2},{4,5},{5,4},{6,7},{7,6},{8,9},{9,8},{10,11... | collective-permute-start | bytes 786440 | tf_op jit(solution)/shard_map/ppermute | solution.py:221
  18.3 1.8 %collective-permute-start.4 = (bf16[1,2,512,128]{3,2,1,0:T(8,128)(2,1)S(1)}, bf16[1,2,512,128]{3,2,1,0:T(8,128)(2,1)S(1)}, u32[]{:S(2)}, u32[]{:S(2)}) collective-permute-start(bf16[1,2,512,128]{3,2,1,0:T(8,128)(2,1)S(1)} %slice.3), channel_id=1, source_target_pairs={{0,1},{1,0},{2,3},{3,2},{4,5},{5,4},{6,7},{7,6},{8,9},{9,8},{10,11... | collective-permute-start | bytes 786440 | tf_op jit(solution)/shard_map/ppermute | solution.py:221
  18.4 1.7 %collective-permute-start.2 = (bf16[2,2,128,128]{3,2,1,0:T(8,128)(2,1)S(1)}, bf16[2,2,128,128]{3,2,1,0:T(8,128)(2,1)S(1)}, u32[]{:S(2)}, u32[]{:S(2)}) collective-permute-start(bf16[2,2,128,128]{3,2,1,0:T(8,128)(2,1)S(1)} %pad_maximum_fusion.near_ref), channel_id=1, source_target_pairs={{0,1},{1,0},{2,3},{3,2},{4,5},{5,4},{6,7},{7,6},{8,9},{9,8},{10,11... | collective-permute-start | bytes 393224 | tf_op jit(solution)/shard_map/ppermute | solution.py:221
  21.1 7.0 %collective-permute-start.5 = (bf16[2,128,128]{2,1,0:T(8,128)(2,1)S(1)}, bf16[2,128,128]{2,1,0:T(8,128)(2,1)S(1)}, u32[]{:S(2)}, u32[]{:S(2)}) collective-permute-start(bf16[2,128,128]{2,1,0:T(8,128)(2,1)S(1)} %get-tuple-element.32), channel_id=1, source_target_pairs={{0,8},{4,12},{8,0},{12,4},{1,9},{5,13},{9,1},{13,5},{2,10},{6,14},... | collective-permute-start | bytes 196616 | tf_op jit(solution)/shard_map/ppermute | solution.py:221
  24.0 6.5 %collective-permute-start.6 = (bf16[2,128,128]{2,1,0:T(8,128)(2,1)S(1)}, bf16[2,128,128]{2,1,0:T(8,128)(2,1)S(1)}, u32[]{:S(2)}, u32[]{:S(2)}) collective-permute-start(bf16[2,128,128]{2,1,0:T(8,128)(2,1)S(1)} %get-tuple-element.33), channel_id=1, source_target_pairs={{0,12},{4,8},{8,4},{12,0},{1,13},{5,9},{9,5},{13,1},{2,14},{6,10},... | collective-permute-start | bytes 196616 | tf_op jit(solution)/shard_map/ppermute | solution.py:221
  25.4 5.3 %collective-permute-start.7 = (bf16[2,128,128]{2,1,0:T(8,128)(2,1)S(1)}, bf16[2,128,128]{2,1,0:T(8,128)(2,1)S(1)}, u32[]{:S(2)}, u32[]{:S(2)}) collective-permute-start(bf16[2,128,128]{2,1,0:T(8,128)(2,1)S(1)} %get-tuple-element.34), channel_id=1, source_target_pairs={{0,4},{4,0},{8,12},{12,8},{1,5},{5,1},{9,13},{13,9},{2,6},{6,2},{1... | collective-permute-start | bytes 196616 | tf_op jit(solution)/shard_map/ppermute | solution.py:221
  38.8 4.3 %collective-permute-start.8 = (bf16[1,2,128,128]{3,2,1,0:T(8,128)(2,1)S(1)}, bf16[1,2,128,128]{3,2,1,0:T(8,128)(2,1)S(1)}, u32[]{:S(2)}, u32[]{:S(2)}) collective-permute-start(bf16[1,2,128,128]{3,2,1,0:T(8,128)(2,1)S(1)} %bitcast.4), channel_id=1, source_target_pairs={{0,2},{1,3},{2,0},{3,1},{4,6},{5,7},{6,4},{7,5},{8,10},{9,11},{10,... | collective-permute-start | bytes 196616 | tf_op jit(solution)/shard_map/ppermute | solution.py:221
  43.2 1.4 %collective-permute-start.9 = (bf16[2,2,128,128]{3,2,1,0:T(8,128)(2,1)S(1)}, bf16[2,2,128,128]{3,2,1,0:T(8,128)(2,1)S(1)}, u32[]{:S(2)}, u32[]{:S(2)}) collective-permute-start(bf16[2,2,128,128]{3,2,1,0:T(8,128)(2,1)S(1)} %pad_maximum_fusion.1.near_ref), channel_id=1, source_target_pairs={{0,1},{1,0},{2,3},{3,2},{4,5},{5,4},{6,7},{7,6},{8,9},{9,8},{10,11... | collective-permute-start | bytes 393224 | tf_op jit(solution)/shard_map/ppermute | solution.py:221
  45.6 8.0 %collective-permute-start.10 = (bf16[2,128,128]{2,1,0:T(8,128)(2,1)S(1)}, bf16[2,128,128]{2,1,0:T(8,128)(2,1)S(1)}, u32[]{:S(2)}, u32[]{:S(2)}) collective-permute-start(bf16[2,128,128]{2,1,0:T(8,128)(2,1)S(1)} %get-tuple-element.38), channel_id=1, source_target_pairs={{0,8},{4,12},{8,0},{12,4},{1,9},{5,13},{9,1},{13,5},{2,10},{6,14},... | collective-permute-start | bytes 196616 | tf_op jit(solution)/shard_map/ppermute | solution.py:221
  48.4 6.4 %collective-permute-start.11 = (bf16[2,128,128]{2,1,0:T(8,128)(2,1)S(1)}, bf16[2,128,128]{2,1,0:T(8,128)(2,1)S(1)}, u32[]{:S(2)}, u32[]{:S(2)}) collective-permute-start(bf16[2,128,128]{2,1,0:T(8,128)(2,1)S(1)} %get-tuple-element.39), channel_id=1, source_target_pairs={{0,12},{4,8},{8,4},{12,0},{1,13},{5,9},{9,5},{13,1},{2,14},{6,10},... | collective-permute-start | bytes 196616 | tf_op jit(solution)/shard_map/ppermute | solution.py:221
  49.1 5.9 %collective-permute-start.12 = (bf16[2,128,128]{2,1,0:T(8,128)(2,1)S(1)}, bf16[2,128,128]{2,1,0:T(8,128)(2,1)S(1)}, u32[]{:S(2)}, u32[]{:S(2)}) collective-permute-start(bf16[2,128,128]{2,1,0:T(8,128)(2,1)S(1)} %get-tuple-element.40), channel_id=1, source_target_pairs={{0,4},{4,0},{8,12},{12,8},{1,5},{5,1},{9,13},{13,9},{2,6},{6,2},{1... | collective-permute-start | bytes 196616 | tf_op jit(solution)/shard_map/ppermute | solution.py:221
